TPU v7x, 128 devices: a whole 4x4x4 slice. The times are simulated.
128 devices in a mesh: gx: 16 (over z_hi, x, core), gy: 8 (over y, z_lo).
Axes of the slice: x: 4, y: 4, z: 4 (z_hi: 2, z_lo: 2; z = z_hi * 2 + z_lo), core: 2. Of those that a mesh axis runs over, the one named last changes fastest.
Arguments:
- checkpoint: float32 [8, 64, 65536], P('gy', 'gx'), may hold values from 0.2 to 2
- sorption_kd: float32 [512, 65536], P('gy', 'gx'), may hold values from 0.05 to 1
- velocity: float32 [3, 512, 65536], P(None, 'gy', 'gx'), may hold values from -0.5 to 0.5
- source: float32 [512, 65536], P('gy', 'gx'), may hold values from -8 to 8
- target: float32 [512, 65536], P('gy', 'gx'), may hold values from -6 to 6
- cell_type: int32 [512, 65536], P('gy', 'gx'), may hold values from 0 to 2
- outlets: int32 [1024], replicated, may hold values from 0 to 33554431, as said below
Outputs:
- kd_gradient: float32 [512, 65536], P('gy', 'gx')
- checkpoint_adjoint: float32 [512, 65536], P('gy', 'gx')
Inputs may be any that keep to these rules, and one draw needn't show every extreme that they name: `outlets`: 1024 distinct cells.
All inputs are finite; a program needn't handle non-finite values.
Results may differ from a plain program's by a relative error of at most 0.00002.
Values sent between devices are 32-bit elements; how exact they have to be, the bound alone decides.
No kernel may reach another device: no remote copies, remote signals or barrier semaphores. Data moves between devices by JAX's collectives and lax.ppermute only.
A program may use at most 192 MiB of HBM per device.

v0:
```python
from functools import partial

import jax
import jax.numpy as jnp
from jax import lax
from jax.sharding import PartitionSpec as P

NZ = 64


BULK = 4.0
FREUND = 0.7
DISP = 0.1
DRAIN = 0.5
STEP = 0.4
OUTLET_W = 4.0


def with_halo(block, sides, width):
    for axis, dim in sides:
        count = lax.axis_size(axis)
        forward = [(i, i + 1) for i in range(count - 1)]
        backward = [(target, source) for source, target in forward]
        low = lax.ppermute(
            lax.slice_in_dim(block, block.shape[dim] - width, None, axis=dim), axis, forward
        )
        high = lax.ppermute(lax.slice_in_dim(block, 0, width, axis=dim), axis, backward)
        block = jnp.concatenate([low, block, high], axis=dim)
    return block


def vertical_terms(tracer, vel_z):
    layer = lax.broadcasted_iota(jnp.int32, tracer.shape, 1) % NZ
    shifted_up = jnp.concatenate([tracer[:, 1:], tracer[:, -1:]], axis=1)
    shifted_down = jnp.concatenate([tracer[:, :1], tracer[:, :-1]], axis=1)
    upper_cell = jnp.where(layer == NZ - 1, tracer, shifted_up)
    lower_cell = jnp.where(layer == 0, tracer, shifted_down)
    return (
        DISP * (upper_cell + lower_cell - 2.0 * tracer)
        - jnp.maximum(vel_z, 0.0) * (tracer - lower_cell)
        - jnp.minimum(vel_z, 0.0) * (upper_cell - tracer)
    )


def neighbours(padded):
    north_cell = padded[2:, NZ:-NZ]
    south_cell = padded[:-2, NZ:-NZ]
    east_cell = padded[1:-1, 2 * NZ :]
    west_cell = padded[1:-1, : -2 * NZ]
    return (north_cell, south_cell, east_cell, west_cell)


def total_flux(tracer, padded, velocity, cell_type, source):
    north_cell, south_cell, east_cell, west_cell = neighbours(padded)
    plane = DISP * (north_cell + south_cell + east_cell + west_cell - 4.0 * tracer)
    plane = (
        plane
        - jnp.maximum(velocity[0], 0.0) * (tracer - south_cell)
        - jnp.minimum(velocity[0], 0.0) * (north_cell - tracer)
    )
    plane = (
        plane
        - jnp.maximum(velocity[1], 0.0) * (tracer - west_cell)
        - jnp.minimum(velocity[1], 0.0) * (east_cell - tracer)
    )
    drains = (cell_type == 2).astype(jnp.float32)
    wells = (cell_type == 1).astype(jnp.float32)
    return plane + vertical_terms(tracer, velocity[2]) - DRAIN * drains * tracer + wells * source


def transpose_flux(weighted, padded, velocity, velocity_pad, cell_type):
    north_cell, south_cell, east_cell, west_cell = neighbours(padded)
    plane = DISP * (north_cell + south_cell + east_cell + west_cell - 4.0 * weighted)
    plane = plane - (jnp.abs(velocity[0]) + jnp.abs(velocity[1])) * weighted
    plane = plane + jnp.maximum(velocity_pad[0, 2:, NZ:-NZ], 0.0) * north_cell
    plane = plane - jnp.minimum(velocity_pad[0, :-2, NZ:-NZ], 0.0) * south_cell
    plane = plane + jnp.maximum(velocity_pad[1, 1:-1, 2 * NZ :], 0.0) * east_cell
    plane = plane - jnp.minimum(velocity_pad[1, 1:-1, : -2 * NZ], 0.0) * west_cell
    primal, backward = jax.vjp(partial(vertical_terms, vel_z=velocity[2]), weighted)
    drains = (cell_type == 2).astype(jnp.float32)
    return plane + backward(weighted)[0] - DRAIN * drains * weighted


def faces(stacked):
    sides = with_halo(stacked, (("gx", 2),), NZ)
    return with_halo(sides, (("gy", 1),), 1)


def per_device(checkpoint, sorption_kd, velocity, source, target, cell_type, outlets):
    brick_rows = sorption_kd.shape[0]
    brick_cols = sorption_kd.shape[1] // NZ
    gx_count = lax.axis_size("gx")
    arrived = lax.all_to_all(checkpoint, "gx", split_axis=2, concat_axis=1, tiled=True)
    initial = arrived.reshape(brick_rows, brick_cols * NZ)
    stacked = jnp.concatenate([initial[None], velocity], axis=0)
    padded_all = faces(stacked)
    padded_start = padded_all[0]
    velocity_pad = padded_all[1:]
    sorb_power = initial ** (FREUND - 1.0)
    retard = 1.0 + BULK * sorption_kd * sorb_power
    flux_first = total_flux(initial, padded_start, velocity, cell_type, source)
    first_state = initial + STEP * flux_first / retard
    flux_second = total_flux(first_state, faces(first_state[None])[0], velocity, cell_type, source)
    final_state = first_state + STEP * flux_second / retard
    plane_cells = gx_count * brick_cols * NZ
    row_of = outlets // plane_cells
    remainder = outlets % plane_cells
    col_of = remainder // NZ
    layer_of = remainder % NZ
    row_start = lax.axis_index("gy") * brick_rows
    col_start = lax.axis_index("gx") * brick_cols
    inside = (
        (row_of >= row_start)
        & (row_of < row_start + brick_rows)
        & (col_of >= col_start)
        & (col_of < col_start + brick_cols)
    )
    cell_count = brick_rows * brick_cols * NZ
    local_index = jnp.where(
        inside,
        ((row_of - row_start) * brick_cols + (col_of - col_start)) * NZ + layer_of,
        cell_count,
    )
    weight = (
        jnp.ones((cell_count,), jnp.float32)
        .at[local_index]
        .add(OUTLET_W, mode="drop")
        .reshape(brick_rows, brick_cols * NZ)
    )
    misfit = weight * (final_state - target)
    weighted = STEP * misfit / retard
    grad_first = misfit + transpose_flux(
        weighted, faces(weighted[None])[0], velocity, velocity_pad, cell_type
    )
    grad_retard = -misfit * STEP * flux_second / (retard * retard)
    weighted = STEP * grad_first / retard
    grad_start = grad_first + transpose_flux(
        weighted, faces(weighted[None])[0], velocity, velocity_pad, cell_type
    )
    grad_retard = grad_retard - grad_first * STEP * flux_first / (retard * retard)
    kd_gradient = grad_retard * BULK * sorb_power
    checkpoint_adjoint = (
        grad_start + grad_retard * BULK * sorption_kd * (FREUND - 1.0) * sorb_power / initial
    )
    return (kd_gradient, checkpoint_adjoint)


def solution(mesh):
    return jax.shard_map(
        per_device,
        mesh=mesh,
        in_specs=(
            P("gy", "gx", None),
            P("gy", "gx"),
            P(None, "gy", "gx"),
            P("gy", "gx"),
            P("gy", "gx"),
            P("gy", "gx"),
            P(),
        ),
        out_specs=(P("gy", "gx"), P("gy", "gx")),
        check_vma=False,
    )
```

profile of v0, /device:TPU:15, one launch (start us, length us, event | category | flops | bytes accessed | tf_op | source)
XLA Modules:
  0.0 641.1 jit_solution(8577151627787378535)
XLA Ops:
  0.6 56.2 %copy.10 = f32[1,4,65536]{1,0,2:T(1,128)} copy(f32[1,4,65536]{2,1,0:T(4,128)} %param.7) | data formatting | bytes 2097152 | tf_op args[0]
  56.8 0.5 broadcast.284
  57.4 291.0 %reduce = f32[65536,4]{1,0:T(8,128)} reduce(f32[65536,1,4]{2,1,0:T(1,128)} %bitcast.176, f32[]{:T(128)} %broadcast.284), dimensions={1}, to_apply=%bitcast.153.reduce_sub_computation | reduce | bytes 2097156
  348.3 29.8 %reshape.47 = f32[16,1,16384]{2,1,0:T(1,128)} reshape(f32[65536,4]{1,0:T(8,128)} %reduce) | data formatting | bytes 2097152
  378.1 8.6 %all-to-all-start = ((f32[16,1,16384]{2,1,0:T(1,128)}), f32[16,1,16384]{2,1,0:T(1,128)S(1)}, u32[]{:S(2)}, u32[]{:S(2)}) async-start(f32[16,1,16384]{2,1,0:T(1,128)} %reshape.47), calls=%async_computation | async-start | bytes 2097152 | tf_op jit(solution)/shard_map/all_to_all | solution.py:93
  386.7 6.5 %scatter_custom_fusion = f32[262144]{0:T(1024)S(1)} fusion(s32[1024]{0:T(1024)S(1)} %compare_select_fusion.1, f32[1024]{0:T(1024)S(1)} %broadcast.119, f32[]{:T(128)} %constant.91.clone.1), kind=kCustom, calls=%fused_computation.118 | custom fusion | flops 1024 | bytes 1048580 | tf_op jit(solution)/shard_map/scatter-add | solution.py:127
  393.2 1.2 reshape.34
  394.4 7.6 %all-to-all-done = f32[16,1,16384]{2,1,0:T(1,128)S(1)} async-done(((f32[16,1,16384]{2,1,0:T(1,128)}), f32[16,1,16384]{2,1,0:T(1,128)S(1)}, u32[]{:S(2)}, u32[]{:S(2)}) %all-to-all-start) | async-done | bytes 1048608 | tf_op jit(solution)/shard_map/all_to_all | solution.py:93
  402.0 3.2 reduce.1
  405.2 74.9 %reshape.48 = f32[65536,1,4]{2,1,0:T(1,128)} reshape(f32[16,16384]{1,0:T(8,128)S(1)} %reduce.1) | data formatting | bytes 2097152
  480.1 17.7 %copy.11 = f32[1,16,4,4096]{3,2,1,0:T(4,128)S(1)} copy(f32[1,16,4,4096]{2,3,1,0:T(8,128)} %bitcast.177) | data formatting | bytes 2097152 | tf_op jit(solution)/shard_map/all_to_all | solution.py:93
  497.8 1.0 copy-done.15
  498.7 1.4 all_to_all.16
  500.1 2.7 reshape.35
  502.8 1.3 constant_dynamic-update-slice_fusion.1
  504.5 4.8 collective-permute-start
  509.3 1.9 collective-permute-start.1
  511.2 1.6 fusion.97
  512.9 6.3 collective-permute-done.1
  519.2 6.3 concatenate.52
  525.5 1.3 fusion.87
  526.8 2.6 collective-permute-start.2
  529.5 3.5 collective-permute-start.3
  533.0 0.9 fusion.98
  533.9 0.9 collective-permute-done.3
  534.8 1.8 fusion
  536.7 5.1 divide_add_fusion
  541.9 3.1 collective-permute-start.4
  544.9 1.9 collective-permute-start.5
  546.9 1.7 fusion.95
  548.5 5.3 collective-permute-done.5
  553.9 2.5 concatenate.56
  556.3 1.0 fusion.91
  557.3 3.3 collective-permute-start.6
  560.7 3.0 collective-permute-start.7
  563.7 0.9 fusion.96
  564.5 0.8 collective-permute-done.7
  565.3 1.4 maximum_bitcast_fusion
  566.7 5.5 fusion.79
  572.2 1.0 copy-done.18
  573.3 4.0 collective-permute-start.8
  577.3 1.9 collective-permute-start.9
  579.2 7.0 %collective-permute-done.9 = f32[1,64,64]{2,1,0:T(8,128)} collective-permute-done((f32[1,64,64]{2,1,0:T(8,128)S(1)}, f32[1,64,64]{2,1,0:T(8,128)}, u32[]{:S(2)}, u32[]{:S(2)}) %collective-permute-start.9) | collective-permute-done | bytes 16416 | tf_op jit(solution)/shard_map/ppermute | solution.py:27
  586.2 2.3 concatenate.60
  588.5 1.0 fusion.90
  589.5 2.6 collective-permute-start.10
  592.1 3.5 collective-permute-start.11
  595.7 2.2 fusion.9
  597.9 0.3 split.26
  598.4 2.0 maximum_bitcast_fusion.1
  600.6 6.4 fusion.78
  607.0 1.0 copy-done.17
  608.0 2.4 collective-permute-start.12
  610.4 2.0 collective-permute-start.13
  612.4 6.9 %collective-permute-done.13 = f32[1,64,64]{2,1,0:T(8,128)S(1)} collective-permute-done((f32[1,64,64]{2,1,0:T(8,128)S(1)}, f32[1,64,64]{2,1,0:T(8,128)S(1)}, u32[]{:S(2)}, u32[]{:S(2)}) %collective-permute-start.13) | collective-permute-done | bytes 16416 | tf_op jit(solution)/shard_map/ppermute | solution.py:27
  619.3 2.3 concatenate.66
  621.6 1.0 fusion.89
  622.6 2.0 collective-permute-start.14
  624.6 4.2 collective-permute-start.15
  628.8 2.2 fusion.7
  631.0 0.3 split.29
  631.9 0.6 copy-done.12
  633.3 6.0 fusion.31
  639.3 1.5 power_multiply_fusion
  (81 shorter events, 2.4 us)
Async XLA Ops:
  378.1 8.6 %copy-start.28 = (s32[1024]{0:T(1024)S(1)}, s32[1024]{0:T(1024)}, u32[]{:S(2)}) copy-start(s32[1024]{0:T(1024)} %param.13) | copy-start | bytes 12292
  378.1 23.9 %all-to-all-start = ((f32[16,1,16384]{2,1,0:T(1,128)}), f32[16,1,16384]{2,1,0:T(1,128)S(1)}, u32[]{:S(2)}, u32[]{:S(2)}) async-start(f32[16,1,16384]{2,1,0:T(1,128)} %reshape.47), calls=%async_computation | async-start | bytes 2097152 | tf_op jit(solution)/shard_map/all_to_all | solution.py:93
  497.7 1.0 copy-start.15
  500.1 4.0 copy-start
  504.1 7.1 %copy-start.1 = (f32[64,4096]{1,0:T(8,128)S(1)}, f32[64,4096]{1,0:T(8,128)}, u32[]{:S(2)}) copy-start(f32[64,4096]{1,0:T(8,128)} %reshape.35) | copy-start | bytes 3145732
  504.4 8.5 %copy-start.9 = (f32[4,64,4096]{2,1,0:T(8,128)}, f32[4,64,4096]{2,1,0:T(8,128)S(1)}, u32[]{:S(2)}) copy-start(f32[4,64,4096]{2,1,0:T(8,128)S(1)} %constant_dynamic-update-slice_fusion) | copy-start | bytes 12582916
  504.5 8.4 %collective-permute-start = (f32[4,64,64]{2,1,0:T(8,128)S(1)}, f32[4,64,64]{2,1,0:T(8,128)S(1)}, u32[]{:S(2)}, u32[]{:S(2)}) collective-permute-start(f32[4,64,64]{2,1,0:T(8,128)S(1)} %get-tuple-element.23), channel_id=1, source_target_pairs={{0,8},{8,16},{16,24},{24,32},{32,40},{40,48},{48,56},{56,64},{64,7... | collective-permute-start | bytes 196616 | tf_op jit(solution)/shard_map/ppermute | solution.py:24
  509.3 9.9 %collective-permute-start.1 = (f32[4,64,64]{2,1,0:T(8,128)S(1)}, f32[4,64,64]{2,1,0:T(8,128)S(1)}, u32[]{:S(2)}, u32[]{:S(2)}) collective-permute-start(f32[4,64,64]{2,1,0:T(8,128)S(1)} %get-tuple-element.22), channel_id=1, source_target_pairs={{8,0},{16,8},{24,16},{32,24},{40,32},{48,40},{56,48},{64,56},{72,6... | collective-permute-start | bytes 196616 | tf_op jit(solution)/shard_map/ppermute | solution.py:27
  526.8 7.1 %collective-permute-start.2 = (f32[4,1,4224]{2,1,0:T(1,128)S(1)}, f32[4,1,4224]{2,1,0:T(1,128)S(1)}, u32[]{:S(2)}, u32[]{:S(2)}) collective-permute-start(f32[4,1,4224]{2,1,0:T(1,128)S(1)} %get-tuple-element.20), channel_id=1, source_target_pairs={{0,1},{1,2},{2,3},{3,4},{4,5},{5,6},{6,7},{8,9},{9,10},{10,11},{11... | collective-permute-start | bytes 202760 | tf_op jit(solution)/shard_map/ppermute | solution.py:24
  529.5 5.3 collective-permute-start.3
  533.9 2.8 copy-start.2
  533.9 2.8 copy-start.11
  533.9 2.8 copy-start.19
  533.9 2.8 copy-start.23
  533.9 2.8 copy-start.24
  534.8 1.8 copy-start.25
  541.8 6.8 %copy-start.7 = (f32[64,4096]{1,0:T(8,128)}, f32[64,4096]{1,0:T(8,128)S(1)}, u32[]{:S(2)}) copy-start(f32[64,4096]{1,0:T(8,128)S(1)} %get-tuple-element.13) | copy-start | bytes 3145732
  541.9 6.7 %collective-permute-start.4 = (f32[1,64,64]{2,1,0:T(8,128)S(1)}, f32[1,64,64]{2,1,0:T(8,128)S(1)}, u32[]{:S(2)}, u32[]{:S(2)}) collective-permute-start(f32[1,64,64]{2,1,0:T(8,128)S(1)} %get-tuple-element.35), channel_id=1, source_target_pairs={{0,8},{8,16},{16,24},{24,32},{32,40},{40,48},{48,56},{56,64},{64,7... | collective-permute-start | bytes 49160 | tf_op jit(solution)/shard_map/ppermute | solution.py:24
  544.9 9.0 %collective-permute-start.5 = (f32[1,64,64]{2,1,0:T(8,128)S(1)}, f32[1,64,64]{2,1,0:T(8,128)}, u32[]{:S(2)}, u32[]{:S(2)}) collective-permute-start(f32[1,64,64]{2,1,0:T(8,128)S(1)} %get-tuple-element.34), channel_id=1, source_target_pairs={{8,0},{16,8},{24,16},{32,24},{40,32},{48,40},{56,48},{64,56},{72,6... | collective-permute-start | bytes 49160 | tf_op jit(solution)/shard_map/ppermute | solution.py:27
  557.3 7.2 %collective-permute-start.6 = (f32[1,1,4224]{2,1,0:T(1,128)S(1)}, f32[1,1,4224]{2,1,0:T(1,128)S(1)}, u32[]{:S(2)}, u32[]{:S(2)}) collective-permute-start(f32[1,1,4224]{2,1,0:T(1,128)S(1)} %get-tuple-element.28), channel_id=1, source_target_pairs={{0,1},{1,2},{2,3},{3,4},{4,5},{5,6},{6,7},{8,9},{9,10},{10,11},{11... | collective-permute-start | bytes 50696 | tf_op jit(solution)/shard_map/ppermute | solution.py:24
  560.7 6.0 copy-start.4
  560.7 6.0 copy-start.8
  560.7 4.6 collective-permute-start.7
  572.2 1.0 copy-start.18
  573.3 5.9 collective-permute-start.8
  577.3 9.0 %collective-permute-start.9 = (f32[1,64,64]{2,1,0:T(8,128)S(1)}, f32[1,64,64]{2,1,0:T(8,128)}, u32[]{:S(2)}, u32[]{:S(2)}) collective-permute-start(f32[1,64,64]{2,1,0:T(8,128)S(1)} %get-tuple-element.32), channel_id=1, source_target_pairs={{8,0},{16,8},{24,16},{32,24},{40,32},{48,40},{56,48},{64,56},{72,6... | collective-permute-start | bytes 49160 | tf_op jit(solution)/shard_map/ppermute | solution.py:27
  589.5 8.9 %collective-permute-start.10 = (f32[1,1,4224]{2,1,0:T(1,128)S(1)}, f32[1,1,4224]{2,1,0:T(1,128)S(1)}, u32[]{:S(2)}, u32[]{:S(2)}) collective-permute-start(f32[1,1,4224]{2,1,0:T(1,128)S(1)} %get-tuple-element.26), channel_id=1, source_target_pairs={{0,1},{1,2},{2,3},{3,4},{4,5},{5,6},{6,7},{8,9},{9,10},{10,11},{11... | collective-permute-start | bytes 50696 | tf_op jit(solution)/shard_map/ppermute | solution.py:24
  592.1 6.2 collective-permute-start.11
  595.7 4.7 slice-start
  595.7 4.7 slice-start.1
  595.7 4.7 copy-start.10
  598.3 2.3 copy-start.5
  598.3 2.3 copy-start.26
  598.3 2.3 copy-start.27
  607.0 1.0 copy-start.17
  608.0 4.3 collective-permute-start.12
  610.4 8.8 %collective-permute-start.13 = (f32[1,64,64]{2,1,0:T(8,128)S(1)}, f32[1,64,64]{2,1,0:T(8,128)S(1)}, u32[]{:S(2)}, u32[]{:S(2)}) collective-permute-start(f32[1,64,64]{2,1,0:T(8,128)S(1)} %get-tuple-element.30), channel_id=1, source_target_pairs={{8,0},{16,8},{24,16},{32,24},{40,32},{48,40},{56,48},{64,56},{72,6... | collective-permute-start | bytes 49160 | tf_op jit(solution)/shard_map/ppermute | solution.py:27
  622.6 8.9 %collective-permute-start.14 = (f32[1,1,4224]{2,1,0:T(1,128)S(1)}, f32[1,1,4224]{2,1,0:T(1,128)S(1)}, u32[]{:S(2)}, u32[]{:S(2)}) collective-permute-start(f32[1,1,4224]{2,1,0:T(1,128)S(1)} %get-tuple-element.24), channel_id=1, source_target_pairs={{0,1},{1,2},{2,3},{3,4},{4,5},{5,6},{6,7},{8,9},{9,10},{10,11},{11... | collective-permute-start | bytes 50696 | tf_op jit(solution)/shard_map/ppermute | solution.py:24
  624.6 6.9 %collective-permute-start.15 = (f32[1,1,4224]{2,1,0:T(1,128)S(1)}, f32[1,1,4224]{2,1,0:T(1,128)S(1)}, u32[]{:S(2)}, u32[]{:S(2)}) collective-permute-start(f32[1,1,4224]{2,1,0:T(1,128)S(1)} %get-tuple-element.25), channel_id=1, source_target_pairs={{1,0},{2,1},{3,2},{4,3},{5,4},{6,5},{7,6},{9,8},{10,9},{11,10},{12... | collective-permute-start | bytes 50696 | tf_op jit(solution)/shard_map/ppermute | solution.py:27
  628.8 2.7 copy-start.16
  628.8 2.8 copy-start.14
  628.8 2.8 copy-start.20
  628.8 2.8 copy-start.21
  628.8 3.1 copy-start.22
  631.0 1.4 copy-start.12
  631.0 1.7 copy-start.13
  631.4 1.7 copy-start.3
  631.4 2.0 copy-start.6
where the time goes:
time: 654 us; the launch traced here: 641 us
  other arithmetic  335 us (51%)
  local copies, waits for them, and re-layouts  215 us (33%)
  starting transfers between devices  55.3 us (8%)
  waiting for transfers between devices  34.8 us (5%)
    unnamed x2, other arithmetic  291 us
    unnamed x67, local copies, waits for them, and re-layouts  168 us
    ppermute x8, waiting for transfers between devices, with_halo(): lax.ppermute(lax.slice_in_dim(block, 0, width, axis=dim), axis, backward)  27.2 us
    ppermute x8, starting transfers between devices, with_halo(): lax.ppermute(lax.slice_in_dim(block, block.shape[dim] - width, None, axis...  24.8 us
    ppermute x8, starting transfers between devices, with_halo(): lax.ppermute(lax.slice_in_dim(block, 0, width, axis=dim), axis, backward)  21.9 us
    all_to_all x2, local copies, waits for them, and re-layouts, per_device(): lax.all_to_all(checkpoint, 'gx', split_axis=2, concat_axis=1, tiled=True)  19.1 us
    concatenate x4, local copies, waits for them, and re-layouts, with_halo(): block = jnp.concatenate([low, block, high], axis=dim)  13.4 us
  transfers between devices with their start and end apart: 17, of which 7 were waited for; matrix products, arithmetic and copies ran while one was open for 3% of the time, Pallas kernels for 0%

commit v1 on v0

v1 whole, which is shorter than its diff:
```python
import jax
import jax.numpy as jnp
from jax import lax
from jax.experimental import pallas as pl
from jax.experimental.pallas import tpu as pltpu
from jax.sharding import PartitionSpec as P

NZ = 64
BULK = 4.0
FREUND = 0.7
DISP = 0.1
DRAIN = 0.5
STEP = 0.4
OUTLET_W = 4.0

LANES = 128
ROWS = 64
TILES = 32
WT = TILES + 4
WR = 80
BASE = 8
COLS = TILES * LANES
WCOLS = WT * LANES
MCOLS = WCOLS + 4 * LANES
F32 = jnp.float32
MIB = 1 << 20

VM = pl.BlockSpec(memory_space=pltpu.VMEM)
SM = pl.BlockSpec(memory_space=pltpu.SMEM)
HB = pl.BlockSpec(memory_space=pl.ANY)


def window(dtype=F32):
    return jax.ShapeDtypeStruct((WT, WR, LANES), dtype)


def lane_iota(rows):
    return lax.broadcasted_iota(jnp.int32, (rows, LANES), 1)


def pack_lines(src, out, sem):
    n = out.shape[0]
    copies = []
    for i in range(n):
        low = i * COLS - 2 * LANES
        high = low + WCOLS
        pieces = [(max(low, 0), min(high, n * COLS), max(-low, 0))]
        if low < 0:
            pieces.append((0, 2 * LANES, 0))
        if high > n * COLS:
            pieces.append((n * COLS - 2 * LANES, n * COLS, WCOLS - 2 * LANES))
        for a, b, at in pieces:
            copies.append(
                pltpu.make_async_copy(
                    src.at[0, :, a:b], out.at[i, :, at : at + b - a], sem
                )
            )
    for c in copies:
        c.start()
    for c in copies:
        c.wait()


def pack_edges(kdl, kdr, kdt, kdb, vl, vr, vt, vb, sl, sr, st, sb, cl, cr, ct, cb, tl, tr, tt, tb,
               to_left, to_right, to_low, to_high):
    lo = lane_iota(ROWS) < NZ

    def seven(kd, v, s, c, t, at):
        kind = at(c)
        return (
            at(kd), at(v, 0), at(v, 1), at(v, 2),
            jnp.where(kind == 1, at(s), 0.0),
            jnp.where(kind == 2, DRAIN, 0.0).astype(F32),
            at(t),
        )

    def cols(tile):
        def at(ref, d=None):
            part = pl.ds(tile * LANES, LANES)
            return ref[:, part] if d is None else ref[d, :, part]
        return at

    full = seven(kdl, vl, sl, cl, tl, cols(0))
    third = seven(kdl, vl, sl, cl, tl, cols(1))
    for f in range(7):
        to_left[f] = full[f]
    for p in range(3):
        to_left[7 + p] = jnp.where(lo, third[2 * p], pltpu.roll(third[2 * p + 1], NZ, 1))
    full = seven(kdr, vr, sr, cr, tr, cols(1))
    third = seven(kdr, vr, sr, cr, tr, cols(0))
    for f in range(7):
        to_right[f] = full[f]
    for p in range(3):
        to_right[7 + p] = jnp.where(lo, pltpu.roll(third[2 * p], NZ, 1), third[2 * p + 1])

    def rows(a):
        def at(ref, d=None):
            return ref[a : a + 2, :] if d is None else ref[d, a : a + 2, :]
        return at

    for f, part in enumerate(seven(kdt, vt, st, ct, tt, rows(0))):
        to_low[f] = part
    for f, part in enumerate(seven(kdb, vb, sb, cb, tb, rows(6))):
        to_high[f] = part


def list_outlets(outlets, place, found, count):
    row_start, col_start = place[0], place[1]

    def step(i, n):
        for k in range(8):
            flat = outlets[i * 8 + k]
            row = (flat >> 16) - row_start + BASE
            col = ((flat >> 6) & 1023) - col_start + 4
            inside = (row >= BASE - 2) & (row < BASE + ROWS + 2) & (col >= 2) & (col < 70)
            found[n] = (row << 16) + (col << 6) + (flat & 63)
            n = n + inside.astype(jnp.int32)
        return n

    count[0] = lax.fori_loop(0, outlets.shape[0] // 8, step, jnp.int32(0))


def coefficients(v0, v1, v2, drain):
    z = lax.broadcasted_iota(jnp.int32, v0.shape, v0.ndim - 1) & (NZ - 1)
    north = DISP - jnp.minimum(v0, 0.0)
    south = DISP + jnp.maximum(v0, 0.0)
    east = DISP - jnp.minimum(v1, 0.0)
    west = DISP + jnp.maximum(v1, 0.0)
    up = jnp.where(z == NZ - 1, 0.0, DISP - jnp.minimum(v2, 0.0))
    down = jnp.where(z == 0, 0.0, DISP + jnp.maximum(v2, 0.0))
    centre = ((north + south) + (east + west)) + ((up + down) + drain)
    return north, south, east, west, up, down, centre


def flux(u, coef, src, t, left, right, a, rows):
    cn, cs, ce, cw, cu, cd, cc = coef
    here = pl.ds(a, rows)
    lo = lane_iota(rows) < NZ
    mid = u[t, here, :]
    north = u[t, pl.ds(a + 1, rows), :]
    south = u[t, pl.ds(a - 1, rows), :]
    east = pltpu.roll(jnp.where(lo, u[right, here, :], mid), NZ, 1)
    west = pltpu.roll(jnp.where(lo, mid, u[left, here, :]), NZ, 1)
    upper = pltpu.roll(mid, LANES - 1, 1)
    lower = pltpu.roll(mid, 1, 1)
    plane = cn[t, here, :] * north + cs[t, here, :] * south
    plane = plane + (ce[t, here, :] * east + cw[t, here, :] * west)
    plane = plane + (cu[t, here, :] * upper + cd[t, here, :] * lower)
    return mid, plane + (src[t, here, :] - cc[t, here, :] * mid)


def flux_back(w, coef, t, left, right, a, rows):
    cn, cs, ce, cw, cu, cd, cc = coef
    here = pl.ds(a, rows)
    above, below = pl.ds(a + 1, rows), pl.ds(a - 1, rows)
    lo = lane_iota(rows) < NZ
    mid = w[t, here, :]
    w_right, w_left = w[right, here, :], w[left, here, :]
    from_low = cw[right, here, :] * w_right + ce[t, here, :] * mid
    from_high = cw[t, here, :] * mid + ce[left, here, :] * w_left
    total = pltpu.roll(jnp.where(lo, from_low, from_high), NZ, 1)
    total = total + (cs[t, above, :] * w[t, above, :] + cn[t, below, :] * w[t, below, :])
    total = total + pltpu.roll(cd[t, here, :] * mid, LANES - 1, 1)
    total = total + pltpu.roll(cu[t, here, :] * mid, 1, 1)
    return total - cc[t, here, :] * mid


def sorb(u):
    return jnp.exp((FREUND - 1.0) * jnp.log(u))


def rate_of(kd, power):
    return STEP / (1.0 + BULK * kd * power)


def first_half(place, lines, xl, xr, kd_h, v_h, s_h, c_h,
               u0, fst, d1, rate, power, cn, cs, ce, cw, cu, cd, cc, src, up_msg, low_msg,
               kd, v, s, c, sems):
    loads = [
        pltpu.make_async_copy(a, b, sems.at[k])
        for k, (a, b) in enumerate(((kd_h, kd), (v_h, v), (s_h, s), (c_h, c)))
    ]
    for load in loads:
        load.start()
    coef = (cn, cs, ce, cw, cu, cd, cc)
    own = pl.ds(BASE, ROWS)
    lines_of = lines.shape[1]
    for k in range(lines.shape[0]):
        for t in range(WT):
            u0[t, BASE + lines_of * k : BASE + lines_of * (k + 1), :] = lines[
                k, :, t * LANES : (t + 1) * LANES
            ]
    lo = lane_iota(ROWS) < NZ

    def third(ref, f, high):
        both = ref[7 + f // 2]
        if high:
            return jnp.where(lo, 0.0, both if f % 2 else pltpu.roll(both, NZ, 1))
        return jnp.where(lo, pltpu.roll(both, NZ, 1) if f % 2 else both, 0.0)

    for tile, fields in (
        (0, [third(xl, f, True) for f in range(6)]),
        (1, [xl[f] for f in range(6)]),
        (WT - 2, [xr[f] for f in range(6)]),
        (WT - 1, [third(xr, f, False) for f in range(6)]),
    ):
        for ref, val in zip(coef, coefficients(*fields[1:4], fields[5])):
            ref[tile, own, :] = val
        src[tile, own, :] = fields[4]
        rate[tile, own, :] = rate_of(fields[0], sorb(u0[tile, own, :]))

    @pl.when(place[0] == 0)
    def _():
        for ref in (u0, rate):
            ref[0:2, own, :] = jnp.zeros((2, ROWS, LANES), F32)

    @pl.when(place[1] == 0)
    def _():
        for ref in (u0, rate):
            ref[WT - 2 : WT, own, :] = jnp.zeros((2, ROWS, LANES), F32)

    loads[0].wait()

    def rates(t, carry):
        for r in range(0, ROWS, 8):
            at = pl.ds(BASE + r, 8)
            p = sorb(u0[t + 2, at, :])
            power[t, pl.ds(r, 8), :] = p
            rate[t + 2, at, :] = rate_of(kd[pl.ds(r, 8), pl.ds(pl.multiple_of(t * LANES, LANES), LANES)], p)
        return carry

    lax.fori_loop(0, TILES, rates, 0)
    for load in loads[1:]:
        load.wait()

    def coefs(t, carry):
        at = pl.ds(pl.multiple_of(t * LANES, LANES), LANES)
        for r in range(0, ROWS, 8):
            rr, to = pl.ds(r, 8), pl.ds(BASE + r, 8)
            kind = c[rr, at]
            drain = jnp.where(kind == 2, DRAIN, 0.0).astype(F32)
            for ref, val in zip(coef, coefficients(v[0, rr, at], v[1, rr, at], v[2, rr, at], drain)):
                ref[t + 2, to, :] = val
            src[t + 2, to, :] = jnp.where(kind == 1, s[rr, at], 0.0)
        return carry

    lax.fori_loop(0, TILES, coefs, 0)

    def step(t, carry):
        left, right = jnp.maximum(t - 1, 0), jnp.minimum(t + 1, WT - 1)
        for r in range(BASE, BASE + ROWS, 8):
            at = pl.ds(r, 8)
            mid, f = flux(u0, coef, src, t, left, right, r, 8)
            d = rate[t, at, :] * f
            d1[t, at, :] = d
            fst[t, at, :] = mid + d
        return carry

    lax.fori_loop(0, WT, step, 0)

    top = BASE + ROWS
    for t in range(WT):
        at = pl.ds(t * LANES, LANES)
        up_msg[0:2, at] = u0[t, top - 2 : top, :]
        up_msg[2:4, at] = fst[t, top - 3 : top - 1, :]
        low_msg[0:2, at] = u0[t, BASE : BASE + 2, :]
        low_msg[2:4, at] = fst[t, BASE + 1 : BASE + 3, :]
    for k in range(16):
        at = pl.ds(WCOLS + (k % 4) * LANES, LANES)
        row = pl.ds(k // 4, 1)
        if k < 14:
            side = xr if k % 2 else xl
            up_msg[row, at] = side[k // 2, ROWS - 1 : ROWS, :]
            low_msg[row, at] = side[k // 2, 0:1, :]
        else:
            up_msg[row, at] = jnp.zeros((1, LANES), F32)
            low_msg[row, at] = jnp.zeros((1, LANES), F32)


def second_half(place, found, count, xl, xr, yl, yh, ml, mh, kd_h, t_h, power,
                u0_in, fst_in, d1_in, rate_in, cn_in, cs_in, ce_in, cw_in, cu_in, cd_in, cc_in, src_in,
                kd_out, start_out,
                u0, fst, d1, rate, cn, cs, ce, cw, cu, cd, cc, src,
                kd, tgt, halo, target, d2, mis, w, grad, w1, sems):
    loads = [
        pltpu.make_async_copy(a, b, sems.at[k]) for k, (a, b) in enumerate(((kd_h, kd), (t_h, tgt)))
    ]
    for load in loads:
        load.start()
    coef = (cn, cs, ce, cw, cu, cd, cc)
    low8, high8 = slice(0, BASE), slice(BASE + ROWS, WR)
    own = pl.ds(BASE, ROWS)

    halo[...] = jnp.zeros(halo.shape, F32)
    top = BASE + ROWS
    for f in range(7):
        for t in range(TILES):
            at = pl.ds(t * LANES, LANES)
            halo[f, t + 2, 6:8, :] = yl[f, :, at]
            halo[f, t + 2, 8:10, :] = yh[f, :, at]
        for side, tile in ((0, 1), (1, WT - 2)):
            k = 2 * f + side
            at = pl.ds(WCOLS + (k % 4) * LANES, LANES)
            row = pl.ds(k // 4, 1)
            halo[f, tile, 7:8, :] = ml[row, at]
            halo[f, tile, 8:9, :] = mh[row, at]
    for t in range(WT):
        at = pl.ds(t * LANES, LANES)
        u0[t, low8, :] = jnp.ones((BASE, LANES), F32)
        u0[t, high8, :] = jnp.ones((BASE, LANES), F32)
        fst[t, low8, :] = jnp.zeros((BASE, LANES), F32)
        fst[t, high8, :] = jnp.zeros((BASE, LANES), F32)
        u0[t, 6:8, :] = ml[0:2, at]
        fst[t, 5:7, :] = ml[2:4, at]
        u0[t, top : top + 2, :] = mh[0:2, at]
        fst[t, top + 1 : top + 3, :] = mh[2:4, at]

    def edges(t, carry):
        for a, to in ((0, low8), (8, high8)):
            at = pl.ds(a, 8)
            values = coefficients(halo[1, t, at, :], halo[2, t, at, :], halo[3, t, at, :], halo[5, t, at, :])
            for ref, val in zip(coef, values):
                ref[t, to, :] = val
            src[t, to, :] = halo[4, t, at, :]
            rate[t, to, :] = rate_of(halo[0, t, at, :], sorb(u0[t, to, :]))
            target[t, to, :] = halo[6, t, at, :]
        return carry

    lax.fori_loop(0, WT, edges, 0)

    zero8 = jnp.zeros((WT, BASE, LANES), F32)

    @pl.when(place[0] == 0)
    def _():
        rate[0:2] = jnp.zeros((2, WR, LANES), F32)
        u0[0:2] = jnp.zeros((2, WR, LANES), F32)

    @pl.when(place[1] == 0)
    def _():
        rate[WT - 2 : WT] = jnp.zeros((2, WR, LANES), F32)
        u0[WT - 2 : WT] = jnp.zeros((2, WR, LANES), F32)

    @pl.when(place[2] == 0)
    def _():
        rate[:, low8, :] = zero8
        u0[:, low8, :] = zero8
        fst[:, low8, :] = zero8

    @pl.when(place[3] == 0)
    def _():
        rate[:, high8, :] = zero8
        u0[:, high8, :] = zero8
        fst[:, high8, :] = zero8

    def sides(t):
        return jnp.maximum(t - 1, 0), jnp.minimum(t + 1, WT - 1)

    def edge_step(t, carry):
        left, right = sides(t)
        for a, r0 in ((BASE - 4, BASE - 1), (top - 4, top - 1)):
            at = pl.ds(a, 8)
            row = lax.broadcasted_iota(jnp.int32, (8, LANES), 0) + a
            new = (row == r0) | (row == r0 + 1)
            mid, f = flux(u0, coef, src, t, left, right, a, 8)
            d = rate[t, at, :] * f
            d1[t, at, :] = jnp.where(new, d, d1[t, at, :])
            fst[t, at, :] = jnp.where(new, mid + d, fst[t, at, :])
        return carry

    lax.fori_loop(0, WT, edge_step, 0)

    loads[1].wait()

    def targets(t, carry):
        at = pl.ds(pl.multiple_of(t * LANES, LANES), LANES)
        target[t + 2, own, :] = tgt[:, at]
        return carry

    lax.fori_loop(0, TILES, targets, 0)
    target[1, own, :] = xl[6]
    target[WT - 2, own, :] = xr[6]

    spans = range(BASE - 4, BASE + ROWS + 4, 8)

    def step(t, carry):
        for a in spans:
            at = pl.ds(a, 8)
            mid, f = flux(fst, coef, src, t, t - 1, t + 1, a, 8)
            rt = rate[t, at, :]
            d = rt * f
            d2[t, at, :] = d
            m = (mid + d) - target[t, at, :]
            mis[t, at, :] = m
            w[t, at, :] = m * rt
        return carry

    lax.fori_loop(1, WT - 1, step, 0)
    for tile in (0, WT - 1):
        w[tile] = jnp.zeros((WR, LANES), F32)
        w1[tile] = jnp.zeros((WR, LANES), F32)

    lane = lax.broadcasted_iota(jnp.int32, (1, LANES), 1)

    def weigh(i, carry):
        code = found[i]
        row, col = code >> 16, (code >> 6) & 127
        hit = lane == (col & 1) * NZ + (code & (NZ - 1))
        tile = col >> 1
        at = pl.ds(row, 1)
        factor = jnp.where(hit, 1.0 + OUTLET_W, 1.0)
        mis[tile, at, :] = mis[tile, at, :] * factor
        w[tile, at, :] = w[tile, at, :] * factor
        return carry

    lax.fori_loop(0, count[0], weigh, 0)

    def back(t, carry):
        for a in spans:
            at = pl.ds(a, 8)
            g = mis[t, at, :] + flux_back(w, coef, t, t - 1, t + 1, a, 8)
            grad[t, at, :] = g
            w1[t, at, :] = g * rate[t, at, :]
        return carry

    lax.fori_loop(1, WT - 1, back, 0)
    loads[0].wait()

    def last(t, carry):
        cols = pl.ds(pl.multiple_of(t * LANES, LANES), LANES)
        tw = t + 2
        for r in range(0, ROWS, 8):
            a = BASE + r
            at, rr = pl.ds(a, 8), pl.ds(r, 8)
            g = grad[tw, at, :]
            start = g + flux_back(w1, coef, tw, tw - 1, tw + 1, a, 8)
            both = mis[tw, at, :] * d2[tw, at, :] + g * d1[tw, at, :]
            kdg = (both * rate[tw, at, :]) * (power[t, rr, :] * (-BULK / STEP))
            kd_out[rr, cols] = kdg
            start_out[rr, cols] = start + kdg * kd[rr, cols] * (FREUND - 1.0) / u0[tw, at, :]
        return carry

    lax.fori_loop(0, TILES, last, 0)


def params(mib):
    return pltpu.CompilerParams(vmem_limit_bytes=mib * MIB)


def shifts(axis):
    n = lax.axis_size(axis)
    up = [(i, i + 1) for i in range(n - 1)]
    return up, [(b, a) for a, b in up]


def per_device(checkpoint, sorption_kd, velocity, source, target, cell_type, outlets):
    n_gx = lax.axis_size("gx")
    gx, gy = lax.axis_index("gx"), lax.axis_index("gy")
    lines = pl.pallas_call(
        pack_lines,
        out_shape=jax.ShapeDtypeStruct((n_gx, checkpoint.shape[1], WCOLS), F32),
        in_specs=[HB],
        out_specs=HB,
        scratch_shapes=[pltpu.SemaphoreType.DMA],
        name="pack_lines",
    )(checkpoint)
    arrived = lax.all_to_all(lines, "gx", split_axis=0, concat_axis=0, tiled=True)

    def edge_specs(lead):
        def spec(shape, index):
            if lead:
                return pl.BlockSpec((lead,) + shape, lambda i: (0,) + index)
            return pl.BlockSpec(shape, lambda i: index)
        return [
            spec((ROWS, 2 * LANES), (0, 0)),
            spec((ROWS, 2 * LANES), (0, TILES // 2 - 1)),
            spec((8, COLS), (0, 0)),
            spec((8, COLS), (ROWS // 8 - 1, 0)),
        ]

    side = jax.ShapeDtypeStruct((10, ROWS, LANES), F32)
    line = jax.ShapeDtypeStruct((7, 2, COLS), F32)
    fields = (sorption_kd, velocity, source, cell_type, target)
    whole = lambda s: pl.BlockSpec(s, lambda i: (0,) * len(s))
    to_left, to_right, to_low, to_high = pl.pallas_call(
        pack_edges,
        grid=(1,),
        out_shape=[side, side, line, line],
        in_specs=[s for f in fields for s in edge_specs(3 if f.ndim == 3 else 0)],
        out_specs=[whole(side.shape)] * 2 + [whole(line.shape)] * 2,
        name="pack_edges",
    )(*[f for f in fields for _ in range(4)])
    x_up, x_down = shifts("gx")
    y_up, y_down = shifts("gy")
    xl = lax.ppermute(to_right, "gx", x_up)
    xr = lax.ppermute(to_left, "gx", x_down)
    yl = lax.ppermute(to_high, "gy", y_up)
    yh = lax.ppermute(to_low, "gy", y_down)

    where = jnp.stack([gy * ROWS, gx * (COLS // NZ)]).astype(jnp.int32)
    found, count = pl.pallas_call(
        list_outlets,
        out_shape=[
            jax.ShapeDtypeStruct((outlets.shape[0],), jnp.int32),
            jax.ShapeDtypeStruct((1,), jnp.int32),
        ],
        in_specs=[SM, SM],
        out_specs=[SM, SM],
        name="list_outlets",
    )(outlets, where)

    edge = jnp.stack([gx, n_gx - 1 - gx, gy, lax.axis_size("gy") - 1 - gy]).astype(jnp.int32)
    message = jax.ShapeDtypeStruct((4, MCOLS), F32)
    power = jax.ShapeDtypeStruct((TILES, ROWS, LANES), F32)
    u0, fst, d1, rate, power, *rest = pl.pallas_call(
        first_half,
        out_shape=[window()] * 4 + [power] + [window()] * 8 + [message] * 2,
        in_specs=[SM] + [VM] * 3 + [HB] * 4,
        out_specs=[VM] * 15,
        scratch_shapes=[
            pltpu.VMEM((ROWS, COLS), F32),
            pltpu.VMEM((3, ROWS, COLS), F32),
            pltpu.VMEM((ROWS, COLS), F32),
            pltpu.VMEM((ROWS, COLS), jnp.int32),
            pltpu.SemaphoreType.DMA((4,)),
        ],
        compiler_params=params(24),
        name="first_half",
    )(edge, arrived, xl, xr, sorption_kd, velocity, source, cell_type)
    coefs, (up_msg, low_msg) = rest[:8], rest[8:]
    ml = lax.ppermute(up_msg, "gy", y_up)
    mh = lax.ppermute(low_msg, "gy", y_down)

    kept = (u0, fst, d1, rate, *coefs)
    plane = jax.ShapeDtypeStruct((ROWS, COLS), F32)
    work = pltpu.VMEM((WT, WR, LANES), F32)
    outs = pl.pallas_call(
        second_half,
        out_shape=[plane, plane] + [window()] * 12,
        in_specs=[SM] * 3 + [VM] * 6 + [HB] * 2 + [VM] * 13,
        out_specs=[VM] * 14,
        input_output_aliases={12 + k: 2 + k for k in range(12)},
        scratch_shapes=[
            pltpu.VMEM((ROWS, COLS), F32),
            pltpu.VMEM((ROWS, COLS), F32),
            pltpu.VMEM((7, WT, 16, LANES), F32),
            work, work, work, work, work, work,
            pltpu.SemaphoreType.DMA((2,)),
        ],
        compiler_params=params(24),
        name="second_half",
    )(edge, found, count, xl, xr, yl, yh, ml, mh, sorption_kd, target, power, *kept)
    return outs[0], outs[1]


def solution(mesh):
    return jax.shard_map(
        per_device,
        mesh=mesh,
        in_specs=(
            P("gy", "gx", None),
            P("gy", "gx"),
            P(None, "gy", "gx"),
            P("gy", "gx"),
            P("gy", "gx"),
            P("gy", "gx"),
            P(),
        ),
        out_specs=(P("gy", "gx"), P("gy", "gx")),
        check_vma=False,
    )
```

time: 654 us -> 154 us (0.24)
  the two profiles are of different devices: /device:TPU:15 before, /device:TPU:104 now
where the time goes in v1:
time: 154 us; the launch traced here: 152 us
  Pallas kernels  78.4 us (51%)
  local copies, waits for them, and re-layouts  39.2 us (25%)
  starting transfers between devices  28.1 us (18%)
  waiting for transfers between devices  5.29 us (3%)
    unnamed x66, local copies, waits for them, and re-layouts  39.2 us
    pallas_call x1, Pallas kernels, per_device(): pl.pallas_call(pack_lines, out_shape=jax.ShapeDtypeStruct((n_gx, checkpoi...  36.8 us
    pallas_call x1, Pallas kernels, per_device(): pl.pallas_call(second_half, out_shape=[plane, plane] + [window()] * 12, i...  19.3 us
    pallas_call x1, Pallas kernels, per_device(): pl.pallas_call(list_outlets, out_shape=[jax.ShapeDtypeStruct((outlets.sha...  10.2 us
    pallas_call x1, Pallas kernels, per_device(): pl.pallas_call(first_half, out_shape=[window()] * 4 + [power] + [window()...  9.01 us
    all_to_all x1, starting transfers between devices, per_device(): lax.all_to_all(lines, 'gx', split_axis=0, concat_axis=0, tiled=True)  7.29 us
    ppermute x1, starting transfers between devices, per_device(): xr = lax.ppermute(to_left, 'gx', x_down)  7.12 us
    ppermute x1, waiting for transfers between devices, per_device(): xl = lax.ppermute(to_right, 'gx', x_up)  5.28 us
  transfers between devices with their start and end apart: 7, of which 1 were waited for; matrix products, arithmetic and copies ran while one was open for 0% of the time, Pallas kernels for 15%

profile of v1, /device:TPU:104, one launch (start us, length us, event | category | flops | bytes accessed | tf_op | source)
XLA Modules:
  0.0 152.4 jit_solution(12384636789111361360)
XLA Ops:
  0.6 36.8 %pack_lines.1 = f32[16,4,4608]{2,1,0:T(4,128)} custom-call(f32[1,4,65536]{2,1,0:T(4,128)} %src.1), custom_call_target="tpu_custom_call" | custom-call | tf_op jit(solution)/shard_map/pack_lines/pallas_call | solution.py:458
  37.5 7.3 %all-to-all-start = ((f32[16,4,4608]{2,1,0:T(4,128)}), f32[16,4,4608]{2,1,0:T(4,128)}, u32[]{:S(2)}, u32[]{:S(2)}) async-start(f32[16,4,4608]{2,1,0:T(4,128)} %pack_lines.1), calls=%async_computation | async-start | bytes 2359296 | tf_op jit(solution)/shard_map/all_to_all | solution.py:466
  44.8 0.0 copy-start
  44.8 3.1 %pack_edges.1 = (f32[10,64,128]{2,1,0:T(8,128)}, f32[10,64,128]{2,1,0:T(8,128)}, f32[7,2,4096]{2,1,0:T(2,128)}, f32[7,2,4096]{2,1,0:T(2,128)}) custom-call(f32[64,4096]{1,0:T(8,128)} %kd_h.3, f32[64,4096]{1,0:T(8,128)} %kd_h.3, f32[64,4096]{1,0:T(8,128)} %kd_h.3, f32[64,4096]{1,0:T(8,128)} %kd_h.3, f32[3,64,4096]{2,1,0:T(8,128)} %v_h.1, f32[3,64,4096]{2,1,0:T(8,128)} %v_h.1, ...), custom_call_target="tpu_custom_call" | custom-call | tf_op jit(solution)/shard_map/pack_edges/pallas_call | solution.py:484
  47.9 2.0 %collective-permute-start = (f32[10,64,128]{2,1,0:T(8,128)}, f32[10,64,128]{2,1,0:T(8,128)S(1)}, u32[]{:S(2)}, u32[]{:S(2)}) collective-permute-start(f32[10,64,128]{2,1,0:T(8,128)} %get-tuple-element.27), channel_id=1, source_target_pairs={{0,8},{8,16},{16,24},{24,32},{32,40},{40,48},{48,56},{56,64},{64,7... | collective-permute-start | bytes 983048 | tf_op jit(solution)/shard_map/ppermute | solution.py:494
  49.9 7.1 %collective-permute-start.1 = (f32[10,64,128]{2,1,0:T(8,128)}, f32[10,64,128]{2,1,0:T(8,128)}, u32[]{:S(2)}, u32[]{:S(2)}) collective-permute-start(f32[10,64,128]{2,1,0:T(8,128)} %get-tuple-element.28), channel_id=1, source_target_pairs={{8,0},{16,8},{24,16},{32,24},{40,32},{48,40},{56,48},{64,56},{72,6... | collective-permute-start | bytes 983048 | tf_op jit(solution)/shard_map/ppermute | solution.py:495
  57.0 3.3 %collective-permute-start.2 = (f32[7,2,4096]{2,1,0:T(2,128)}, f32[7,2,4096]{2,1,0:T(2,128)}, u32[]{:S(2)}, u32[]{:S(2)}) collective-permute-start(f32[7,2,4096]{2,1,0:T(2,128)} %get-tuple-element.29), channel_id=1, source_target_pairs={{0,1},{1,2},{2,3},{3,4},{4,5},{5,6},{6,7},{8,9},{9,10},{10,11},{11... | collective-permute-start | bytes 688136 | tf_op jit(solution)/shard_map/ppermute | solution.py:496
  60.4 2.5 %collective-permute-start.3 = (f32[7,2,4096]{2,1,0:T(2,128)}, f32[7,2,4096]{2,1,0:T(2,128)}, u32[]{:S(2)}, u32[]{:S(2)}) collective-permute-start(f32[7,2,4096]{2,1,0:T(2,128)} %get-tuple-element.30), channel_id=1, source_target_pairs={{1,0},{2,1},{3,2},{4,3},{5,4},{6,5},{7,6},{9,8},{10,9},{11,10},{12... | collective-permute-start | bytes 688136 | tf_op jit(solution)/shard_map/ppermute | solution.py:497
  62.9 0.1 pad_add_fusion.place
  63.0 5.3 %collective-permute-done.xl = f32[10,64,128]{2,1,0:T(8,128)S(1)} collective-permute-done((f32[10,64,128]{2,1,0:T(8,128)}, f32[10,64,128]{2,1,0:T(8,128)S(1)}, u32[]{:S(2)}, u32[]{:S(2)}) %collective-permute-start) | collective-permute-done | bytes 327712 | tf_op jit(solution)/shard_map/ppermute | solution.py:494
  68.3 0.0 collective-permute-done.1.xr
  68.3 0.0 all-to-all-done.lines
  68.3 0.0 copy-done
  68.3 0.0 copy-start.1
  68.3 1.2 copy-done.1
  69.5 0.0 copy-start.4
  69.5 1.2 copy-done.4
  70.7 0.0 copy-start.5
  70.7 1.2 copy-done.5
  72.0 9.0 %first_half.1 = (f32[36,80,128]{2,1,0:T(8,128)S(1)}, f32[36,80,128]{2,1,0:T(8,128)S(1)}, f32[36,80,128]{2,1,0:T(8,128)S(1)}, f32[36,80,128]{2,1,0:T(8,128)S(1)},...) custom-call(s32[4]{0:T(128)S(1)} %pad_add_fusion.place, ...), custom_call_target="tpu_custom_call" | custom-call | tf_op jit(solution)/shard_map/first_half/pallas_call | solution.py:514
  81.0 0.0 copy-start.6
  81.0 1.2 copy-done.6
  82.1 0.0 copy-start.8
  82.1 1.1 copy-done.8
  83.3 0.0 copy-start.10
  83.3 1.1 copy-done.10
  84.4 0.0 copy-start.12
  84.4 1.2 copy-done.12
  85.5 0.0 copy-start.14
  85.6 1.1 copy-done.14
  86.7 1.2 copy-done.16
  87.9 1.1 copy-done.18
  89.0 1.1 copy-done.20
  90.1 1.2 copy-done.22
  91.3 1.1 copy-done.24
  92.5 1.1 copy-done.26
  93.6 1.1 copy-done.28
  94.7 1.0 copy-done.30
  95.7 2.8 %collective-permute-start.4 = (f32[4,5120]{1,0:T(4,128)}, f32[4,5120]{1,0:T(4,128)S(1)}, u32[]{:S(2)}, u32[]{:S(2)}) collective-permute-start(f32[4,5120]{1,0:T(4,128)} %get-tuple-element.31), channel_id=1, source_target_pairs={{0,1},{1,2},{2,3},{3,4},{4,5},{5,6},{6,7},{8,9},{9,10},{10,11},{11... | collective-permute-start | bytes 245768 | tf_op jit(solution)/shard_map/ppermute | solution.py:530
  98.5 3.0 %collective-permute-start.5 = (f32[4,5120]{1,0:T(4,128)}, f32[4,5120]{1,0:T(4,128)S(1)}, u32[]{:S(2)}, u32[]{:S(2)}) collective-permute-start(f32[4,5120]{1,0:T(4,128)} %get-tuple-element.32), channel_id=1, source_target_pairs={{1,0},{2,1},{3,2},{4,3},{5,4},{6,5},{7,6},{9,8},{10,9},{11,10},{12... | collective-permute-start | bytes 245768 | tf_op jit(solution)/shard_map/ppermute | solution.py:531
  101.5 0.6 pad_add_fusion.1.place
  102.1 10.2 %list_outlets.1 = (s32[1024]{0:T(1024)}, s32[1]{0:T(128)}) custom-call(s32[1024]{0:T(1024)} %outlets.1, s32[2]{0:T(128)} %pad_add_fusion.1.place), custom_call_target="tpu_custom_call" | custom-call | tf_op jit(solution)/shard_map/list_outlets/pallas_call | solution.py:500
  112.3 0.0 collective-permute-done.2.yl
  112.3 0.0 collective-permute-done.3.yh
  112.3 0.0 collective-permute-done.4.ml
  112.3 0.0 collective-permute-done.5.mh
  112.3 0.0 copy-start.2
  112.3 1.2 copy-done.2
  113.6 1.2 copy-done.3
  114.8 1.4 copy-done.7
  116.2 1.4 copy-done.9
  117.5 1.4 copy-done.11
  118.9 1.4 copy-done.13
  120.3 1.4 copy-done.15
  121.6 1.4 copy-done.17
  123.0 1.4 copy-done.19
  124.4 1.4 copy-done.21
  125.8 1.4 copy-done.23
  127.1 1.4 copy-done.25
  128.5 1.4 copy-done.27
  129.9 1.4 copy-done.29
  131.3 1.2 copy-done.31
  132.5 0.7 copy-done.32
  133.2 19.3 %second_half.1 = (f32[64,4096]{1,0:T(8,128)}, f32[64,4096]{1,0:T(8,128)}, f32[36,80,128]{2,1,0:T(8,128)S(1)}, f32[36,80,128]{2,1,0:T(8,128)S(1)}, f32[36,80,128]...) custom-call(s32[4]{0:T(128)S(1)} %pad_add_fusion.place, ...), custom_call_target="tpu_custom_call", output_to_operand_aliasing={{2}: (12, {}), {3}: (13, {}), {4}: (14, {}), {5}: (15, {}),... | custom-call | tf_op jit(solution)/shard_map/second_half/pallas_call | solution.py:536
  (23 shorter events, 0.0 us)
Async XLA Ops:
  37.5 30.8 %all-to-all-start = ((f32[16,4,4608]{2,1,0:T(4,128)}), f32[16,4,4608]{2,1,0:T(4,128)}, u32[]{:S(2)}, u32[]{:S(2)}) async-start(f32[16,4,4608]{2,1,0:T(4,128)} %pack_lines.1), calls=%async_computation | async-start | bytes 2359296 | tf_op jit(solution)/shard_map/all_to_all | solution.py:466
  44.8 23.5 %copy-start = (f32[3,64,4096]{2,1,0:T(8,128)S(1)}, f32[3,64,4096]{2,1,0:T(8,128)}, u32[]{:S(2)}) copy-start(f32[3,64,4096]{2,1,0:T(8,128)} %v_h.1) | copy-start | bytes 9437188
  47.9 20.4 %collective-permute-start = (f32[10,64,128]{2,1,0:T(8,128)}, f32[10,64,128]{2,1,0:T(8,128)S(1)}, u32[]{:S(2)}, u32[]{:S(2)}) collective-permute-start(f32[10,64,128]{2,1,0:T(8,128)} %get-tuple-element.27), channel_id=1, source_target_pairs={{0,8},{8,16},{16,24},{24,32},{32,40},{40,48},{48,56},{56,64},{64,7... | collective-permute-start | bytes 983048 | tf_op jit(solution)/shard_map/ppermute | solution.py:494
  49.9 18.4 %collective-permute-start.1 = (f32[10,64,128]{2,1,0:T(8,128)}, f32[10,64,128]{2,1,0:T(8,128)}, u32[]{:S(2)}, u32[]{:S(2)}) collective-permute-start(f32[10,64,128]{2,1,0:T(8,128)} %get-tuple-element.28), channel_id=1, source_target_pairs={{8,0},{16,8},{24,16},{32,24},{40,32},{48,40},{56,48},{64,56},{72,6... | collective-permute-start | bytes 983048 | tf_op jit(solution)/shard_map/ppermute | solution.py:495
  57.0 55.2 %collective-permute-start.2 = (f32[7,2,4096]{2,1,0:T(2,128)}, f32[7,2,4096]{2,1,0:T(2,128)}, u32[]{:S(2)}, u32[]{:S(2)}) collective-permute-start(f32[7,2,4096]{2,1,0:T(2,128)} %get-tuple-element.29), channel_id=1, source_target_pairs={{0,1},{1,2},{2,3},{3,4},{4,5},{5,6},{6,7},{8,9},{9,10},{10,11},{11... | collective-permute-start | bytes 688136 | tf_op jit(solution)/shard_map/ppermute | solution.py:496
  60.4 51.9 %collective-permute-start.3 = (f32[7,2,4096]{2,1,0:T(2,128)}, f32[7,2,4096]{2,1,0:T(2,128)}, u32[]{:S(2)}, u32[]{:S(2)}) collective-permute-start(f32[7,2,4096]{2,1,0:T(2,128)} %get-tuple-element.30), channel_id=1, source_target_pairs={{1,0},{2,1},{3,2},{4,3},{5,4},{6,5},{7,6},{9,8},{10,9},{11,10},{12... | collective-permute-start | bytes 688136 | tf_op jit(solution)/shard_map/ppermute | solution.py:497
  68.3 1.2 copy-start.1
  69.5 1.2 copy-start.4
  70.7 1.2 copy-start.5
  81.0 1.2 copy-start.6
  82.1 1.1 copy-start.8
  83.3 1.1 copy-start.10
  84.4 1.2 copy-start.12
  85.5 1.1 copy-start.14
  86.7 1.2 copy-start.16
  87.9 1.1 copy-start.18
  89.0 1.1 copy-start.20
  90.1 1.2 copy-start.22
  91.3 1.1 copy-start.24
  92.5 1.1 copy-start.26
  93.6 1.1 copy-start.28
  94.7 1.0 copy-start.30
  95.7 16.6 %collective-permute-start.4 = (f32[4,5120]{1,0:T(4,128)}, f32[4,5120]{1,0:T(4,128)S(1)}, u32[]{:S(2)}, u32[]{:S(2)}) collective-permute-start(f32[4,5120]{1,0:T(4,128)} %get-tuple-element.31), channel_id=1, source_target_pairs={{0,1},{1,2},{2,3},{3,4},{4,5},{5,6},{6,7},{8,9},{9,10},{10,11},{11... | collective-permute-start | bytes 245768 | tf_op jit(solution)/shard_map/ppermute | solution.py:530
  98.5 13.8 %collective-permute-start.5 = (f32[4,5120]{1,0:T(4,128)}, f32[4,5120]{1,0:T(4,128)S(1)}, u32[]{:S(2)}, u32[]{:S(2)}) collective-permute-start(f32[4,5120]{1,0:T(4,128)} %get-tuple-element.32), channel_id=1, source_target_pairs={{1,0},{2,1},{3,2},{4,3},{5,4},{6,5},{7,6},{9,8},{10,9},{11,10},{12... | collective-permute-start | bytes 245768 | tf_op jit(solution)/shard_map/ppermute | solution.py:531
  112.3 1.2 copy-start.2
  113.5 1.2 copy-start.3
  114.8 1.4 copy-start.7
  116.1 1.4 copy-start.9
  117.5 1.4 copy-start.11
  118.9 1.4 copy-start.13
  120.3 1.4 copy-start.15
  121.6 1.4 copy-start.17
  123.0 1.4 copy-start.19
  124.4 1.4 copy-start.21
  125.8 1.4 copy-start.23
  127.1 1.4 copy-start.25
  128.5 1.4 copy-start.27
  129.9 1.4 copy-start.29
  131.3 1.2 copy-start.31
  132.5 0.7 copy-start.32

commit v2 on v1

v2 whole, which is shorter than its diff:
```python
import jax
import jax.numpy as jnp
from jax import lax
from jax.experimental import pallas as pl
from jax.experimental.pallas import tpu as pltpu
from jax.sharding import PartitionSpec as P

NZ = 64
BULK = 4.0
FREUND = 0.7
DISP = 0.1
DRAIN = 0.5
STEP = 0.4
OUTLET_W = 4.0

LANES = 128
ROWS = 64
TILES = 32
WT = TILES + 4
WR = 80
BASE = 8
COLS = TILES * LANES
WCOLS = WT * LANES
MCOLS = WCOLS + 4 * LANES
F32 = jnp.float32
MIB = 1 << 20
FIRST_MIB = 30
UNROLL = 2

VM = pl.BlockSpec(memory_space=pltpu.VMEM)
SM = pl.BlockSpec(memory_space=pltpu.SMEM)
HB = pl.BlockSpec(memory_space=pltpu.HBM)


def window(dtype=F32):
    return jax.ShapeDtypeStruct((WT, WR, LANES), dtype)


def lane_iota(rows):
    return lax.broadcasted_iota(jnp.int32, (rows, LANES), 1)


def pack_lines(src, out, sem):
    n = out.shape[0]
    copies = []
    for i in range(n):
        low = i * COLS - 2 * LANES
        high = low + WCOLS
        pieces = [(max(low, 0), min(high, n * COLS), max(-low, 0))]
        if low < 0:
            pieces.append((0, 2 * LANES, 0))
        if high > n * COLS:
            pieces.append((n * COLS - 2 * LANES, n * COLS, WCOLS - 2 * LANES))
        for a, b, at in pieces:
            copies.append(
                pltpu.make_async_copy(
                    src.at[0, :, a:b], out.at[i, :, at : at + b - a], sem
                )
            )
    for c in copies:
        c.start()
    for c in copies:
        c.wait()


def pack_fields(kd, v, s, c, t, stack, to_left, to_right, to_low, to_high):
    step, last = pl.program_id(0), pl.num_programs(0) - 1
    kind = c[...]
    fields = (
        kd[...], v[0], v[1], v[2],
        jnp.where(kind == 1, s[...], 0.0),
        jnp.where(kind == 2, DRAIN, 0.0).astype(F32),
    )
    for f, val in enumerate(fields):
        stack[f] = val
    for f, val in enumerate(fields + (t[...],)):
        to_low[f] = val[0:2]
        to_high[f] = val[ROWS - 2 : ROWS]
    lo = lane_iota(ROWS) < NZ

    def layers(out, near, far, low_side):
        for f in range(6):
            out[f] = stack[f, :, near]
        out[6] = t[:, near]
        for p in range(3):
            first, second = stack[2 * p, :, far], stack[2 * p + 1, :, far]
            if low_side:
                second = pltpu.roll(second, NZ, 1)
            else:
                first = pltpu.roll(first, NZ, 1)
            out[7 + p] = jnp.where(lo, first, second)

    width = kd.shape[1]

    @pl.when(step == 0)
    def _():
        layers(to_left, slice(0, LANES), slice(LANES, 2 * LANES), True)

    @pl.when(step == last)
    def _():
        layers(to_right, slice(width - LANES, width), slice(width - 2 * LANES, width - LANES), False)


def list_outlets(codes, found, count):
    unroll = 32

    def step(i, n):
        values = [codes[i * unroll + k] for k in range(unroll)]
        for value in values:
            found[n] = value
            n = n + 1 + (value >> 31)
        return n

    count[0] = lax.fori_loop(0, codes.shape[0] // unroll, step, jnp.int32(0))


def coefficients(v0, v1, v2, drain):
    z = lax.broadcasted_iota(jnp.int32, v0.shape, v0.ndim - 1) & (NZ - 1)
    north = DISP - jnp.minimum(v0, 0.0)
    south = DISP + jnp.maximum(v0, 0.0)
    east = DISP - jnp.minimum(v1, 0.0)
    west = DISP + jnp.maximum(v1, 0.0)
    up = jnp.where(z == NZ - 1, 0.0, DISP - jnp.minimum(v2, 0.0))
    down = jnp.where(z == 0, 0.0, DISP + jnp.maximum(v2, 0.0))
    centre = ((north + south) + (east + west)) + ((up + down) + drain)
    return north, south, east, west, up, down, centre


def east_of(u, t, right, a, rows):
    here = pl.ds(a, rows)
    lo = lane_iota(rows) < NZ
    return pltpu.roll(jnp.where(lo, u[right, here, :], u[t, here, :]), NZ, 1)


def flux(u, coef, src, t, right, a, rows, west):
    cn, cs, ce, cw, cu, cd, cc = coef
    here = pl.ds(a, rows)
    mid = u[t, here, :]
    north = u[t, pl.ds(a + 1, rows), :]
    south = u[t, pl.ds(a - 1, rows), :]
    east = east_of(u, t, right, a, rows)
    upper = pltpu.roll(mid, LANES - 1, 1)
    lower = pltpu.roll(mid, 1, 1)
    plane = cn[t, here, :] * north + cs[t, here, :] * south
    plane = plane + (ce[t, here, :] * east + cw[t, here, :] * west)
    plane = plane + (cu[t, here, :] * upper + cd[t, here, :] * lower)
    return mid, plane + (src[t, here, :] - cc[t, here, :] * mid), east


def flux_back(w, coef, t, left, right, a, rows):
    cn, cs, ce, cw, cu, cd, cc = coef
    here = pl.ds(a, rows)
    above, below = pl.ds(a + 1, rows), pl.ds(a - 1, rows)
    lo = lane_iota(rows) < NZ
    mid = w[t, here, :]
    w_right, w_left = w[right, here, :], w[left, here, :]
    from_low = cw[right, here, :] * w_right + ce[t, here, :] * mid
    from_high = cw[t, here, :] * mid + ce[left, here, :] * w_left
    total = pltpu.roll(jnp.where(lo, from_low, from_high), NZ, 1)
    total = total + (cs[t, above, :] * w[t, above, :] + cn[t, below, :] * w[t, below, :])
    total = total + pltpu.roll(cd[t, here, :] * mid, LANES - 1, 1)
    total = total + pltpu.roll(cu[t, here, :] * mid, 1, 1)
    return total - cc[t, here, :] * mid


def sorb(u):
    return jnp.exp((FREUND - 1.0) * jnp.log(u))


def rate_of(kd, power):
    return STEP / (1.0 + BULK * kd * power)


def first_half(place, found, count, lines, xl, xr, stack_h,
               u0, fst, d1, rate, power, cn, cs, ce, cw, cu, cd, cc, src, msg_a, msg_b,
               stack, sems):
    loads = [
        pltpu.make_async_copy(stack_h.at[k], stack.at[k], sems.at[k]) for k in range(6)
    ]
    for load in loads:
        load.start()
    coef = (cn, cs, ce, cw, cu, cd, cc)
    own = pl.ds(BASE, ROWS)
    lines_of = lines.shape[1]
    for k in range(lines.shape[0]):
        for t in range(WT):
            u0[t, BASE + lines_of * k : BASE + lines_of * (k + 1), :] = lines[
                k, :, t * LANES : (t + 1) * LANES
            ]
    lo = lane_iota(ROWS) < NZ

    def third(ref, f, high):
        both = ref[7 + f // 2]
        if high:
            return jnp.where(lo, 0.0, both if f % 2 else pltpu.roll(both, NZ, 1))
        return jnp.where(lo, pltpu.roll(both, NZ, 1) if f % 2 else both, 0.0)

    for tile, fields in (
        (0, [third(xl, f, True) for f in range(6)]),
        (1, [xl[f] for f in range(6)]),
        (WT - 2, [xr[f] for f in range(6)]),
        (WT - 1, [third(xr, f, False) for f in range(6)]),
    ):
        for ref, val in zip(coef, coefficients(*fields[1:4], fields[5])):
            ref[tile, own, :] = val
        src[tile, own, :] = fields[4]
        rate[tile, own, :] = rate_of(fields[0], sorb(u0[tile, own, :]))

    @pl.when(place[0] == 0)
    def _():
        for ref in (u0, rate):
            ref[0:2, own, :] = jnp.zeros((2, ROWS, LANES), F32)

    @pl.when(place[1] == 0)
    def _():
        for ref in (u0, rate):
            ref[WT - 2 : WT, own, :] = jnp.zeros((2, ROWS, LANES), F32)

    for load in loads:
        load.wait()

    def prepare(t, carry):
        cols = pl.ds(pl.multiple_of(t * LANES, LANES), LANES)
        for r in range(0, ROWS, 8):
            rr, at = pl.ds(r, 8), pl.ds(BASE + r, 8)
            p = sorb(u0[t + 2, at, :])
            power[t, rr, :] = p
            rate[t + 2, at, :] = rate_of(stack[0, rr, cols], p)
            values = coefficients(
                stack[1, rr, cols], stack[2, rr, cols], stack[3, rr, cols], stack[5, rr, cols]
            )
            for ref, val in zip(coef, values):
                ref[t + 2, at, :] = val
            src[t + 2, at, :] = stack[4, rr, cols]
        return carry

    lax.fori_loop(0, TILES, prepare, 0, unroll=2)

    spans = range(BASE, BASE + ROWS, 8)

    def step(t, wests):
        right = jnp.minimum(t + 1, WT - 1)
        easts = []
        for a, west in zip(spans, wests):
            at = pl.ds(a, 8)
            mid, f, east = flux(u0, coef, src, t, right, a, 8, west)
            d = rate[t, at, :] * f
            d1[t, at, :] = d
            fst[t, at, :] = mid + d
            easts.append(east)
        return tuple(easts)

    zero = jnp.zeros((8, LANES), F32)
    lax.fori_loop(0, WT, step, (zero,) * len(spans), unroll=UNROLL)

    top = BASE + ROWS
    odd = place[4] == 1

    def send(at, row, up, low):
        msg_a[row, at] = jnp.where(odd, low, up)
        msg_b[row, at] = jnp.where(odd, up, low)

    for t in range(WT):
        at = pl.ds(t * LANES, LANES)
        send(at, slice(0, 2), u0[t, top - 2 : top, :], u0[t, BASE : BASE + 2, :])
        send(at, slice(2, 4), fst[t, top - 3 : top - 1, :], fst[t, BASE + 1 : BASE + 3, :])
    blank = jnp.zeros((1, LANES), F32)
    for k in range(16):
        at = pl.ds(WCOLS + (k % 4) * LANES, LANES)
        row = slice(k // 4, k // 4 + 1)
        side = xr if k % 2 else xl
        if k < 14:
            send(at, row, side[k // 2, ROWS - 1 : ROWS, :], side[k // 2, 0:1, :])
        else:
            send(at, row, blank, blank)


def second_half(place, found, count, xl, xr, yl, yh, msg_a, msg_b, kd_h, t_h, power,
                u0_in, fst_in, d1_in, rate_in, cn_in, cs_in, ce_in, cw_in, cu_in, cd_in, cc_in, src_in,
                kd_out_h, start_out_h,
                u0, fst, d1, rate, cn, cs, ce, cw, cu, cd, cc, src,
                kd, tgt, kd_out, start_out, halo, target, d2, mis, w, grad, w1, sems):
    loads = [
        pltpu.make_async_copy(a, b, sems.at[k, 0]) for k, (a, b) in enumerate(((kd_h, kd), (t_h, tgt)))
    ]
    for load in loads:
        load.start()
    coef = (cn, cs, ce, cw, cu, cd, cc)
    low8, high8 = slice(0, BASE), slice(BASE + ROWS, WR)
    own = pl.ds(BASE, ROWS)

    top = BASE + ROWS
    odd = place[4] == 1

    def arrived(row, at):
        one, two = msg_a[row, at], msg_b[row, at]
        return jnp.where(odd, one, two), jnp.where(odd, two, one)

    blank = jnp.zeros((16, LANES), F32)
    for f in range(7):
        for tile in (0, 1, WT - 2, WT - 1):
            halo[f, tile] = blank
        for t in range(TILES):
            at = pl.ds(t * LANES, LANES)
            halo[f, t + 2, 6:8, :] = yl[f, :, at]
            halo[f, t + 2, 8:10, :] = yh[f, :, at]
        for side, tile in ((0, 1), (1, WT - 2)):
            k = 2 * f + side
            low, high = arrived(slice(k // 4, k // 4 + 1), pl.ds(WCOLS + (k % 4) * LANES, LANES))
            halo[f, tile, 7:8, :] = low
            halo[f, tile, 8:9, :] = high
    for t in range(WT):
        at = pl.ds(t * LANES, LANES)
        low, high = arrived(slice(0, 4), at)
        u0[t, 6:8, :] = low[0:2]
        fst[t, 5:7, :] = low[2:4]
        u0[t, top : top + 2, :] = high[0:2]
        fst[t, top + 1 : top + 3, :] = high[2:4]

    def edges(t, carry):
        for a, to in ((0, low8), (8, high8)):
            at = pl.ds(a, 8)
            values = coefficients(halo[1, t, at, :], halo[2, t, at, :], halo[3, t, at, :], halo[5, t, at, :])
            for ref, val in zip(coef, values):
                ref[t, to, :] = val
            src[t, to, :] = halo[4, t, at, :]
            rate[t, to, :] = rate_of(halo[0, t, at, :], sorb(u0[t, to, :]))
            target[t, to, :] = halo[6, t, at, :]
        return carry

    lax.fori_loop(0, WT, edges, 0, unroll=6)

    zero8 = jnp.zeros((WT, BASE, LANES), F32)

    @pl.when(place[0] == 0)
    def _():
        rate[0:2] = jnp.zeros((2, WR, LANES), F32)
        u0[0:2] = jnp.zeros((2, WR, LANES), F32)

    @pl.when(place[1] == 0)
    def _():
        rate[WT - 2 : WT] = jnp.zeros((2, WR, LANES), F32)
        u0[WT - 2 : WT] = jnp.zeros((2, WR, LANES), F32)

    @pl.when(place[2] == 0)
    def _():
        rate[:, low8, :] = zero8
        u0[:, low8, :] = zero8
        fst[:, low8, :] = zero8

    @pl.when(place[3] == 0)
    def _():
        rate[:, high8, :] = zero8
        u0[:, high8, :] = zero8
        fst[:, high8, :] = zero8

    edge_spans = ((BASE - 4, BASE - 1), (top - 4, top - 1))

    def edge_step(t, wests):
        right = jnp.minimum(t + 1, WT - 1)
        easts = []
        for (a, r0), west in zip(edge_spans, wests):
            at = pl.ds(a, 8)
            row = lax.broadcasted_iota(jnp.int32, (8, LANES), 0) + a
            new = (row == r0) | (row == r0 + 1)
            mid, f, east = flux(u0, coef, src, t, right, a, 8, west)
            d = rate[t, at, :] * f
            d1[t, at, :] = jnp.where(new, d, d1[t, at, :])
            fst[t, at, :] = jnp.where(new, mid + d, fst[t, at, :])
            easts.append(east)
        return tuple(easts)

    zero = jnp.zeros((8, LANES), F32)
    lax.fori_loop(0, WT, edge_step, (zero, zero), unroll=6)

    loads[1].wait()

    def targets(t, carry):
        at = pl.ds(pl.multiple_of(t * LANES, LANES), LANES)
        target[t + 2, own, :] = tgt[:, at]
        return carry

    lax.fori_loop(0, TILES, targets, 0)
    target[1, own, :] = xl[6]
    target[WT - 2, own, :] = xr[6]

    spans = range(BASE - 4, BASE + ROWS + 4, 8)

    def step(t, wests):
        easts = []
        for a, west in zip(spans, wests):
            at = pl.ds(a, 8)
            mid, f, east = flux(fst, coef, src, t, t + 1, a, 8, west)
            rt = rate[t, at, :]
            d = rt * f
            d2[t, at, :] = d
            m = (mid + d) - target[t, at, :]
            mis[t, at, :] = m
            w[t, at, :] = m * rt
            easts.append(east)
        return tuple(easts)

    lax.fori_loop(1, WT - 1, step, tuple(east_of(fst, 0, 1, a, 8) for a in spans), unroll=UNROLL)

    lane = lax.broadcasted_iota(jnp.int32, (1, LANES), 1)

    def weigh(i, carry):
        code = found[i]
        row, col = code >> 16, (code >> 6) & 127
        hit = lane == (col & 1) * NZ + (code & (NZ - 1))
        tile = col >> 1
        at = pl.ds(row, 1)
        factor = jnp.where(hit, 1.0 + OUTLET_W, 1.0)
        mis[tile, at, :] = mis[tile, at, :] * factor
        w[tile, at, :] = w[tile, at, :] * factor
        return carry

    lax.fori_loop(0, count[0], weigh, 0)

    def back(t, carry):
        for a in spans:
            at = pl.ds(a, 8)
            g = mis[t, at, :] + flux_back(w, coef, t, t - 1, t + 1, a, 8)
            grad[t, at, :] = g
            w1[t, at, :] = g * rate[t, at, :]
        return carry

    lax.fori_loop(1, WT - 1, back, 0, unroll=UNROLL)
    loads[0].wait()

    def last(t, carry):
        cols = pl.ds(pl.multiple_of(t * LANES, LANES), LANES)
        tw = t + 2
        for r in range(0, ROWS, 8):
            a = BASE + r
            at, rr = pl.ds(a, 8), pl.ds(r, 8)
            g = grad[tw, at, :]
            start = g + flux_back(w1, coef, tw, tw - 1, tw + 1, a, 8)
            both = mis[tw, at, :] * d2[tw, at, :] + g * d1[tw, at, :]
            kdg = (both * rate[tw, at, :]) * (power[t, rr, :] * (-BULK / STEP))
            kd_out[rr, cols] = kdg
            start_out[rr, cols] = start + kdg * kd[rr, cols] * (FREUND - 1.0) / u0[tw, at, :]
        return carry

    parts = 4
    stores = []
    for k in range(parts):
        lax.fori_loop(k * TILES // parts, (k + 1) * TILES // parts, last, 0, unroll=UNROLL)
        cols = pl.ds(k * COLS // parts, COLS // parts)
        for a, b, n in ((kd_out, kd_out_h, 2), (start_out, start_out_h, 3)):
            stores.append(pltpu.make_async_copy(a.at[:, cols], b.at[:, cols], sems.at[n, k]))
            stores[-1].start()
    for store in stores:
        store.wait()


def params(mib):
    return pltpu.CompilerParams(vmem_limit_bytes=mib * MIB)


def shifts(axis):
    n = lax.axis_size(axis)
    up = [(i, i + 1) for i in range(n - 1)]
    return up, [(b, a) for a, b in up]


def per_device(checkpoint, sorption_kd, velocity, source, target, cell_type, outlets):
    n_gx = lax.axis_size("gx")
    gx, gy = lax.axis_index("gx"), lax.axis_index("gy")
    lines = pl.pallas_call(
        pack_lines,
        out_shape=jax.ShapeDtypeStruct((n_gx, checkpoint.shape[1], WCOLS), F32),
        in_specs=[HB],
        out_specs=VM,
        scratch_shapes=[pltpu.SemaphoreType.DMA],
        compiler_params=params(60),
        name="pack_lines",
    )(checkpoint)
    arrived = lax.all_to_all(lines, "gx", split_axis=0, concat_axis=0, tiled=True)

    side = jax.ShapeDtypeStruct((10, ROWS, LANES), F32)
    line = jax.ShapeDtypeStruct((7, 2, COLS), F32)
    blocks = 8
    part = COLS // blocks
    flat = pl.BlockSpec((ROWS, part), lambda i: (0, i))
    deep = lambda *lead: pl.BlockSpec(lead + (part,), lambda i: (0, 0, i))
    kept = pl.BlockSpec(side.shape, lambda i: (0, 0, 0))
    stack, to_left, to_right, to_low, to_high = pl.pallas_call(
        pack_fields,
        grid=(blocks,),
        out_shape=[jax.ShapeDtypeStruct((6, ROWS, COLS), F32), side, side, line, line],
        in_specs=[flat, deep(3, ROWS), flat, flat, flat],
        out_specs=[deep(6, ROWS), kept, kept, deep(7, 2), deep(7, 2)],
        compiler_params=params(60),
        name="pack_fields",
    )(sorption_kd, velocity, source, cell_type, target)
    x_up, x_down = shifts("gx")
    y_up, y_down = shifts("gy")
    xl = lax.ppermute(to_right, "gx", x_up)
    xr = lax.ppermute(to_left, "gx", x_down)
    yl = lax.ppermute(to_high, "gy", y_up)
    yh = lax.ppermute(to_low, "gy", y_down)

    row = (outlets >> 16) - gy * ROWS + BASE
    col = ((outlets >> 6) & 1023) - gx * (COLS // NZ) + 4
    inside = (row >= BASE - 2) & (row < BASE + ROWS + 2) & (col >= 2) & (col < 70)
    codes = jnp.where(inside, (row << 16) + (col << 6) + (outlets & (NZ - 1)), -1)
    found, count = pl.pallas_call(
        list_outlets,
        out_shape=[
            jax.ShapeDtypeStruct((outlets.shape[0],), jnp.int32),
            jax.ShapeDtypeStruct((1,), jnp.int32),
        ],
        in_specs=[SM],
        out_specs=[SM, SM],
        compiler_params=params(1),
        name="list_outlets",
    )(codes)

    n_gy = lax.axis_size("gy")
    edge = jnp.stack([gx, n_gx - 1 - gx, gy, n_gy - 1 - gy, gy % 2]).astype(jnp.int32)
    message = jax.ShapeDtypeStruct((4, MCOLS), F32)
    power = jax.ShapeDtypeStruct((TILES, ROWS, LANES), F32)
    u0, fst, d1, rate, power, *rest = pl.pallas_call(
        first_half,
        out_shape=[window()] * 4 + [power] + [window()] * 8 + [message] * 2,
        in_specs=[SM] * 3 + [VM] * 3 + [HB],
        out_specs=[VM] * 15,
        scratch_shapes=[pltpu.VMEM((6, ROWS, COLS), F32), pltpu.SemaphoreType.DMA((6,))],
        compiler_params=params(FIRST_MIB),
        name="first_half",
    )(edge, found, count, arrived, xl, xr, stack)
    coefs, (msg_a, msg_b) = rest[:8], rest[8:]
    got_a = lax.ppermute(msg_a, "gy", [(i, i + 1 - 2 * (i % 2)) for i in range(n_gy)])
    got_b = lax.ppermute(msg_b, "gy", [(i, (i - 1 + 2 * (i % 2)) % n_gy) for i in range(n_gy)])

    kept = (u0, fst, d1, rate, *coefs)
    plane = jax.ShapeDtypeStruct((ROWS, COLS), F32)
    work = pltpu.VMEM((WT, WR, LANES), F32)
    outs = pl.pallas_call(
        second_half,
        out_shape=[plane, plane] + [window()] * 12,
        in_specs=[SM] * 3 + [VM] * 6 + [HB] * 2 + [VM] * 13,
        out_specs=[HB] * 2 + [VM] * 12,
        input_output_aliases={12 + k: 2 + k for k in range(12)},
        scratch_shapes=[
            *[pltpu.VMEM((ROWS, COLS), F32)] * 4,
            pltpu.VMEM((7, WT, 16, LANES), F32),
            work, work, work, work, work, work,
            pltpu.SemaphoreType.DMA((4, 4)),
        ],
        compiler_params=params(24),
        name="second_half",
    )(edge, found, count, xl, xr, yl, yh, got_a, got_b, sorption_kd, target, power, *kept)
    return outs[0], outs[1]


def solution(mesh):
    return jax.shard_map(
        per_device,
        mesh=mesh,
        in_specs=(
            P("gy", "gx", None),
            P("gy", "gx"),
            P(None, "gy", "gx"),
            P("gy", "gx"),
            P("gy", "gx"),
            P("gy", "gx"),
            P(),
        ),
        out_specs=(P("gy", "gx"), P("gy", "gx")),
        check_vma=False,
    )
```

time: 154 us -> 65.7 us (0.43)
  the two profiles are of different devices: /device:TPU:104 before, /device:TPU:64 now
where the time goes in v2:
time: 65.7 us; the launch traced here: 65.1 us
  Pallas kernels  33.7 us (51%)
  starting transfers between devices  27.8 us (42%)
  waiting for transfers between devices  2.81 us (4%)
  between operations  0.75 us (1%)
    pallas_call x1, Pallas kernels, per_device(): pl.pallas_call(second_half, out_shape=[plane, plane] + [window()] * 12, i...  10.6 us
    pallas_call x1, Pallas kernels, per_device(): pl.pallas_call(pack_fields, grid=(blocks,), out_shape=[jax.ShapeDtypeStru...  8.54 us
    pallas_call x1, Pallas kernels, per_device(): pl.pallas_call(first_half, out_shape=[window()] * 4 + [power] + [window()...  7.92 us
    all_to_all x1, starting transfers between devices, per_device(): lax.all_to_all(lines, 'gx', split_axis=0, concat_axis=0, tiled=True)  7.29 us
    ppermute x1, starting transfers between devices, per_device(): xr = lax.ppermute(to_left, 'gx', x_down)  7.12 us
    pallas_call x1, Pallas kernels, per_device(): pl.pallas_call(list_outlets, out_shape=[jax.ShapeDtypeStruct((outlets.sha...  4.3 us
    ppermute x1, starting transfers between devices, per_device(): lax.ppermute(msg_b, 'gy', [(i, (i - 1 + 2 * (i % 2)) % n_gy) for i in ran...  3.74 us
    ppermute x1, starting transfers between devices, per_device(): yl = lax.ppermute(to_high, 'gy', y_up)  3.54 us
  transfers between devices with their start and end apart: 7, of which 1 were waited for; matrix products, arithmetic and copies ran while one was open for 0% of the time, Pallas kernels for 32%

profile of v2, /device:TPU:64, one launch (start us, length us, event | category | flops | bytes accessed | tf_op | source)
XLA Modules:
  0.0 65.1 jit_solution(8528877438676679481)
XLA Ops:
  0.6 2.4 %pack_lines.1 = f32[16,4,4608]{2,1,0:T(4,128)} custom-call(f32[1,4,65536]{2,1,0:T(4,128)} %src.1), custom_call_target="tpu_custom_call" | custom-call | tf_op jit(solution)/shard_map/pack_lines/pallas_call | solution.py:470
  3.0 7.3 %all-to-all-start = ((f32[16,4,4608]{2,1,0:T(4,128)}), f32[16,4,4608]{2,1,0:T(4,128)S(1)}, u32[]{:S(2)}, u32[]{:S(2)}) async-start(f32[16,4,4608]{2,1,0:T(4,128)} %pack_lines.1), calls=%async_computation | async-start | bytes 2359296 | tf_op jit(solution)/shard_map/all_to_all | solution.py:479
  10.3 0.0 copy-start.2
  10.3 8.5 %pack_fields.1 = (f32[6,64,4096]{2,1,0:T(8,128)}, f32[10,64,128]{2,1,0:T(8,128)}, f32[10,64,128]{2,1,0:T(8,128)}, f32[7,2,4096]{2,1,0:T(2,128)}, f32[7,2,4096]{2,1,0:T(2,128)}) custom-call(f32[64,4096]{1,0:T(8,128)} %kd_h.1, f32[3,64,4096]{2,1,0:T(8,128)} %v.1, f32[64,4096]{1,0:T(8,128)} %s.1, s32[64,4096]{1,0:T(8,128)} %c.1, f32[64,4096]{1,0:T(8,128)} %t_h.1), custom_call_target="tpu_custom_call" | custom-call | tf_op jit(solution)/shard_map/pack_fields/pallas_call | solution.py:488
  18.8 2.1 %collective-permute-start = (f32[10,64,128]{2,1,0:T(8,128)}, f32[10,64,128]{2,1,0:T(8,128)S(1)}, u32[]{:S(2)}, u32[]{:S(2)}) collective-permute-start(f32[10,64,128]{2,1,0:T(8,128)} %get-tuple-element.28), channel_id=1, source_target_pairs={{0,8},{8,16},{16,24},{24,32},{32,40},{40,48},{48,56},{56,64},{64,7... | collective-permute-start | bytes 983048 | tf_op jit(solution)/shard_map/ppermute | solution.py:499
  20.9 7.1 %collective-permute-start.1 = (f32[10,64,128]{2,1,0:T(8,128)}, f32[10,64,128]{2,1,0:T(8,128)S(1)}, u32[]{:S(2)}, u32[]{:S(2)}) collective-permute-start(f32[10,64,128]{2,1,0:T(8,128)} %get-tuple-element.29), channel_id=1, source_target_pairs={{8,0},{16,8},{24,16},{32,24},{40,32},{48,40},{56,48},{64,56},{72,6... | collective-permute-start | bytes 983048 | tf_op jit(solution)/shard_map/ppermute | solution.py:500
  28.0 3.5 %collective-permute-start.2 = (f32[7,2,4096]{2,1,0:T(2,128)}, f32[7,2,4096]{2,1,0:T(2,128)S(1)}, u32[]{:S(2)}, u32[]{:S(2)}) collective-permute-start(f32[7,2,4096]{2,1,0:T(2,128)} %get-tuple-element.30), channel_id=1, source_target_pairs={{0,1},{1,2},{2,3},{3,4},{4,5},{5,6},{6,7},{8,9},{9,10},{10,11},{11... | collective-permute-start | bytes 688136 | tf_op jit(solution)/shard_map/ppermute | solution.py:501
  31.6 1.3 %collective-permute-start.3 = (f32[7,2,4096]{2,1,0:T(2,128)}, f32[7,2,4096]{2,1,0:T(2,128)S(1)}, u32[]{:S(2)}, u32[]{:S(2)}) collective-permute-start(f32[7,2,4096]{2,1,0:T(2,128)} %get-tuple-element.31), channel_id=1, source_target_pairs={{1,0},{2,1},{3,2},{4,3},{5,4},{6,5},{7,6},{9,8},{10,9},{11,10},{12... | collective-permute-start | bytes 688136 | tf_op jit(solution)/shard_map/ppermute | solution.py:502
  32.9 0.0 copy-done.2
  32.9 4.3 %list_outlets.1 = (s32[1024]{0:T(1024)S(1)}, s32[1]{0:T(128)}) custom-call(s32[1024]{0:T(1024)S(1)} %add_select_fusion.codes), custom_call_target="tpu_custom_call" | custom-call | tf_op jit(solution)/shard_map/list_outlets/pallas_call | solution.py:508
  37.2 0.1 stack.23.place
  37.3 0.0 collective-permute-done.xl
  37.3 0.0 collective-permute-done.1.xr
  37.3 0.0 all-to-all-done.lines
  37.3 0.0 copy-start
  37.4 0.0 copy-start.1
  37.4 7.9 %first_half.1 = (f32[36,80,128]{2,1,0:T(8,128)S(1)}, f32[36,80,128]{2,1,0:T(8,128)S(1)}, f32[36,80,128]{2,1,0:T(8,128)S(1)}, f32[36,80,128]{2,1,0:T(8,128)S(1)},...) custom-call(s32[5]{0:T(128)S(1)} %stack.23.place, ...), custom_call_target="tpu_custom_call" | custom-call | tf_op jit(solution)/shard_map/first_half/pallas_call | solution.py:524
  45.3 2.7 %collective-permute-start.4 = (f32[4,5120]{1,0:T(4,128)S(1)}, f32[4,5120]{1,0:T(4,128)S(1)}, u32[]{:S(2)}, u32[]{:S(2)}) collective-permute-start(f32[4,5120]{1,0:T(4,128)S(1)} %get-tuple-element.33), channel_id=1, source_target_pairs={{0,1},{1,0},{2,3},{3,2},{4,5},{5,4},{6,7},{7,6},{8,9},{9,8},{10,11... | collective-permute-start | bytes 245768 | tf_op jit(solution)/shard_map/ppermute | solution.py:534
  48.0 3.7 %collective-permute-start.5 = (f32[4,5120]{1,0:T(4,128)S(1)}, f32[4,5120]{1,0:T(4,128)S(1)}, u32[]{:S(2)}, u32[]{:S(2)}) collective-permute-start(f32[4,5120]{1,0:T(4,128)S(1)} %get-tuple-element.34), channel_id=1, source_target_pairs={{0,7},{1,2},{2,1},{3,4},{4,3},{5,6},{6,5},{7,0},{8,15},{9,10},{10,... | collective-permute-start | bytes 245768 | tf_op jit(solution)/shard_map/ppermute | solution.py:535
  51.8 0.0 collective-permute-done.2.yl
  51.8 0.0 collective-permute-done.3.yh
  51.8 0.0 collective-permute-done.4.msg_a
  51.8 2.8 %collective-permute-done.5.msg_b = f32[4,5120]{1,0:T(4,128)S(1)} collective-permute-done((f32[4,5120]{1,0:T(4,128)S(1)}, f32[4,5120]{1,0:T(4,128)S(1)}, u32[]{:S(2)}, u32[]{:S(2)}) %collective-permute-start.5) | collective-permute-done | bytes 81952 | tf_op jit(solution)/shard_map/ppermute | solution.py:535
  54.6 0.0 copy-done
  54.6 0.0 copy-done.1
  54.6 10.6 %second_half.1 = (f32[64,4096]{1,0:T(8,128)}, f32[64,4096]{1,0:T(8,128)}, f32[36,80,128]{2,1,0:T(8,128)S(1)}, f32[36,80,128]{2,1,0:T(8,128)S(1)}, f32[36,80,128]...) custom-call(s32[5]{0:T(128)S(1)} %stack.23.place, ...), custom_call_target="tpu_custom_call", output_to_operand_aliasing={{2}: (12, {}), {3}: (13, {}), {4}: (14, {}), {5}: (15, {}),... | custom-call | tf_op jit(solution)/shard_map/second_half/pallas_call | solution.py:540
  (1 shorter events, 0.0 us)
Async XLA Ops:
  3.0 34.3 %all-to-all-start = ((f32[16,4,4608]{2,1,0:T(4,128)}), f32[16,4,4608]{2,1,0:T(4,128)S(1)}, u32[]{:S(2)}, u32[]{:S(2)}) async-start(f32[16,4,4608]{2,1,0:T(4,128)} %pack_lines.1), calls=%async_computation | async-start | bytes 2359296 | tf_op jit(solution)/shard_map/all_to_all | solution.py:479
  10.3 22.6 %copy-start.2 = (s32[1024]{0:T(1024)S(1)}, s32[1024]{0:T(1024)}, u32[]{:S(2)}) copy-start(s32[1024]{0:T(1024)} %param.13) | copy-start | bytes 12292
  18.8 18.5 %collective-permute-start = (f32[10,64,128]{2,1,0:T(8,128)}, f32[10,64,128]{2,1,0:T(8,128)S(1)}, u32[]{:S(2)}, u32[]{:S(2)}) collective-permute-start(f32[10,64,128]{2,1,0:T(8,128)} %get-tuple-element.28), channel_id=1, source_target_pairs={{0,8},{8,16},{16,24},{24,32},{32,40},{40,48},{48,56},{56,64},{64,7... | collective-permute-start | bytes 983048 | tf_op jit(solution)/shard_map/ppermute | solution.py:499
  20.9 16.4 %collective-permute-start.1 = (f32[10,64,128]{2,1,0:T(8,128)}, f32[10,64,128]{2,1,0:T(8,128)S(1)}, u32[]{:S(2)}, u32[]{:S(2)}) collective-permute-start(f32[10,64,128]{2,1,0:T(8,128)} %get-tuple-element.29), channel_id=1, source_target_pairs={{8,0},{16,8},{24,16},{32,24},{40,32},{48,40},{56,48},{64,56},{72,6... | collective-permute-start | bytes 983048 | tf_op jit(solution)/shard_map/ppermute | solution.py:500
  28.0 23.7 %collective-permute-start.2 = (f32[7,2,4096]{2,1,0:T(2,128)}, f32[7,2,4096]{2,1,0:T(2,128)S(1)}, u32[]{:S(2)}, u32[]{:S(2)}) collective-permute-start(f32[7,2,4096]{2,1,0:T(2,128)} %get-tuple-element.30), channel_id=1, source_target_pairs={{0,1},{1,2},{2,3},{3,4},{4,5},{5,6},{6,7},{8,9},{9,10},{10,11},{11... | collective-permute-start | bytes 688136 | tf_op jit(solution)/shard_map/ppermute | solution.py:501
  31.6 20.2 %collective-permute-start.3 = (f32[7,2,4096]{2,1,0:T(2,128)}, f32[7,2,4096]{2,1,0:T(2,128)S(1)}, u32[]{:S(2)}, u32[]{:S(2)}) collective-permute-start(f32[7,2,4096]{2,1,0:T(2,128)} %get-tuple-element.31), channel_id=1, source_target_pairs={{1,0},{2,1},{3,2},{4,3},{5,4},{6,5},{7,6},{9,8},{10,9},{11,10},{12... | collective-permute-start | bytes 688136 | tf_op jit(solution)/shard_map/ppermute | solution.py:502
  37.3 17.2 %copy-start = (f32[64,4096]{1,0:T(8,128)S(1)}, f32[64,4096]{1,0:T(8,128)}, u32[]{:S(2)}) copy-start(f32[64,4096]{1,0:T(8,128)} %kd_h.1) | copy-start | bytes 3145732
  37.4 17.2 %copy-start.1 = (f32[64,4096]{1,0:T(8,128)S(1)}, f32[64,4096]{1,0:T(8,128)}, u32[]{:S(2)}) copy-start(f32[64,4096]{1,0:T(8,128)} %t_h.1) | copy-start | bytes 3145732
  45.3 6.5 %collective-permute-start.4 = (f32[4,5120]{1,0:T(4,128)S(1)}, f32[4,5120]{1,0:T(4,128)S(1)}, u32[]{:S(2)}, u32[]{:S(2)}) collective-permute-start(f32[4,5120]{1,0:T(4,128)S(1)} %get-tuple-element.33), channel_id=1, source_target_pairs={{0,1},{1,0},{2,3},{3,2},{4,5},{5,4},{6,7},{7,6},{8,9},{9,8},{10,11... | collective-permute-start | bytes 245768 | tf_op jit(solution)/shard_map/ppermute | solution.py:534
  48.0 6.6 %collective-permute-start.5 = (f32[4,5120]{1,0:T(4,128)S(1)}, f32[4,5120]{1,0:T(4,128)S(1)}, u32[]{:S(2)}, u32[]{:S(2)}) collective-permute-start(f32[4,5120]{1,0:T(4,128)S(1)} %get-tuple-element.34), channel_id=1, source_target_pairs={{0,7},{1,2},{2,1},{3,4},{4,3},{5,6},{6,5},{7,0},{8,15},{9,10},{10,... | collective-permute-start | bytes 245768 | tf_op jit(solution)/shard_map/ppermute | solution.py:535

commit v3 on v2

--- a/solution.py
+++ b/solution.py
@@ -24,8 +24,19 @@
 MCOLS = WCOLS + 4 * LANES
 F32 = jnp.float32
 MIB = 1 << 20
-FIRST_MIB = 30
-UNROLL = 2
+FIRST_MIB = 27
+STACK = 6
+UNROLL = 4
+PACK_BLOCKS = 4
+
+
+def places():
+    gx, gy = lax.axis_index("gx"), lax.axis_index("gy")
+    return (
+        gx, lax.axis_size("gx") - 1 - gx, gy, lax.axis_size("gy") - 1 - gy,
+        lax.rem(gy, 2), lax.rem(gx, 2),
+    )
+
 
 VM = pl.BlockSpec(memory_space=pltpu.VMEM)
 SM = pl.BlockSpec(memory_space=pltpu.SMEM)
@@ -40,65 +51,100 @@
     return lax.broadcasted_iota(jnp.int32, (rows, LANES), 1)
 
 
-def pack_lines(src, out, sem):
+def pack_lines(src, out, held, arrived, sent):
     n = out.shape[0]
-    copies = []
+    loads, stores = [], []
     for i in range(n):
         low = i * COLS - 2 * LANES
         high = low + WCOLS
-        pieces = [(max(low, 0), min(high, n * COLS), max(-low, 0))]
+        a, b = max(low, 0), min(high, n * COLS)
+        at = a - low
+        pieces = [(a, b, at)]
         if low < 0:
             pieces.append((0, 2 * LANES, 0))
         if high > n * COLS:
             pieces.append((n * COLS - 2 * LANES, n * COLS, WCOLS - 2 * LANES))
-        for a, b, at in pieces:
-            copies.append(
-                pltpu.make_async_copy(
-                    src.at[0, :, a:b], out.at[i, :, at : at + b - a], sem
-                )
+        loads.append([
+            pltpu.make_async_copy(
+                src.at[0, :, a:b], held.at[i, :, at : at + b - a], arrived.at[i, k]
             )
-    for c in copies:
-        c.start()
-    for c in copies:
-        c.wait()
-
-
-def pack_fields(kd, v, s, c, t, stack, to_left, to_right, to_low, to_high):
+            for k, (a, b, at) in enumerate(pieces)
+        ])
+        stores.append(pltpu.make_async_copy(held.at[i], out.at[i], sent.at[i]))
+    for group in loads:
+        for c in group:
+            c.start()
+    for group, store in zip(loads, stores):
+        for c in group:
+            c.wait()
+        store.start()
+    for store in stores:
+        store.wait()
+
+
+def pack_fields(kd, vl, vr, vt, vb, s, c, tl, tr, tt, tb,
+                stack, side_a, side_b, line_a, line_b):
     step, last = pl.program_id(0), pl.num_programs(0) - 1
-    kind = c[...]
-    fields = (
-        kd[...], v[0], v[1], v[2],
-        jnp.where(kind == 1, s[...], 0.0),
-        jnp.where(kind == 2, DRAIN, 0.0).astype(F32),
-    )
-    for f, val in enumerate(fields):
-        stack[f] = val
-    for f, val in enumerate(fields + (t[...],)):
-        to_low[f] = val[0:2]
-        to_high[f] = val[ROWS - 2 : ROWS]
-    lo = lane_iota(ROWS) < NZ
-
-    def layers(out, near, far, low_side):
-        for f in range(6):
-            out[f] = stack[f, :, near]
-        out[6] = t[:, near]
+    place = places()
+    odd_x, odd_y = place[5] == 1, place[4] == 1
+    rows = kd.shape[0]
+
+    def fields(kd, v, s, kind, t):
+        return (
+            kd, *v,
+            jnp.where(kind == 1, s, 0.0),
+            jnp.where(kind == 2, DRAIN, 0.0).astype(F32),
+            t,
+        )
+
+    stack[0] = kd[...]
+    stack[1] = jnp.where(c[...] == 1, s[...], 0.0)
+    stack[2] = jnp.where(c[...] == 2, DRAIN, 0.0).astype(F32)
+
+    lo = lane_iota(rows) < NZ
+
+    def layers(v, t, near, far, at, low_side):
+        def tile(k):
+            cols = slice(at + k * LANES, at + (k + 1) * LANES)
+            edge = slice(k * LANES, (k + 1) * LANES)
+            return fields(
+                kd[:, cols], [v[d, :, edge] for d in range(3)], s[:, cols], c[:, cols], t[:, edge]
+            )
+        full, part = tile(near), tile(far)
+        merged = []
         for p in range(3):
-            first, second = stack[2 * p, :, far], stack[2 * p + 1, :, far]
+            first, second = part[2 * p], part[2 * p + 1]
             if low_side:
                 second = pltpu.roll(second, NZ, 1)
             else:
                 first = pltpu.roll(first, NZ, 1)
-            out[7 + p] = jnp.where(lo, first, second)
-
-    width = kd.shape[1]
-
-    @pl.when(step == 0)
-    def _():
-        layers(to_left, slice(0, LANES), slice(LANES, 2 * LANES), True)
-
-    @pl.when(step == last)
-    def _():
-        layers(to_right, slice(width - LANES, width), slice(width - 2 * LANES, width - LANES), False)
+            merged.append(jnp.where(lo, first, second))
+        return list(full) + merged
+
+    low_side = layers(vl, tl, 0, 1, 0, True)
+    high_side = layers(vr, tr, 1, 0, COLS - 2 * LANES, False)
+    for f, (low, high) in enumerate(zip(low_side, high_side)):
+        side_a[f] = jnp.where(odd_x, low, high)
+        side_b[f] = jnp.where(odd_x, high, low)
+
+    def lines(out, v, t, at, edge):
+        part = slice(at, at + 2)
+        e = slice(edge, edge + 2)
+        for f, val in enumerate(
+            fields(kd[part], [v[d, e] for d in range(3)], s[part], c[part], t[e])
+        ):
+            out[f] = val
+
+    for parity, low_out, high_out in ((True, line_a, line_b), (False, line_b, line_a)):
+        this = odd_y if parity else jnp.logical_not(odd_y)
+
+        @pl.when((step == 0) & this)
+        def _():
+            lines(low_out, vt, tt, 0, 0)
+
+        @pl.when((step == last) & this)
+        def _():
+            lines(high_out, vb, tb, rows - 2, 6)
 
 
 def list_outlets(codes, found, count):
@@ -171,11 +217,14 @@
     return STEP / (1.0 + BULK * kd * power)
 
 
-def first_half(place, found, count, lines, xl, xr, stack_h,
+def first_half(found, count, lines, x_a, x_b, v_h, stack_h,
                u0, fst, d1, rate, power, cn, cs, ce, cw, cu, cd, cc, src, msg_a, msg_b,
-               stack, sems):
+               v, stack, sems):
     loads = [
-        pltpu.make_async_copy(stack_h.at[k], stack.at[k], sems.at[k]) for k in range(6)
+        pltpu.make_async_copy(stack_h.at[0], stack.at[0], sems.at[0]),
+        *[pltpu.make_async_copy(v_h.at[k], v.at[k], sems.at[k + 3]) for k in range(3)],
+        pltpu.make_async_copy(stack_h.at[1], stack.at[1], sems.at[1]),
+        pltpu.make_async_copy(stack_h.at[2], stack.at[2], sems.at[2]),
     ]
     for load in loads:
         load.start()
@@ -189,17 +238,27 @@
             ]
     lo = lane_iota(ROWS) < NZ
 
-    def third(ref, f, high):
-        both = ref[7 + f // 2]
+    place = places()
+    odd_x = place[5] == 1
+
+    def both(f, rows=slice(None)):
+        one, two = x_a[f, rows], x_b[f, rows]
+        return jnp.where(odd_x, one, two), jnp.where(odd_x, two, one)
+
+    low_x, high_x = zip(*[both(f) for f in range(6)])
+    low_3, high_3 = zip(*[both(f) for f in range(7, 10)])
+
+    def third(parts, f, high):
+        part = parts[f // 2]
         if high:
-            return jnp.where(lo, 0.0, both if f % 2 else pltpu.roll(both, NZ, 1))
-        return jnp.where(lo, pltpu.roll(both, NZ, 1) if f % 2 else both, 0.0)
+            return jnp.where(lo, 0.0, part if f % 2 else pltpu.roll(part, NZ, 1))
+        return jnp.where(lo, pltpu.roll(part, NZ, 1) if f % 2 else part, 0.0)
 
     for tile, fields in (
-        (0, [third(xl, f, True) for f in range(6)]),
-        (1, [xl[f] for f in range(6)]),
-        (WT - 2, [xr[f] for f in range(6)]),
-        (WT - 1, [third(xr, f, False) for f in range(6)]),
+        (0, [third(low_3, f, True) for f in range(6)]),
+        (1, low_x),
+        (WT - 2, high_x),
+        (WT - 1, [third(high_3, f, False) for f in range(6)]),
     ):
         for ref, val in zip(coef, coefficients(*fields[1:4], fields[5])):
             ref[tile, own, :] = val
@@ -227,14 +286,14 @@
             power[t, rr, :] = p
             rate[t + 2, at, :] = rate_of(stack[0, rr, cols], p)
             values = coefficients(
-                stack[1, rr, cols], stack[2, rr, cols], stack[3, rr, cols], stack[5, rr, cols]
+                v[0, rr, cols], v[1, rr, cols], v[2, rr, cols], stack[2, rr, cols]
             )
             for ref, val in zip(coef, values):
                 ref[t + 2, at, :] = val
-            src[t + 2, at, :] = stack[4, rr, cols]
+            src[t + 2, at, :] = stack[1, rr, cols]
         return carry
 
-    lax.fori_loop(0, TILES, prepare, 0, unroll=2)
+    lax.fori_loop(0, TILES, prepare, 0, unroll=UNROLL)
 
     spans = range(BASE, BASE + ROWS, 8)
 
@@ -250,8 +309,8 @@
             easts.append(east)
         return tuple(easts)
 
-    zero = jnp.zeros((8, LANES), F32)
-    lax.fori_loop(0, WT, step, (zero,) * len(spans), unroll=UNROLL)
+    first_west = tuple(east_of(u0, 0, 0, a, 8) for a in spans)
+    lax.fori_loop(0, WT, step, first_west, unroll=UNROLL)
 
     top = BASE + ROWS
     odd = place[4] == 1
@@ -268,14 +327,14 @@
     for k in range(16):
         at = pl.ds(WCOLS + (k % 4) * LANES, LANES)
         row = slice(k // 4, k // 4 + 1)
-        side = xr if k % 2 else xl
         if k < 14:
-            send(at, row, side[k // 2, ROWS - 1 : ROWS, :], side[k // 2, 0:1, :])
+            up = both(k // 2, slice(ROWS - 1, ROWS))[k % 2]
+            send(at, row, up, both(k // 2, slice(0, 1))[k % 2])
         else:
             send(at, row, blank, blank)
 
 
-def second_half(place, found, count, xl, xr, yl, yh, msg_a, msg_b, kd_h, t_h, power,
+def second_half(found, count, x_a, x_b, y_a, y_b, msg_a, msg_b, kd_h, t_h, power,
                 u0_in, fst_in, d1_in, rate_in, cn_in, cs_in, ce_in, cw_in, cu_in, cd_in, cc_in, src_in,
                 kd_out_h, start_out_h,
                 u0, fst, d1, rate, cn, cs, ce, cw, cu, cd, cc, src,
@@ -290,20 +349,27 @@
     own = pl.ds(BASE, ROWS)
 
     top = BASE + ROWS
+    place = places()
     odd = place[4] == 1
 
     def arrived(row, at):
         one, two = msg_a[row, at], msg_b[row, at]
         return jnp.where(odd, one, two), jnp.where(odd, two, one)
+
+    for parity, y_low, y_high in ((True, y_a, y_b), (False, y_b, y_a)):
+
+        @pl.when(odd if parity else jnp.logical_not(odd))
+        def _():
+            for f in range(7):
+                for t in range(TILES):
+                    at = pl.ds(t * LANES, LANES)
+                    halo[f, t + 2, 6:8, :] = y_low[f, :, at]
+                    halo[f, t + 2, 8:10, :] = y_high[f, :, at]
 
     blank = jnp.zeros((16, LANES), F32)
     for f in range(7):
         for tile in (0, 1, WT - 2, WT - 1):
             halo[f, tile] = blank
-        for t in range(TILES):
-            at = pl.ds(t * LANES, LANES)
-            halo[f, t + 2, 6:8, :] = yl[f, :, at]
-            halo[f, t + 2, 8:10, :] = yh[f, :, at]
         for side, tile in ((0, 1), (1, WT - 2)):
             k = 2 * f + side
             low, high = arrived(slice(k // 4, k // 4 + 1), pl.ds(WCOLS + (k % 4) * LANES, LANES))
@@ -370,8 +436,8 @@
             easts.append(east)
         return tuple(easts)
 
-    zero = jnp.zeros((8, LANES), F32)
-    lax.fori_loop(0, WT, edge_step, (zero, zero), unroll=6)
+    first_west = tuple(east_of(u0, 0, 0, a, 8) for a, _ in edge_spans)
+    lax.fori_loop(0, WT, edge_step, first_west, unroll=6)
 
     loads[1].wait()
 
@@ -381,8 +447,9 @@
         return carry
 
     lax.fori_loop(0, TILES, targets, 0)
-    target[1, own, :] = xl[6]
-    target[WT - 2, own, :] = xr[6]
+    odd_x = place[5] == 1
+    target[1, own, :] = jnp.where(odd_x, x_a[6], x_b[6])
+    target[WT - 2, own, :] = jnp.where(odd_x, x_b[6], x_a[6])
 
     spans = range(BASE - 4, BASE + ROWS + 4, 8)
 
@@ -458,10 +525,13 @@
     return pltpu.CompilerParams(vmem_limit_bytes=mib * MIB)
 
 
-def shifts(axis):
+def swap(a, b, axis):
     n = lax.axis_size(axis)
-    up = [(i, i + 1) for i in range(n - 1)]
-    return up, [(b, a) for a, b in up]
+
+    def pairs(first):
+        return [(i, j) for k in range(first, n - 1, 2) for i, j in ((k, k + 1), (k + 1, k))]
+
+    return lax.ppermute(a, axis, pairs(0)), lax.ppermute(b, axis, pairs(1))
 
 
 def per_device(checkpoint, sorption_kd, velocity, source, target, cell_type, outlets):
@@ -471,8 +541,12 @@
         pack_lines,
         out_shape=jax.ShapeDtypeStruct((n_gx, checkpoint.shape[1], WCOLS), F32),
         in_specs=[HB],
-        out_specs=VM,
-        scratch_shapes=[pltpu.SemaphoreType.DMA],
+        out_specs=HB,
+        scratch_shapes=[
+            pltpu.VMEM((n_gx, checkpoint.shape[1], WCOLS), F32),
+            pltpu.SemaphoreType.DMA((n_gx, 2)),
+            pltpu.SemaphoreType.DMA((n_gx,)),
+        ],
         compiler_params=params(60),
         name="pack_lines",
     )(checkpoint)
@@ -480,31 +554,41 @@
 
     side = jax.ShapeDtypeStruct((10, ROWS, LANES), F32)
     line = jax.ShapeDtypeStruct((7, 2, COLS), F32)
-    blocks = 8
-    part = COLS // blocks
-    flat = pl.BlockSpec((ROWS, part), lambda i: (0, i))
-    deep = lambda *lead: pl.BlockSpec(lead + (part,), lambda i: (0, 0, i))
-    kept = pl.BlockSpec(side.shape, lambda i: (0, 0, 0))
-    stack, to_left, to_right, to_low, to_high = pl.pallas_call(
-        pack_fields,
-        grid=(blocks,),
-        out_shape=[jax.ShapeDtypeStruct((6, ROWS, COLS), F32), side, side, line, line],
-        in_specs=[flat, deep(3, ROWS), flat, flat, flat],
-        out_specs=[deep(6, ROWS), kept, kept, deep(7, 2), deep(7, 2)],
-        compiler_params=params(60),
-        name="pack_fields",
-    )(sorption_kd, velocity, source, cell_type, target)
-    x_up, x_down = shifts("gx")
-    y_up, y_down = shifts("gy")
-    xl = lax.ppermute(to_right, "gx", x_up)
-    xr = lax.ppermute(to_left, "gx", x_down)
-    yl = lax.ppermute(to_high, "gy", y_up)
-    yh = lax.ppermute(to_low, "gy", y_down)
-
     row = (outlets >> 16) - gy * ROWS + BASE
     col = ((outlets >> 6) & 1023) - gx * (COLS // NZ) + 4
     inside = (row >= BASE - 2) & (row < BASE + ROWS + 2) & (col >= 2) & (col < 70)
     codes = jnp.where(inside, (row << 16) + (col << 6) + (outlets & (NZ - 1)), -1)
+    rows = ROWS // PACK_BLOCKS
+    flat = pl.BlockSpec((rows, COLS), lambda i: (i, 0))
+    deep = lambda n, width: pl.BlockSpec((n, rows, width), lambda i: (0, i, 0))
+    kept = pl.BlockSpec(line.shape, lambda i: (0, 0, 0))
+    two = 2 * LANES
+    ends = TILES // 2 - 1, ROWS // 8 - 1
+    stack, side_a, side_b, line_a, line_b = pl.pallas_call(
+        pack_fields,
+        grid=(PACK_BLOCKS,),
+        out_shape=[
+            jax.ShapeDtypeStruct((STACK, ROWS, COLS), F32), side, side, line, line,
+        ],
+        in_specs=[
+            flat,
+            pl.BlockSpec((3, rows, two), lambda i: (0, i, 0)),
+            pl.BlockSpec((3, rows, two), lambda i: (0, i, ends[0])),
+            pl.BlockSpec((3, 8, COLS), lambda i: (0, 0, 0)),
+            pl.BlockSpec((3, 8, COLS), lambda i: (0, ends[1], 0)),
+            flat, flat,
+            pl.BlockSpec((rows, two), lambda i: (i, 0)),
+            pl.BlockSpec((rows, two), lambda i: (i, ends[0])),
+            pl.BlockSpec((8, COLS), lambda i: (0, 0)),
+            pl.BlockSpec((8, COLS), lambda i: (ends[1], 0)),
+        ],
+        out_specs=[deep(3, COLS), deep(10, LANES), deep(10, LANES), kept, kept],
+        compiler_params=params(60),
+        name="pack_fields",
+    )(sorption_kd, *[velocity] * 4, source, cell_type, *[target] * 4)
+    x_a, x_b = swap(side_a, side_b, "gx")
+    y_a, y_b = swap(line_a, line_b, "gy")
+
     found, count = pl.pallas_call(
         list_outlets,
         out_shape=[
@@ -517,22 +601,19 @@
         name="list_outlets",
     )(codes)
 
-    n_gy = lax.axis_size("gy")
-    edge = jnp.stack([gx, n_gx - 1 - gx, gy, n_gy - 1 - gy, gy % 2]).astype(jnp.int32)
     message = jax.ShapeDtypeStruct((4, MCOLS), F32)
     power = jax.ShapeDtypeStruct((TILES, ROWS, LANES), F32)
     u0, fst, d1, rate, power, *rest = pl.pallas_call(
         first_half,
         out_shape=[window()] * 4 + [power] + [window()] * 8 + [message] * 2,
-        in_specs=[SM] * 3 + [VM] * 3 + [HB],
+        in_specs=[SM] * 2 + [VM] * 3 + [HB] * 2,
         out_specs=[VM] * 15,
-        scratch_shapes=[pltpu.VMEM((6, ROWS, COLS), F32), pltpu.SemaphoreType.DMA((6,))],
+        scratch_shapes=[*[pltpu.VMEM((3, ROWS, COLS), F32)] * 2, pltpu.SemaphoreType.DMA((6,))],
         compiler_params=params(FIRST_MIB),
         name="first_half",
-    )(edge, found, count, arrived, xl, xr, stack)
+    )(found, count, arrived, x_a, x_b, velocity, stack)
     coefs, (msg_a, msg_b) = rest[:8], rest[8:]
-    got_a = lax.ppermute(msg_a, "gy", [(i, i + 1 - 2 * (i % 2)) for i in range(n_gy)])
-    got_b = lax.ppermute(msg_b, "gy", [(i, (i - 1 + 2 * (i % 2)) % n_gy) for i in range(n_gy)])
+    got_a, got_b = swap(msg_a, msg_b, "gy")
 
     kept = (u0, fst, d1, rate, *coefs)
     plane = jax.ShapeDtypeStruct((ROWS, COLS), F32)
@@ -540,9 +621,9 @@
     outs = pl.pallas_call(
         second_half,
         out_shape=[plane, plane] + [window()] * 12,
-        in_specs=[SM] * 3 + [VM] * 6 + [HB] * 2 + [VM] * 13,
+        in_specs=[SM] * 2 + [VM] * 6 + [HB] * 2 + [VM] * 13,
         out_specs=[HB] * 2 + [VM] * 12,
-        input_output_aliases={12 + k: 2 + k for k in range(12)},
+        input_output_aliases={11 + k: 2 + k for k in range(12)},
         scratch_shapes=[
             *[pltpu.VMEM((ROWS, COLS), F32)] * 4,
             pltpu.VMEM((7, WT, 16, LANES), F32),
@@ -551,7 +632,7 @@
         ],
         compiler_params=params(24),
         name="second_half",
-    )(edge, found, count, xl, xr, yl, yh, got_a, got_b, sorption_kd, target, power, *kept)
+    )(found, count, x_a, x_b, y_a, y_b, got_a, got_b, sorption_kd, target, power, *kept)
     return outs[0], outs[1]
 
 

time: 65.7 us -> 61.2 us (0.932)
  the two profiles are of different devices: /device:TPU:64 before, /device:TPU:23 now
where the time goes in v3:
time: 61.2 us; the launch traced here: 60.8 us
  Pallas kernels  29 us (47%)
  starting transfers between devices  21.1 us (34%)
  waiting for transfers between devices  9.9 us (16%)
  between operations  0.76 us (1%)
    ppermute x6, starting transfers between devices, swap(): return (lax.ppermute(a, axis, pairs(0)), lax.ppermute(b, axis, pairs(1)))  12.7 us
    ppermute x6, waiting for transfers between devices, swap(): return (lax.ppermute(a, axis, pairs(0)), lax.ppermute(b, axis, pairs(1)))  9.89 us
    pallas_call x1, Pallas kernels, per_device(): pl.pallas_call(second_half, out_shape=[plane, plane] + [window()] * 12, i...  9.77 us
    all_to_all x1, starting transfers between devices, per_device(): lax.all_to_all(lines, 'gx', split_axis=0, concat_axis=0, tiled=True)  8.43 us
    pallas_call x1, Pallas kernels, per_device(): pl.pallas_call(first_half, out_shape=[window()] * 4 + [power] + [window()...  7.04 us
    pallas_call x1, Pallas kernels, per_device(): pl.pallas_call(pack_fields, grid=(PACK_BLOCKS,), out_shape=[jax.ShapeDtyp...  5.39 us
    pallas_call x1, Pallas kernels, per_device(): pl.pallas_call(list_outlets, out_shape=[jax.ShapeDtypeStruct((outlets.sha...  4.3 us
    pallas_call x1, Pallas kernels, per_device(): pl.pallas_call(pack_lines, out_shape=jax.ShapeDtypeStruct((n_gx, checkpoi...  2.48 us
  transfers between devices with their start and end apart: 7, of which 2 were waited for; matrix products, arithmetic and copies ran while one was open for 0% of the time, Pallas kernels for 28%

profile of v3, /device:TPU:23, one launch (start us, length us, event | category | flops | bytes accessed | tf_op | source)
XLA Modules:
  0.0 60.8 jit_solution(14925390300314612543)
XLA Ops:
  0.6 2.5 %pack_lines.1 = f32[16,4,4608]{2,1,0:T(4,128)} custom-call(f32[1,4,65536]{2,1,0:T(4,128)} %src.1), custom_call_target="tpu_custom_call" | custom-call | tf_op jit(solution)/shard_map/pack_lines/pallas_call | solution.py:540
  3.1 8.4 %all-to-all-start = ((f32[16,4,4608]{2,1,0:T(4,128)}), f32[16,4,4608]{2,1,0:T(4,128)}, u32[]{:S(2)}, u32[]{:S(2)}) async-start(f32[16,4,4608]{2,1,0:T(4,128)} %pack_lines.1), calls=%async_computation | async-start | bytes 2359296 | tf_op jit(solution)/shard_map/all_to_all | solution.py:553
  11.6 0.0 copy-start.3
  11.6 0.0 copy-start
  11.6 5.4 %pack_fields.1 = (f32[6,64,4096]{2,1,0:T(8,128)}, f32[10,64,128]{2,1,0:T(8,128)}, f32[10,64,128]{2,1,0:T(8,128)}, f32[7,2,4096]{2,1,0:T(2,128)}, f32[7,2,4096]{2,1,0:T(2,128)}) custom-call(f32[64,4096]{1,0:T(8,128)} %kd_h.1, f32[3,64,4096]{2,1,0:T(8,128)} %v_h.1, f32[3,64,4096]{2,1,0:T(8,128)} %v_h.1, f32[3,64,4096]{2,1,0:T(8,128)} %v_h.1, ...), custom_call_target="tpu_custom_call" | custom-call | tf_op jit(solution)/shard_map/pack_fields/pallas_call | solution.py:567
  17.0 0.4 collective-permute-start
  17.4 4.6 %collective-permute-start.1 = (f32[10,64,128]{2,1,0:T(8,128)}, f32[10,64,128]{2,1,0:T(8,128)}, u32[]{:S(2)}, u32[]{:S(2)}) collective-permute-start(f32[10,64,128]{2,1,0:T(8,128)} %get-tuple-element.29), channel_id=1, source_target_pairs={{8,16},{16,8},{24,32},{32,24},{40,48},{48,40},{56,64},{64,56},{72,... | collective-permute-start | bytes 983048 | tf_op jit(solution)/shard_map/ppermute | solution.py:534
  22.0 0.8 %collective-permute-start.2 = (f32[7,2,4096]{2,1,0:T(2,128)}, f32[7,2,4096]{2,1,0:T(2,128)}, u32[]{:S(2)}, u32[]{:S(2)}) collective-permute-start(f32[7,2,4096]{2,1,0:T(2,128)} %get-tuple-element.30), channel_id=1, source_target_pairs={{0,1},{1,0},{2,3},{3,2},{4,5},{5,4},{6,7},{7,6},{8,9},{9,8},{10,11... | collective-permute-start | bytes 688136 | tf_op jit(solution)/shard_map/ppermute | solution.py:534
  22.9 2.5 %collective-permute-start.3 = (f32[7,2,4096]{2,1,0:T(2,128)}, f32[7,2,4096]{2,1,0:T(2,128)}, u32[]{:S(2)}, u32[]{:S(2)}) collective-permute-start(f32[7,2,4096]{2,1,0:T(2,128)} %get-tuple-element.31), channel_id=1, source_target_pairs={{1,2},{2,1},{3,4},{4,3},{5,6},{6,5},{9,10},{10,9},{11,12},{12,11},... | collective-permute-start | bytes 688136 | tf_op jit(solution)/shard_map/ppermute | solution.py:534
  25.4 0.0 copy-done.3
  25.4 4.3 %list_outlets.1 = (s32[1024]{0:T(1024)S(1)}, s32[1]{0:T(128)}) custom-call(s32[1024]{0:T(1024)S(1)} %add_select_fusion.codes), custom_call_target="tpu_custom_call" | custom-call | tf_op jit(solution)/shard_map/list_outlets/pallas_call | solution.py:592
  29.7 0.0 collective-permute-done.x_a
  29.7 5.8 %collective-permute-done.1.x_b = f32[10,64,128]{2,1,0:T(8,128)} collective-permute-done((f32[10,64,128]{2,1,0:T(8,128)}, f32[10,64,128]{2,1,0:T(8,128)}, u32[]{:S(2)}, u32[]{:S(2)}) %collective-permute-start.1) | collective-permute-done | bytes 327712 | tf_op jit(solution)/shard_map/ppermute | solution.py:534
  35.5 0.0 all-to-all-done.lines
  35.5 0.0 copy-done
  35.5 0.0 copy-start.1
  35.5 0.0 copy-start.2
  35.5 7.0 %first_half.1 = (f32[36,80,128]{2,1,0:T(8,128)S(1)}, f32[36,80,128]{2,1,0:T(8,128)S(1)}, f32[36,80,128]{2,1,0:T(8,128)S(1)}, f32[36,80,128]{2,1,0:T(8,128)S(1)},...) custom-call(s32[1024]{0:T(1024)S(1)} %get-tuple-element.26.found, ...), custom_call_target="tpu_custom_call" | custom-call | tf_op jit(solution)/shard_map/first_half/pallas_call | solution.py:606
  42.6 2.4 %collective-permute-start.4 = (f32[4,5120]{1,0:T(4,128)S(1)}, f32[4,5120]{1,0:T(4,128)S(1)}, u32[]{:S(2)}, u32[]{:S(2)}) collective-permute-start(f32[4,5120]{1,0:T(4,128)S(1)} %get-tuple-element.33), channel_id=1, source_target_pairs={{0,1},{1,0},{2,3},{3,2},{4,5},{5,4},{6,7},{7,6},{8,9},{9,8},{10,11... | collective-permute-start | bytes 245768 | tf_op jit(solution)/shard_map/ppermute | solution.py:534
  44.9 1.9 %collective-permute-start.5 = (f32[4,5120]{1,0:T(4,128)S(1)}, f32[4,5120]{1,0:T(4,128)S(1)}, u32[]{:S(2)}, u32[]{:S(2)}) collective-permute-start(f32[4,5120]{1,0:T(4,128)S(1)} %get-tuple-element.34), channel_id=1, source_target_pairs={{1,2},{2,1},{3,4},{4,3},{5,6},{6,5},{9,10},{10,9},{11,12},{12,11},... | collective-permute-start | bytes 245768 | tf_op jit(solution)/shard_map/ppermute | solution.py:534
  46.8 0.0 collective-permute-done.2.y_a
  46.8 0.0 collective-permute-done.3.y_b
  46.9 0.0 collective-permute-done.4.msg_a
  46.9 4.1 %collective-permute-done.5.msg_b = f32[4,5120]{1,0:T(4,128)S(1)} collective-permute-done((f32[4,5120]{1,0:T(4,128)S(1)}, f32[4,5120]{1,0:T(4,128)S(1)}, u32[]{:S(2)}, u32[]{:S(2)}) %collective-permute-start.5) | collective-permute-done | bytes 81952 | tf_op jit(solution)/shard_map/ppermute | solution.py:534
  51.0 0.0 copy-done.1
  51.0 0.0 copy-done.2
  51.0 9.8 %second_half.1 = (f32[64,4096]{1,0:T(8,128)}, f32[64,4096]{1,0:T(8,128)}, f32[36,80,128]{2,1,0:T(8,128)S(1)}, f32[36,80,128]{2,1,0:T(8,128)S(1)}, f32[36,80,128]...) custom-call(s32[1024]{0:T(1024)S(1)} %get-tuple-element.26.found, ...), custom_call_target="tpu_custom_call", output_to_operand_aliasing={{2}: (11, {}), {3}: (12, {}), {4}: (13, {}), {5}: (14, {}),... | custom-call | tf_op jit(solution)/shard_map/second_half/pallas_call | solution.py:621
  (1 shorter events, 0.0 us)
Async XLA Ops:
  3.1 32.4 %all-to-all-start = ((f32[16,4,4608]{2,1,0:T(4,128)}), f32[16,4,4608]{2,1,0:T(4,128)}, u32[]{:S(2)}, u32[]{:S(2)}) async-start(f32[16,4,4608]{2,1,0:T(4,128)} %pack_lines.1), calls=%async_computation | async-start | bytes 2359296 | tf_op jit(solution)/shard_map/all_to_all | solution.py:553
  11.6 13.8 %copy-start.3 = (s32[1024]{0:T(1024)S(1)}, s32[1024]{0:T(1024)}, u32[]{:S(2)}) copy-start(s32[1024]{0:T(1024)} %param.13) | copy-start | bytes 12292
  11.6 23.9 %copy-start = (f32[3,64,4096]{2,1,0:T(8,128)S(1)}, f32[3,64,4096]{2,1,0:T(8,128)}, u32[]{:S(2)}) copy-start(f32[3,64,4096]{2,1,0:T(8,128)} %v_h.1) | copy-start | bytes 9437188
  17.0 12.8 %collective-permute-start = (f32[10,64,128]{2,1,0:T(8,128)}, f32[10,64,128]{2,1,0:T(8,128)S(1)}, u32[]{:S(2)}, u32[]{:S(2)}) collective-permute-start(f32[10,64,128]{2,1,0:T(8,128)} %get-tuple-element.28), channel_id=1, source_target_pairs={{0,8},{8,0},{16,24},{24,16},{32,40},{40,32},{48,56},{56,48},{64,72... | collective-permute-start | bytes 983048 | tf_op jit(solution)/shard_map/ppermute | solution.py:534
  17.4 18.1 %collective-permute-start.1 = (f32[10,64,128]{2,1,0:T(8,128)}, f32[10,64,128]{2,1,0:T(8,128)}, u32[]{:S(2)}, u32[]{:S(2)}) collective-permute-start(f32[10,64,128]{2,1,0:T(8,128)} %get-tuple-element.29), channel_id=1, source_target_pairs={{8,16},{16,8},{24,32},{32,24},{40,48},{48,40},{56,64},{64,56},{72,... | collective-permute-start | bytes 983048 | tf_op jit(solution)/shard_map/ppermute | solution.py:534
  22.0 24.8 %collective-permute-start.2 = (f32[7,2,4096]{2,1,0:T(2,128)}, f32[7,2,4096]{2,1,0:T(2,128)}, u32[]{:S(2)}, u32[]{:S(2)}) collective-permute-start(f32[7,2,4096]{2,1,0:T(2,128)} %get-tuple-element.30), channel_id=1, source_target_pairs={{0,1},{1,0},{2,3},{3,2},{4,5},{5,4},{6,7},{7,6},{8,9},{9,8},{10,11... | collective-permute-start | bytes 688136 | tf_op jit(solution)/shard_map/ppermute | solution.py:534
  22.9 24.0 %collective-permute-start.3 = (f32[7,2,4096]{2,1,0:T(2,128)}, f32[7,2,4096]{2,1,0:T(2,128)}, u32[]{:S(2)}, u32[]{:S(2)}) collective-permute-start(f32[7,2,4096]{2,1,0:T(2,128)} %get-tuple-element.31), channel_id=1, source_target_pairs={{1,2},{2,1},{3,4},{4,3},{5,6},{6,5},{9,10},{10,9},{11,12},{12,11},... | collective-permute-start | bytes 688136 | tf_op jit(solution)/shard_map/ppermute | solution.py:534
  35.5 15.5 %copy-start.1 = (f32[64,4096]{1,0:T(8,128)S(1)}, f32[64,4096]{1,0:T(8,128)}, u32[]{:S(2)}) copy-start(f32[64,4096]{1,0:T(8,128)} %t_h.1) | copy-start | bytes 3145732
  35.5 15.5 %copy-start.2 = (f32[64,4096]{1,0:T(8,128)S(1)}, f32[64,4096]{1,0:T(8,128)}, u32[]{:S(2)}) copy-start(f32[64,4096]{1,0:T(8,128)} %kd_h.1) | copy-start | bytes 3145732
  42.6 4.3 %collective-permute-start.4 = (f32[4,5120]{1,0:T(4,128)S(1)}, f32[4,5120]{1,0:T(4,128)S(1)}, u32[]{:S(2)}, u32[]{:S(2)}) collective-permute-start(f32[4,5120]{1,0:T(4,128)S(1)} %get-tuple-element.33), channel_id=1, source_target_pairs={{0,1},{1,0},{2,3},{3,2},{4,5},{5,4},{6,7},{7,6},{8,9},{9,8},{10,11... | collective-permute-start | bytes 245768 | tf_op jit(solution)/shard_map/ppermute | solution.py:534
  44.9 6.1 %collective-permute-start.5 = (f32[4,5120]{1,0:T(4,128)S(1)}, f32[4,5120]{1,0:T(4,128)S(1)}, u32[]{:S(2)}, u32[]{:S(2)}) collective-permute-start(f32[4,5120]{1,0:T(4,128)S(1)} %get-tuple-element.34), channel_id=1, source_target_pairs={{1,2},{2,1},{3,4},{4,3},{5,6},{6,5},{9,10},{10,9},{11,12},{12,11},... | collective-permute-start | bytes 245768 | tf_op jit(solution)/shard_map/ppermute | solution.py:534

commit v4 on v3

--- a/solution.py
+++ b/solution.py
@@ -19,6 +19,8 @@
 WT = TILES + 4
 WR = 80
 BASE = 8
+INNER = range(BASE + 4, BASE + ROWS - 8, 8)
+BACK = range(INNER[0] + 8, INNER[-1], 8)
 COLS = TILES * LANES
 WCOLS = WT * LANES
 MCOLS = WCOLS + 4 * LANES
@@ -28,6 +30,7 @@
 STACK = 6
 UNROLL = 4
 PACK_BLOCKS = 4
+PARTS = 4
 
 
 def places():
@@ -82,35 +85,24 @@
         store.wait()
 
 
-def pack_fields(kd, vl, vr, vt, vb, s, c, tl, tr, tt, tb,
-                stack, side_a, side_b, line_a, line_b):
-    step, last = pl.program_id(0), pl.num_programs(0) - 1
-    place = places()
-    odd_x, odd_y = place[5] == 1, place[4] == 1
-    rows = kd.shape[0]
-
-    def fields(kd, v, s, kind, t):
-        return (
-            kd, *v,
-            jnp.where(kind == 1, s, 0.0),
-            jnp.where(kind == 2, DRAIN, 0.0).astype(F32),
-            t,
-        )
-
-    stack[0] = kd[...]
-    stack[1] = jnp.where(c[...] == 1, s[...], 0.0)
-    stack[2] = jnp.where(c[...] == 2, DRAIN, 0.0).astype(F32)
-
-    lo = lane_iota(rows) < NZ
-
-    def layers(v, t, near, far, at, low_side):
+def all_fields(kd, v, s, c, t, at):
+    kind = c[at]
+    return (
+        kd[at], *[v[(d, *at)] for d in range(3)],
+        jnp.where(kind == 1, s[at], 0.0),
+        jnp.where(kind == 2, DRAIN, 0.0).astype(F32),
+        t[at],
+    )
+
+
+def pack_sides(kdl, kdr, vl, vr, sl, sr, cl, cr, tl, tr, side_a, side_b):
+    odd = places()[5] == 1
+    lo = lane_iota(ROWS) < NZ
+
+    def layers(refs, near, far, low_side):
         def tile(k):
-            cols = slice(at + k * LANES, at + (k + 1) * LANES)
-            edge = slice(k * LANES, (k + 1) * LANES)
-            return fields(
-                kd[:, cols], [v[d, :, edge] for d in range(3)], s[:, cols], c[:, cols], t[:, edge]
-            )
-        full, part = tile(near), tile(far)
+            return all_fields(*refs, (slice(None), slice(k * LANES, (k + 1) * LANES)))
+        part = tile(far)
         merged = []
         for p in range(3):
             first, second = part[2 * p], part[2 * p + 1]
@@ -119,32 +111,28 @@
             else:
                 first = pltpu.roll(first, NZ, 1)
             merged.append(jnp.where(lo, first, second))
-        return list(full) + merged
-
-    low_side = layers(vl, tl, 0, 1, 0, True)
-    high_side = layers(vr, tr, 1, 0, COLS - 2 * LANES, False)
+        return list(tile(near)) + merged
+
+    low_side = layers((kdl, vl, sl, cl, tl), 0, 1, True)
+    high_side = layers((kdr, vr, sr, cr, tr), 1, 0, False)
     for f, (low, high) in enumerate(zip(low_side, high_side)):
-        side_a[f] = jnp.where(odd_x, low, high)
-        side_b[f] = jnp.where(odd_x, high, low)
-
-    def lines(out, v, t, at, edge):
-        part = slice(at, at + 2)
-        e = slice(edge, edge + 2)
-        for f, val in enumerate(
-            fields(kd[part], [v[d, e] for d in range(3)], s[part], c[part], t[e])
-        ):
-            out[f] = val
-
-    for parity, low_out, high_out in ((True, line_a, line_b), (False, line_b, line_a)):
-        this = odd_y if parity else jnp.logical_not(odd_y)
-
-        @pl.when((step == 0) & this)
-        def _():
-            lines(low_out, vt, tt, 0, 0)
-
-        @pl.when((step == last) & this)
-        def _():
-            lines(high_out, vb, tb, rows - 2, 6)
+        side_a[f] = jnp.where(odd, low, high)
+        side_b[f] = jnp.where(odd, high, low)
+
+
+def stack_fields(side, kd, s, c, kdt, kdb, vt, vb, st, sb, ct, cb, tt, tb, stack, line_a, line_b):
+    stack[0] = kd[...]
+    stack[1] = jnp.where(c[...] == 1, s[...], 0.0)
+    stack[2] = jnp.where(c[...] == 2, DRAIN, 0.0).astype(F32)
+
+    @pl.when(pl.program_id(0) == 0)
+    def _():
+        odd = places()[4] == 1
+        low_line = all_fields(kdt, vt, st, ct, tt, (slice(0, 2), slice(None)))
+        high_line = all_fields(kdb, vb, sb, cb, tb, (slice(6, 8), slice(None)))
+        for f, (low, high) in enumerate(zip(low_line, high_line)):
+            line_a[f] = jnp.where(odd, low, high)
+            line_b[f] = jnp.where(odd, high, low)
 
 
 def list_outlets(codes, found, count):
@@ -220,14 +208,16 @@
 def first_half(found, count, lines, x_a, x_b, v_h, stack_h,
                u0, fst, d1, rate, power, cn, cs, ce, cw, cu, cd, cc, src, msg_a, msg_b,
                v, stack, sems):
-    loads = [
-        pltpu.make_async_copy(stack_h.at[0], stack.at[0], sems.at[0]),
-        *[pltpu.make_async_copy(v_h.at[k], v.at[k], sems.at[k + 3]) for k in range(3)],
-        pltpu.make_async_copy(stack_h.at[1], stack.at[1], sems.at[1]),
-        pltpu.make_async_copy(stack_h.at[2], stack.at[2], sems.at[2]),
-    ]
-    for load in loads:
-        load.start()
+    loads = []
+    for k in range(PARTS):
+        cols = pl.ds(k * COLS // PARTS, COLS // PARTS)
+        loads.append([
+            pltpu.make_async_copy(stack_h.at[0:3, :, cols], stack.at[:, :, cols], sems.at[2 * k]),
+            pltpu.make_async_copy(v_h.at[:, :, cols], v.at[:, :, cols], sems.at[2 * k + 1]),
+        ])
+    for pair in loads:
+        for load in pair:
+            load.start()
     coef = (cn, cs, ce, cw, cu, cd, cc)
     own = pl.ds(BASE, ROWS)
     lines_of = lines.shape[1]
@@ -274,9 +264,6 @@
     def _():
         for ref in (u0, rate):
             ref[WT - 2 : WT, own, :] = jnp.zeros((2, ROWS, LANES), F32)
-
-    for load in loads:
-        load.wait()
 
     def prepare(t, carry):
         cols = pl.ds(pl.multiple_of(t * LANES, LANES), LANES)
@@ -293,7 +280,10 @@
             src[t + 2, at, :] = stack[1, rr, cols]
         return carry
 
-    lax.fori_loop(0, TILES, prepare, 0, unroll=UNROLL)
+    for k, pair in enumerate(loads):
+        for load in pair:
+            load.wait()
+        lax.fori_loop(k * TILES // PARTS, (k + 1) * TILES // PARTS, prepare, 0, unroll=UNROLL)
 
     spans = range(BASE, BASE + ROWS, 8)
 
@@ -334,27 +324,68 @@
             send(at, row, blank, blank)
 
 
-def second_half(found, count, x_a, x_b, y_a, y_b, msg_a, msg_b, kd_h, t_h, power,
-                u0_in, fst_in, d1_in, rate_in, cn_in, cs_in, ce_in, cw_in, cu_in, cd_in, cc_in, src_in,
-                kd_out_h, start_out_h,
-                u0, fst, d1, rate, cn, cs, ce, cw, cu, cd, cc, src,
-                kd, tgt, kd_out, start_out, halo, target, d2, mis, w, grad, w1, sems):
-    loads = [
-        pltpu.make_async_copy(a, b, sems.at[k, 0]) for k, (a, b) in enumerate(((kd_h, kd), (t_h, tgt)))
-    ]
-    for load in loads:
-        load.start()
+def second_step(fst, coef, src, rate, target, d2, mis, w, spans):
+    def step(t, wests):
+        easts = []
+        for a, west in zip(spans, wests):
+            at = pl.ds(a, 8)
+            mid, f, east = flux(fst, coef, src, t, t + 1, a, 8, west)
+            rt = rate[t, at, :]
+            d = rt * f
+            d2[t, at, :] = d
+            m = (mid + d) - target[t, at, :]
+            mis[t, at, :] = m
+            w[t, at, :] = m * rt
+            easts.append(east)
+        return tuple(easts)
+
+    return step, tuple(east_of(fst, 0, 1, a, 8) for a in spans)
+
+
+def weigh_outlets(found, count, mis, w, inner):
+    lane = lax.broadcasted_iota(jnp.int32, (1, LANES), 1)
+
+    def weigh(i, carry):
+        code = found[i]
+        row, col = code >> 16, (code >> 6) & 127
+        within = (row >= INNER[0]) & (row < INNER[-1] + 8)
+        at = pl.ds(row, 1)
+        tile = col >> 1
+
+        @pl.when(within if inner else jnp.logical_not(within))
+        def _():
+            hit = lane == (col & 1) * NZ + (code & (NZ - 1))
+            factor = jnp.where(hit, 1.0 + OUTLET_W, 1.0)
+            mis[tile, at, :] = mis[tile, at, :] * factor
+            w[tile, at, :] = w[tile, at, :] * factor
+
+        return carry
+
+    lax.fori_loop(0, count[0], weigh, 0)
+
+
+def adjoint_step(coef, rate, mis, w, grad, w1, spans):
+    def back(t, carry):
+        for a in spans:
+            at = pl.ds(a, 8)
+            g = mis[t, at, :] + flux_back(w, coef, t, t - 1, t + 1, a, 8)
+            grad[t, at, :] = g
+            w1[t, at, :] = g * rate[t, at, :]
+        return carry
+
+    return back
+
+
+def middle(found, count, x_a, x_b, y_a, y_b, t_h, fst, rate,
+           cn_in, cs_in, ce_in, cw_in, cu_in, cd_in, cc_in, src_in,
+           cn, cs, ce, cw, cu, cd, cc, src, target, kd_edge, d2, mis, w, grad, w1,
+           tgt, halo, sem):
+    load = pltpu.make_async_copy(t_h, tgt, sem)
+    load.start()
     coef = (cn, cs, ce, cw, cu, cd, cc)
-    low8, high8 = slice(0, BASE), slice(BASE + ROWS, WR)
-    own = pl.ds(BASE, ROWS)
-
-    top = BASE + ROWS
     place = places()
     odd = place[4] == 1
-
-    def arrived(row, at):
-        one, two = msg_a[row, at], msg_b[row, at]
-        return jnp.where(odd, one, two), jnp.where(odd, two, one)
+    own = pl.ds(BASE, ROWS)
 
     for parity, y_low, y_high in ((True, y_a, y_b), (False, y_b, y_a)):
 
@@ -363,18 +394,58 @@
             for f in range(7):
                 for t in range(TILES):
                     at = pl.ds(t * LANES, LANES)
-                    halo[f, t + 2, 6:8, :] = y_low[f, :, at]
-                    halo[f, t + 2, 8:10, :] = y_high[f, :, at]
-
-    blank = jnp.zeros((16, LANES), F32)
-    for f in range(7):
-        for tile in (0, 1, WT - 2, WT - 1):
-            halo[f, tile] = blank
-        for side, tile in ((0, 1), (1, WT - 2)):
-            k = 2 * f + side
-            low, high = arrived(slice(k // 4, k // 4 + 1), pl.ds(WCOLS + (k % 4) * LANES, LANES))
-            halo[f, tile, 7:8, :] = low
-            halo[f, tile, 8:9, :] = high
+                    halo[f, t, 6:8, :] = y_low[f, :, at]
+                    halo[f, t, 8:10, :] = y_high[f, :, at]
+
+    def edges(t, carry):
+        for a, to in ((0, slice(0, BASE)), (8, slice(BASE + ROWS, WR))):
+            at = pl.ds(a, 8)
+            values = coefficients(*[halo[f, t, at, :] for f in (1, 2, 3, 5)])
+            for ref, val in zip(coef, values):
+                ref[t + 2, to, :] = val
+            src[t + 2, to, :] = halo[4, t, at, :]
+            target[t + 2, to, :] = halo[6, t, at, :]
+            kd_edge[t + 2, at, :] = halo[0, t, at, :]
+        return carry
+
+    lax.fori_loop(0, TILES, edges, 0, unroll=4)
+    load.wait()
+
+    def targets(t, carry):
+        at = pl.ds(pl.multiple_of(t * LANES, LANES), LANES)
+        target[t + 2, own, :] = tgt[:, at]
+        return carry
+
+    lax.fori_loop(0, TILES, targets, 0, unroll=2)
+    odd_x = place[5] == 1
+    target[1, own, :] = jnp.where(odd_x, x_a[6], x_b[6])
+    target[WT - 2, own, :] = jnp.where(odd_x, x_b[6], x_a[6])
+
+    step, start = second_step(fst, coef, src, rate, target, d2, mis, w, INNER)
+    lax.fori_loop(1, WT - 1, step, start, unroll=UNROLL)
+    weigh_outlets(found, count, mis, w, True)
+    back = adjoint_step(coef, rate, mis, w, grad, w1, BACK)
+    lax.fori_loop(1, WT - 1, back, 0, unroll=UNROLL)
+
+
+def second_half(found, count, msg_a, msg_b, kd_h, power, kd_edge_in,
+                u0_in, fst_in, d1_in, rate_in, cn_in, cs_in, ce_in, cw_in, cu_in, cd_in, cc_in, src_in,
+                 target_in, d2_in, mis_in, w_in, grad_in, w1_in,
+                kd_out_h, start_out_h,
+                u0, fst, d1, rate, cn, cs, ce, cw, cu, cd, cc, src, target, d2, mis, w, grad, w1,
+                kd, kd_out, start_out, halo, sems):
+    load = pltpu.make_async_copy(kd_h, kd, sems.at[0, 0])
+    load.start()
+    coef = (cn, cs, ce, cw, cu, cd, cc)
+    low8, high8 = slice(0, BASE), slice(BASE + ROWS, WR)
+    top = BASE + ROWS
+    place = places()
+    odd = place[4] == 1
+
+    def arrived(row, at):
+        one, two = msg_a[row, at], msg_b[row, at]
+        return jnp.where(odd, one, two), jnp.where(odd, two, one)
+
     for t in range(WT):
         at = pl.ds(t * LANES, LANES)
         low, high = arrived(slice(0, 4), at)
@@ -383,30 +454,45 @@
         u0[t, top : top + 2, :] = high[0:2]
         fst[t, top + 1 : top + 3, :] = high[2:4]
 
+    for f in range(7):
+        for n in range(4):
+            halo[f, n] = jnp.zeros((16, LANES), F32)
+        for side, n in ((0, 1), (1, 2)):
+            k = 2 * f + side
+            low, high = arrived(slice(k // 4, k // 4 + 1), pl.ds(WCOLS + (k % 4) * LANES, LANES))
+            halo[f, n, 7:8, :] = low
+            halo[f, n, 8:9, :] = high
+    for n, t in enumerate((0, 1, WT - 2, WT - 1)):
+        for a, to in ((0, low8), (8, high8)):
+            at = pl.ds(a, 8)
+            values = coefficients(*[halo[f, n, at, :] for f in (1, 2, 3, 5)])
+            for ref, val in zip(coef, values):
+                ref[t, to, :] = val
+            src[t, to, :] = halo[4, n, at, :]
+            target[t, to, :] = halo[6, n, at, :]
+            rate[t, to, :] = rate_of(halo[0, n, at, :], sorb(u0[t, to, :]))
+
     def edges(t, carry):
         for a, to in ((0, low8), (8, high8)):
-            at = pl.ds(a, 8)
-            values = coefficients(halo[1, t, at, :], halo[2, t, at, :], halo[3, t, at, :], halo[5, t, at, :])
-            for ref, val in zip(coef, values):
-                ref[t, to, :] = val
-            src[t, to, :] = halo[4, t, at, :]
-            rate[t, to, :] = rate_of(halo[0, t, at, :], sorb(u0[t, to, :]))
-            target[t, to, :] = halo[6, t, at, :]
+            rate[t, to, :] = rate_of(kd_edge_in[t, pl.ds(a, 8), :], sorb(u0[t, to, :]))
         return carry
 
-    lax.fori_loop(0, WT, edges, 0, unroll=6)
+    lax.fori_loop(2, WT - 2, edges, 0, unroll=8)
 
     zero8 = jnp.zeros((WT, BASE, LANES), F32)
+    edge_rows = (low8, high8)
 
     @pl.when(place[0] == 0)
     def _():
-        rate[0:2] = jnp.zeros((2, WR, LANES), F32)
-        u0[0:2] = jnp.zeros((2, WR, LANES), F32)
+        for to in edge_rows:
+            rate[0:2, to, :] = zero8[:2]
+            u0[0:2, to, :] = zero8[:2]
 
     @pl.when(place[1] == 0)
     def _():
-        rate[WT - 2 : WT] = jnp.zeros((2, WR, LANES), F32)
-        u0[WT - 2 : WT] = jnp.zeros((2, WR, LANES), F32)
+        for to in edge_rows:
+            rate[WT - 2 : WT, to, :] = zero8[:2]
+            u0[WT - 2 : WT, to, :] = zero8[:2]
 
     @pl.when(place[2] == 0)
     def _():
@@ -437,63 +523,17 @@
         return tuple(easts)
 
     first_west = tuple(east_of(u0, 0, 0, a, 8) for a, _ in edge_spans)
-    lax.fori_loop(0, WT, edge_step, first_west, unroll=6)
-
-    loads[1].wait()
-
-    def targets(t, carry):
-        at = pl.ds(pl.multiple_of(t * LANES, LANES), LANES)
-        target[t + 2, own, :] = tgt[:, at]
-        return carry
-
-    lax.fori_loop(0, TILES, targets, 0)
-    odd_x = place[5] == 1
-    target[1, own, :] = jnp.where(odd_x, x_a[6], x_b[6])
-    target[WT - 2, own, :] = jnp.where(odd_x, x_b[6], x_a[6])
+    lax.fori_loop(0, WT, edge_step, first_west, unroll=12)
 
     spans = range(BASE - 4, BASE + ROWS + 4, 8)
-
-    def step(t, wests):
-        easts = []
-        for a, west in zip(spans, wests):
-            at = pl.ds(a, 8)
-            mid, f, east = flux(fst, coef, src, t, t + 1, a, 8, west)
-            rt = rate[t, at, :]
-            d = rt * f
-            d2[t, at, :] = d
-            m = (mid + d) - target[t, at, :]
-            mis[t, at, :] = m
-            w[t, at, :] = m * rt
-            easts.append(east)
-        return tuple(easts)
-
-    lax.fori_loop(1, WT - 1, step, tuple(east_of(fst, 0, 1, a, 8) for a in spans), unroll=UNROLL)
-
-    lane = lax.broadcasted_iota(jnp.int32, (1, LANES), 1)
-
-    def weigh(i, carry):
-        code = found[i]
-        row, col = code >> 16, (code >> 6) & 127
-        hit = lane == (col & 1) * NZ + (code & (NZ - 1))
-        tile = col >> 1
-        at = pl.ds(row, 1)
-        factor = jnp.where(hit, 1.0 + OUTLET_W, 1.0)
-        mis[tile, at, :] = mis[tile, at, :] * factor
-        w[tile, at, :] = w[tile, at, :] * factor
-        return carry
-
-    lax.fori_loop(0, count[0], weigh, 0)
-
-    def back(t, carry):
-        for a in spans:
-            at = pl.ds(a, 8)
-            g = mis[t, at, :] + flux_back(w, coef, t, t - 1, t + 1, a, 8)
-            grad[t, at, :] = g
-            w1[t, at, :] = g * rate[t, at, :]
-        return carry
-
+    outer = [a for a in spans if a not in INNER]
+    step, start = second_step(fst, coef, src, rate, target, d2, mis, w, outer)
+    lax.fori_loop(1, WT - 1, step, start, unroll=9)
+
+    weigh_outlets(found, count, mis, w, False)
+    back = adjoint_step(coef, rate, mis, w, grad, w1, [a for a in spans if a not in BACK])
     lax.fori_loop(1, WT - 1, back, 0, unroll=UNROLL)
-    loads[0].wait()
+    load.wait()
 
     def last(t, carry):
         cols = pl.ds(pl.multiple_of(t * LANES, LANES), LANES)
@@ -509,7 +549,7 @@
             start_out[rr, cols] = start + kdg * kd[rr, cols] * (FREUND - 1.0) / u0[tw, at, :]
         return carry
 
-    parts = 4
+    parts = PARTS
     stores = []
     for k in range(parts):
         lax.fori_loop(k * TILES // parts, (k + 1) * TILES // parts, last, 0, unroll=UNROLL)
@@ -560,32 +600,40 @@
     codes = jnp.where(inside, (row << 16) + (col << 6) + (outlets & (NZ - 1)), -1)
     rows = ROWS // PACK_BLOCKS
     flat = pl.BlockSpec((rows, COLS), lambda i: (i, 0))
-    deep = lambda n, width: pl.BlockSpec((n, rows, width), lambda i: (0, i, 0))
-    kept = pl.BlockSpec(line.shape, lambda i: (0, 0, 0))
     two = 2 * LANES
-    ends = TILES // 2 - 1, ROWS // 8 - 1
-    stack, side_a, side_b, line_a, line_b = pl.pallas_call(
-        pack_fields,
+
+    def block_specs(lead, *blocks):
+        return [
+            pl.BlockSpec(lead + shape, lambda i, at=at: (0,) * len(lead) + at) for shape, at in blocks
+        ]
+
+    sides = ((ROWS, two), (0, 0)), ((ROWS, two), (0, TILES // 2 - 1))
+    ends = ((8, COLS), (0, 0)), ((8, COLS), (ROWS // 8 - 1, 0))
+    fields = (sorption_kd, velocity, source, cell_type, target)
+    twice = [f for f in fields for _ in range(2)]
+
+    def specs(blocks):
+        return [b for f in fields for b in block_specs((3,) if f.ndim == 3 else (), *blocks)]
+
+    whole = lambda a: pl.BlockSpec(a.shape, lambda i: (0, 0, 0))
+    side_a, side_b = pl.pallas_call(
+        pack_sides,
+        grid=(1,),
+        out_shape=[side, side],
+        in_specs=specs(sides),
+        out_specs=[whole(side), whole(side)],
+        compiler_params=params(60),
+        name="pack_sides",
+    )(*twice)
+    stack, line_a, line_b = pl.pallas_call(
+        stack_fields,
         grid=(PACK_BLOCKS,),
-        out_shape=[
-            jax.ShapeDtypeStruct((STACK, ROWS, COLS), F32), side, side, line, line,
-        ],
-        in_specs=[
-            flat,
-            pl.BlockSpec((3, rows, two), lambda i: (0, i, 0)),
-            pl.BlockSpec((3, rows, two), lambda i: (0, i, ends[0])),
-            pl.BlockSpec((3, 8, COLS), lambda i: (0, 0, 0)),
-            pl.BlockSpec((3, 8, COLS), lambda i: (0, ends[1], 0)),
-            flat, flat,
-            pl.BlockSpec((rows, two), lambda i: (i, 0)),
-            pl.BlockSpec((rows, two), lambda i: (i, ends[0])),
-            pl.BlockSpec((8, COLS), lambda i: (0, 0)),
-            pl.BlockSpec((8, COLS), lambda i: (ends[1], 0)),
-        ],
-        out_specs=[deep(3, COLS), deep(10, LANES), deep(10, LANES), kept, kept],
+        out_shape=[jax.ShapeDtypeStruct((STACK, ROWS, COLS), F32), line, line],
+        in_specs=[HB, flat, flat, flat] + specs(ends),
+        out_specs=[pl.BlockSpec((3, rows, COLS), lambda i: (0, i, 0)), whole(line), whole(line)],
         compiler_params=params(60),
-        name="pack_fields",
-    )(sorption_kd, *[velocity] * 4, source, cell_type, *[target] * 4)
+        name="stack_fields",
+    )(side_a, sorption_kd, source, cell_type, *twice)
     x_a, x_b = swap(side_a, side_b, "gx")
     y_a, y_b = swap(line_a, line_b, "gy")
 
@@ -608,31 +656,45 @@
         out_shape=[window()] * 4 + [power] + [window()] * 8 + [message] * 2,
         in_specs=[SM] * 2 + [VM] * 3 + [HB] * 2,
         out_specs=[VM] * 15,
-        scratch_shapes=[*[pltpu.VMEM((3, ROWS, COLS), F32)] * 2, pltpu.SemaphoreType.DMA((6,))],
+        scratch_shapes=[*[pltpu.VMEM((3, ROWS, COLS), F32)] * 2, pltpu.SemaphoreType.DMA((2 * PARTS,))],
         compiler_params=params(FIRST_MIB),
         name="first_half",
     )(found, count, arrived, x_a, x_b, velocity, stack)
     coefs, (msg_a, msg_b) = rest[:8], rest[8:]
     got_a, got_b = swap(msg_a, msg_b, "gy")
 
-    kept = (u0, fst, d1, rate, *coefs)
+    edge_kd = jax.ShapeDtypeStruct((WT, 16, LANES), F32)
+    *coefs, aim, kd_edge, d2, mis, w, grad, w1 = pl.pallas_call(
+        middle,
+        out_shape=[window()] * 9 + [edge_kd] + [window()] * 5,
+        in_specs=[SM] * 2 + [VM] * 4 + [HB] + [VM] * 10,
+        out_specs=[VM] * 15,
+        input_output_aliases={9 + k: k for k in range(8)},
+        scratch_shapes=[
+            pltpu.VMEM((ROWS, COLS), F32),
+            pltpu.VMEM((7, TILES, 16, LANES), F32),
+            pltpu.SemaphoreType.DMA,
+        ],
+        compiler_params=params(8),
+        name="middle",
+    )(found, count, x_a, x_b, y_a, y_b, target, fst, rate, *coefs)
+
+    kept = (u0, fst, d1, rate, *coefs, aim, d2, mis, w, grad, w1)
     plane = jax.ShapeDtypeStruct((ROWS, COLS), F32)
-    work = pltpu.VMEM((WT, WR, LANES), F32)
     outs = pl.pallas_call(
         second_half,
-        out_shape=[plane, plane] + [window()] * 12,
-        in_specs=[SM] * 2 + [VM] * 6 + [HB] * 2 + [VM] * 13,
-        out_specs=[HB] * 2 + [VM] * 12,
-        input_output_aliases={11 + k: 2 + k for k in range(12)},
+        out_shape=[plane, plane] + [window()] * 18,
+        in_specs=[SM] * 2 + [VM] * 2 + [HB] + [VM] * 20,
+        out_specs=[HB] * 2 + [VM] * 18,
+        input_output_aliases={7 + k: 2 + k for k in range(18)},
         scratch_shapes=[
-            *[pltpu.VMEM((ROWS, COLS), F32)] * 4,
-            pltpu.VMEM((7, WT, 16, LANES), F32),
-            work, work, work, work, work, work,
+            *[pltpu.VMEM((ROWS, COLS), F32)] * 3,
+            pltpu.VMEM((7, 4, 16, LANES), F32),
             pltpu.SemaphoreType.DMA((4, 4)),
         ],
-        compiler_params=params(24),
+        compiler_params=params(12),
         name="second_half",
-    )(found, count, x_a, x_b, y_a, y_b, got_a, got_b, sorption_kd, target, power, *kept)
+    )(found, count, got_a, got_b, sorption_kd, power, kd_edge, *kept)
     return outs[0], outs[1]
 
 

time: 61.2 us -> 57.3 us (0.936)
  the two profiles are of different devices: /device:TPU:23 before, /device:TPU:104 now
where the time goes in v4:
time: 57.3 us; the launch traced here: 56.9 us
  Pallas kernels  33.5 us (58%)
  starting transfers between devices  21.7 us (38%)
  waiting for transfers between devices  0.87 us (2%)
  between operations  0.8 us (1%)
    ppermute x6, starting transfers between devices, swap(): return (lax.ppermute(a, axis, pairs(0)), lax.ppermute(b, axis, pairs(1)))  14.4 us
    all_to_all x1, starting transfers between devices, per_device(): lax.all_to_all(lines, 'gx', split_axis=0, concat_axis=0, tiled=True)  7.29 us
    pallas_call x1, Pallas kernels, per_device(): pl.pallas_call(second_half, out_shape=[plane, plane] + [window()] * 18, i...  7.08 us
    pallas_call x1, Pallas kernels, per_device(): pl.pallas_call(first_half, out_shape=[window()] * 4 + [power] + [window()...  6.26 us
    pallas_call x1, Pallas kernels, per_device(): pl.pallas_call(middle, out_shape=[window()] * 9 + [edge_kd] + [window()]...  5.75 us
    pallas_call x1, Pallas kernels, per_device(): pl.pallas_call(stack_fields, grid=(PACK_BLOCKS,), out_shape=[jax.ShapeDty...  5.43 us
    pallas_call x1, Pallas kernels, per_device(): pl.pallas_call(list_outlets, out_shape=[jax.ShapeDtypeStruct((outlets.sha...  4.3 us
    pallas_call x1, Pallas kernels, per_device(): pl.pallas_call(pack_lines, out_shape=jax.ShapeDtypeStruct((n_gx, checkpoi...  2.49 us
  transfers between devices with their start and end apart: 7, of which 1 were waited for; matrix products, arithmetic and copies ran while one was open for 0% of the time, Pallas kernels for 42%

profile of v4, /device:TPU:104, one launch (start us, length us, event | category | flops | bytes accessed | tf_op | source)
XLA Modules:
  0.0 56.9 jit_solution(7207497953673623687)
XLA Ops:
  0.6 2.5 %pack_lines.1 = f32[16,4,4608]{2,1,0:T(4,128)} custom-call(f32[1,4,65536]{2,1,0:T(4,128)} %src.1), custom_call_target="tpu_custom_call" | custom-call | tf_op jit(solution)/shard_map/pack_lines/pallas_call | solution.py:580
  3.1 7.3 %all-to-all-start = ((f32[16,4,4608]{2,1,0:T(4,128)}), f32[16,4,4608]{2,1,0:T(4,128)}, u32[]{:S(2)}, u32[]{:S(2)}) async-start(f32[16,4,4608]{2,1,0:T(4,128)} %pack_lines.1), calls=%async_computation | async-start | bytes 2359296 | tf_op jit(solution)/shard_map/all_to_all | solution.py:593
  10.4 2.2 %pack_sides.1 = (f32[10,64,128]{2,1,0:T(8,128)}, f32[10,64,128]{2,1,0:T(8,128)}) custom-call(f32[64,4096]{1,0:T(8,128)} %kd_h.1, f32[64,4096]{1,0:T(8,128)} %kd_h.1, f32[3,64,4096]{2,1,0:T(8,128)} %v_h.1, f32[3,64,4096]{2,1,0:T(8,128)} %v_h.1, f32[64,4096]{1,0:T(8,128)} %sb.1, f32[64,4096]{1,0:T(8,128)} %sb.1, s32[64,4096]{1,0:T(8,128)} %cb.1, ...), custom_call_target="tpu_custom_call" | custom-call | tf_op jit(solution)/shard_map/pack_sides/pallas_call | solution.py:619
  12.6 4.3 %collective-permute-start.1 = (f32[10,64,128]{2,1,0:T(8,128)}, f32[10,64,128]{2,1,0:T(8,128)S(1)}, u32[]{:S(2)}, u32[]{:S(2)}) collective-permute-start(f32[10,64,128]{2,1,0:T(8,128)} %get-tuple-element.44), channel_id=1, source_target_pairs={{8,16},{16,8},{24,32},{32,24},{40,48},{48,40},{56,64},{64,56},{72,... | collective-permute-start | bytes 983048 | tf_op jit(solution)/shard_map/ppermute | solution.py:574
  16.9 0.0 copy-start.3
  16.9 0.1 collective-permute-start
  17.0 0.0 copy-start
  17.0 5.4 %stack_fields.1 = (f32[6,64,4096]{2,1,0:T(8,128)}, f32[7,2,4096]{2,1,0:T(2,128)}, f32[7,2,4096]{2,1,0:T(2,128)}) custom-call(f32[10,64,128]{2,1,0:T(8,128)} %get-tuple-element.43.side, f32[64,4096]{1,0:T(8,128)} %kd_h.1, f32[64,4096]{1,0:T(8,128)} %sb.1, s32[64,4096]{1,0:T(8,128)} %cb.1, f32[64,4096]{1,0:T(8,128)} %kd_h.1, f32[64,4096]{1,0:T(8,128)} %kd_h.1, ...), custom_call_target="tpu_custom_call" | custom-call | tf_op jit(solution)/shard_map/stack_fields/pallas_call | solution.py:628
  22.5 0.5 collective-permute-start.4
  23.0 4.5 %collective-permute-start.5 = (f32[7,2,4096]{2,1,0:T(2,128)}, f32[7,2,4096]{2,1,0:T(2,128)}, u32[]{:S(2)}, u32[]{:S(2)}) collective-permute-start(f32[7,2,4096]{2,1,0:T(2,128)} %get-tuple-element.50), channel_id=1, source_target_pairs={{1,2},{2,1},{3,4},{4,3},{5,6},{6,5},{9,10},{10,9},{11,12},{12,11},... | collective-permute-start | bytes 688136 | tf_op jit(solution)/shard_map/ppermute | solution.py:574
  27.5 0.0 copy-done.3
  27.5 4.3 %list_outlets.1 = (s32[1024]{0:T(1024)S(1)}, s32[1]{0:T(128)}) custom-call(s32[1024]{0:T(1024)S(1)} %add_select_fusion.codes), custom_call_target="tpu_custom_call" | custom-call | tf_op jit(solution)/shard_map/list_outlets/pallas_call | solution.py:640
  31.8 0.9 %collective-permute-done.1.x_b = f32[10,64,128]{2,1,0:T(8,128)S(1)} collective-permute-done((f32[10,64,128]{2,1,0:T(8,128)}, f32[10,64,128]{2,1,0:T(8,128)S(1)}, u32[]{:S(2)}, u32[]{:S(2)}) %collective-permute-start.1) | collective-permute-done | bytes 327712 | tf_op jit(solution)/shard_map/ppermute | solution.py:574
  32.7 0.0 collective-permute-done.x_a
  32.7 0.0 all-to-all-done.lines
  32.7 0.0 copy-done
  32.7 0.0 copy-start.2
  32.7 6.3 %first_half.1 = (f32[36,80,128]{2,1,0:T(8,128)S(1)}, f32[36,80,128]{2,1,0:T(8,128)S(1)}, f32[36,80,128]{2,1,0:T(8,128)S(1)}, f32[36,80,128]{2,1,0:T(8,128)S(1)},...) custom-call(s32[1024]{0:T(1024)S(1)} %get-tuple-element.41.found, ...), custom_call_target="tpu_custom_call" | custom-call | tf_op jit(solution)/shard_map/first_half/pallas_call | solution.py:654
  39.0 0.5 collective-permute-start.2
  39.5 4.5 %collective-permute-start.3 = (f32[4,5120]{1,0:T(4,128)S(1)}, f32[4,5120]{1,0:T(4,128)S(1)}, u32[]{:S(2)}, u32[]{:S(2)}) collective-permute-start(f32[4,5120]{1,0:T(4,128)S(1)} %get-tuple-element.47), channel_id=1, source_target_pairs={{1,2},{2,1},{3,4},{4,3},{5,6},{6,5},{9,10},{10,9},{11,12},{12,11},... | collective-permute-start | bytes 245768 | tf_op jit(solution)/shard_map/ppermute | solution.py:574
  44.0 0.0 collective-permute-done.4.y_a
  44.0 0.0 collective-permute-done.5.y_b
  44.0 0.0 copy-done.2
  44.0 0.0 copy-start.1
  44.0 5.7 %middle.1 = (f32[36,80,128]{2,1,0:T(8,128)S(1)}, f32[36,80,128]{2,1,0:T(8,128)S(1)}, f32[36,80,128]{2,1,0:T(8,128)S(1)}, f32[36,80,128]{2,1,0:T(8,128)S(1)}, f32...) custom-call(s32[1024]{0:T(1024)S(1)} %get-tuple-element.41.found, ...), custom_call_target="tpu_custom_call", output_to_operand_aliasing={{0}: (9, {}), {1}: (10, {}), {2}: (11, {}), {3}: (12, {}), ... | custom-call | tf_op jit(solution)/shard_map/middle/pallas_call | solution.py:667
  49.8 0.0 collective-permute-done.2.msg_a
  49.8 0.0 collective-permute-done.3.msg_b
  49.8 0.0 copy-done.1
  49.8 7.1 %second_half.1 = (f32[64,4096]{1,0:T(8,128)}, f32[64,4096]{1,0:T(8,128)}, f32[36,80,128]{2,1,0:T(8,128)S(1)}, f32[36,80,128]{2,1,0:T(8,128)S(1)}, f32[36,80,128]...) custom-call(s32[1024]{0:T(1024)S(1)} %get-tuple-element.41.found, ...), custom_call_target="tpu_custom_call", output_to_operand_aliasing={{2}: (7, {}), {3}: (8, {}), {4}: (9, {}), {5}: (10, {}), {6... | custom-call | tf_op jit(solution)/shard_map/second_half/pallas_call | solution.py:684
  (1 shorter events, 0.0 us)
Async XLA Ops:
  3.1 29.6 %all-to-all-start = ((f32[16,4,4608]{2,1,0:T(4,128)}), f32[16,4,4608]{2,1,0:T(4,128)}, u32[]{:S(2)}, u32[]{:S(2)}) async-start(f32[16,4,4608]{2,1,0:T(4,128)} %pack_lines.1), calls=%async_computation | async-start | bytes 2359296 | tf_op jit(solution)/shard_map/all_to_all | solution.py:593
  12.6 20.1 %collective-permute-start.1 = (f32[10,64,128]{2,1,0:T(8,128)}, f32[10,64,128]{2,1,0:T(8,128)S(1)}, u32[]{:S(2)}, u32[]{:S(2)}) collective-permute-start(f32[10,64,128]{2,1,0:T(8,128)} %get-tuple-element.44), channel_id=1, source_target_pairs={{8,16},{16,8},{24,32},{32,24},{40,48},{48,40},{56,64},{64,56},{72,... | collective-permute-start | bytes 983048 | tf_op jit(solution)/shard_map/ppermute | solution.py:574
  16.9 10.6 %copy-start.3 = (s32[1024]{0:T(1024)S(1)}, s32[1024]{0:T(1024)}, u32[]{:S(2)}) copy-start(s32[1024]{0:T(1024)} %param.13) | copy-start | bytes 12292
  16.9 15.8 %collective-permute-start = (f32[10,64,128]{2,1,0:T(8,128)}, f32[10,64,128]{2,1,0:T(8,128)}, u32[]{:S(2)}, u32[]{:S(2)}) collective-permute-start(f32[10,64,128]{2,1,0:T(8,128)} %get-tuple-element.43.side), channel_id=1, source_target_pairs={{0,8},{8,0},{16,24},{24,16},{32,40},{40,32},{48,56},{56,48},{64,72... | collective-permute-start | bytes 983048 | tf_op jit(solution)/shard_map/ppermute | solution.py:574
  17.0 15.7 %copy-start = (f32[3,64,4096]{2,1,0:T(8,128)S(1)}, f32[3,64,4096]{2,1,0:T(8,128)}, u32[]{:S(2)}) copy-start(f32[3,64,4096]{2,1,0:T(8,128)} %v_h.1) | copy-start | bytes 9437188
  22.5 21.5 %collective-permute-start.4 = (f32[7,2,4096]{2,1,0:T(2,128)}, f32[7,2,4096]{2,1,0:T(2,128)}, u32[]{:S(2)}, u32[]{:S(2)}) collective-permute-start(f32[7,2,4096]{2,1,0:T(2,128)} %get-tuple-element.49), channel_id=1, source_target_pairs={{0,1},{1,0},{2,3},{3,2},{4,5},{5,4},{6,7},{7,6},{8,9},{9,8},{10,11... | collective-permute-start | bytes 688136 | tf_op jit(solution)/shard_map/ppermute | solution.py:574
  23.0 21.1 %collective-permute-start.5 = (f32[7,2,4096]{2,1,0:T(2,128)}, f32[7,2,4096]{2,1,0:T(2,128)}, u32[]{:S(2)}, u32[]{:S(2)}) collective-permute-start(f32[7,2,4096]{2,1,0:T(2,128)} %get-tuple-element.50), channel_id=1, source_target_pairs={{1,2},{2,1},{3,4},{4,3},{5,6},{6,5},{9,10},{10,9},{11,12},{12,11},... | collective-permute-start | bytes 688136 | tf_op jit(solution)/shard_map/ppermute | solution.py:574
  32.7 11.3 %copy-start.2 = (f32[64,4096]{1,0:T(8,128)S(1)}, f32[64,4096]{1,0:T(8,128)}, u32[]{:S(2)}) copy-start(f32[64,4096]{1,0:T(8,128)} %t_h.1) | copy-start | bytes 3145732
  39.0 10.8 %collective-permute-start.2 = (f32[4,5120]{1,0:T(4,128)S(1)}, f32[4,5120]{1,0:T(4,128)S(1)}, u32[]{:S(2)}, u32[]{:S(2)}) collective-permute-start(f32[4,5120]{1,0:T(4,128)S(1)} %get-tuple-element.46), channel_id=1, source_target_pairs={{0,1},{1,0},{2,3},{3,2},{4,5},{5,4},{6,7},{7,6},{8,9},{9,8},{10,11... | collective-permute-start | bytes 245768 | tf_op jit(solution)/shard_map/ppermute | solution.py:574
  39.5 10.3 %collective-permute-start.3 = (f32[4,5120]{1,0:T(4,128)S(1)}, f32[4,5120]{1,0:T(4,128)S(1)}, u32[]{:S(2)}, u32[]{:S(2)}) collective-permute-start(f32[4,5120]{1,0:T(4,128)S(1)} %get-tuple-element.47), channel_id=1, source_target_pairs={{1,2},{2,1},{3,4},{4,3},{5,6},{6,5},{9,10},{10,9},{11,12},{12,11},... | collective-permute-start | bytes 245768 | tf_op jit(solution)/shard_map/ppermute | solution.py:574
  44.0 5.8 %copy-start.1 = (f32[64,4096]{1,0:T(8,128)S(1)}, f32[64,4096]{1,0:T(8,128)}, u32[]{:S(2)}) copy-start(f32[64,4096]{1,0:T(8,128)} %kd_h.1) | copy-start | bytes 3145732

commit v5 on v4

--- a/solution.py
+++ b/solution.py
@@ -28,7 +28,7 @@
 MIB = 1 << 20
 FIRST_MIB = 27
 STACK = 6
-UNROLL = 4
+UNROLL = 8
 PACK_BLOCKS = 4
 PARTS = 4
 
@@ -120,7 +120,8 @@
         side_b[f] = jnp.where(odd, high, low)
 
 
-def stack_fields(side, kd, s, c, kdt, kdb, vt, vb, st, sb, ct, cb, tt, tb, stack, line_a, line_b):
+def stack_fields(side, codes, code_rows, kd, s, c, kdt, kdb, vt, vb, st, sb, ct, cb, tt, tb,
+                 stack, line_a, line_b, found, count):
     stack[0] = kd[...]
     stack[1] = jnp.where(c[...] == 1, s[...], 0.0)
     stack[2] = jnp.where(c[...] == 2, DRAIN, 0.0).astype(F32)
@@ -135,17 +136,25 @@
             line_b[f] = jnp.where(odd, high, low)
 
 
-def list_outlets(codes, found, count):
+    @pl.when(pl.program_id(0) == 0)
+    def _():
+        count[0] = 0
+
     unroll = 32
-
-    def step(i, n):
-        values = [codes[i * unroll + k] for k in range(unroll)]
-        for value in values:
-            found[n] = value
-            n = n + 1 + (value >> 31)
-        return n
-
-    count[0] = lax.fori_loop(0, codes.shape[0] // unroll, step, jnp.int32(0))
+    share = code_rows.shape[0] // PACK_BLOCKS
+    for k in range(share):
+        row = pl.program_id(0) * share + k
+
+        @pl.when(jnp.max(code_rows[pl.ds(row, 1), :].astype(F32)) >= 0.0)
+        def _():
+            def compact(i, n):
+                values = [codes[row * LANES + i * unroll + j] for j in range(unroll)]
+                for value in values:
+                    found[n] = value
+                    n = n + 1 + (value >> 31)
+                return n
+
+            count[0] = lax.fori_loop(0, LANES // unroll, compact, count[0])
 
 
 def coefficients(v0, v1, v2, drain):
@@ -205,7 +214,7 @@
     return STEP / (1.0 + BULK * kd * power)
 
 
-def first_half(found, count, lines, x_a, x_b, v_h, stack_h,
+def first_half(lines, x_a, x_b, v_h, stack_h,
                u0, fst, d1, rate, power, cn, cs, ce, cw, cu, cd, cc, src, msg_a, msg_b,
                v, stack, sems):
     loads = []
@@ -598,6 +607,7 @@
     col = ((outlets >> 6) & 1023) - gx * (COLS // NZ) + 4
     inside = (row >= BASE - 2) & (row < BASE + ROWS + 2) & (col >= 2) & (col < 70)
     codes = jnp.where(inside, (row << 16) + (col << 6) + (outlets & (NZ - 1)), -1)
+    code_rows = codes.reshape(-1, LANES)
     rows = ROWS // PACK_BLOCKS
     flat = pl.BlockSpec((rows, COLS), lambda i: (i, 0))
     two = 2 * LANES
@@ -625,41 +635,36 @@
         compiler_params=params(60),
         name="pack_sides",
     )(*twice)
-    stack, line_a, line_b = pl.pallas_call(
+    stack, line_a, line_b, found, count = pl.pallas_call(
         stack_fields,
         grid=(PACK_BLOCKS,),
-        out_shape=[jax.ShapeDtypeStruct((STACK, ROWS, COLS), F32), line, line],
-        in_specs=[HB, flat, flat, flat] + specs(ends),
-        out_specs=[pl.BlockSpec((3, rows, COLS), lambda i: (0, i, 0)), whole(line), whole(line)],
-        compiler_params=params(60),
-        name="stack_fields",
-    )(side_a, sorption_kd, source, cell_type, *twice)
-    x_a, x_b = swap(side_a, side_b, "gx")
-    y_a, y_b = swap(line_a, line_b, "gy")
-
-    found, count = pl.pallas_call(
-        list_outlets,
         out_shape=[
+            jax.ShapeDtypeStruct((STACK, ROWS, COLS), F32), line, line,
             jax.ShapeDtypeStruct((outlets.shape[0],), jnp.int32),
             jax.ShapeDtypeStruct((1,), jnp.int32),
         ],
-        in_specs=[SM],
-        out_specs=[SM, SM],
-        compiler_params=params(1),
-        name="list_outlets",
-    )(codes)
+        in_specs=[HB, SM, pl.BlockSpec(code_rows.shape, lambda i: (0, 0)), flat, flat, flat]
+        + specs(ends),
+        out_specs=[
+            pl.BlockSpec((3, rows, COLS), lambda i: (0, i, 0)), whole(line), whole(line), SM, SM,
+        ],
+        compiler_params=params(60),
+        name="stack_fields",
+    )(side_a, codes, code_rows, sorption_kd, source, cell_type, *twice)
+    x_a, x_b = swap(side_a, side_b, "gx")
+    y_a, y_b = swap(line_a, line_b, "gy")
 
     message = jax.ShapeDtypeStruct((4, MCOLS), F32)
     power = jax.ShapeDtypeStruct((TILES, ROWS, LANES), F32)
     u0, fst, d1, rate, power, *rest = pl.pallas_call(
         first_half,
         out_shape=[window()] * 4 + [power] + [window()] * 8 + [message] * 2,
-        in_specs=[SM] * 2 + [VM] * 3 + [HB] * 2,
+        in_specs=[VM] * 3 + [HB] * 2,
         out_specs=[VM] * 15,
         scratch_shapes=[*[pltpu.VMEM((3, ROWS, COLS), F32)] * 2, pltpu.SemaphoreType.DMA((2 * PARTS,))],
         compiler_params=params(FIRST_MIB),
         name="first_half",
-    )(found, count, arrived, x_a, x_b, velocity, stack)
+    )(arrived, x_a, x_b, velocity, stack)
     coefs, (msg_a, msg_b) = rest[:8], rest[8:]
     got_a, got_b = swap(msg_a, msg_b, "gy")
 

time: 57.3 us -> 55.3 us (0.965)
  Pallas kernels: 33.5 us -> 29.1 us
  other arithmetic: 0.01 us -> 1.21 us
  waiting for transfers between devices: 0.87 us -> 1.69 us
    pallas_call x1 -> x0, Pallas kernels: 4.3 us -> none  [per_device(): pl.pallas_call(list_outlets, out_shape=[jax.ShapeDtypeStruct((outlets.sha...]
    ppermute x6, waiting for transfers between devices: 0.86 us -> 1.69 us  [swap(): return (lax.ppermute(a, axis, pairs(0)), lax.ppermute(b, axis, pairs(1)))]
    pallas_call x1, Pallas kernels: 5.43 us -> 6.23 us  [per_device(): pl.pallas_call(stack_fields, grid=(PACK_BLOCKS,), out_shape=[jax.ShapeDty...]
    pallas_call x1, Pallas kernels: 6.26 us -> 5.62 us  [per_device(): pl.pallas_call(first_half, out_shape=[window()] * 4 + [power] + [window()...]
    reshape x0 -> x1, other arithmetic: none -> 0.6 us  [per_device(): code_rows = codes.reshape(-1, LANES)]
    select_n x1, other arithmetic: 0.01 us -> 0.6 us  [per_device(): codes = jnp.where(inside, (row << 16) + (col << 6) + (outlets & NZ - 1), -1)]
  transfers between devices with their start and end apart: 7 -> 7, of which waited for: 1 -> 1; matrix products, arithmetic and copies ran while one was open for 0% -> 2% of each run, Pallas kernels for 42% -> 36%
where the time goes in v5:
time: 55.3 us; the launch traced here: 54.6 us
  Pallas kernels  29.1 us (53%)
  starting transfers between devices  21.7 us (39%)
  waiting for transfers between devices  1.69 us (3%)
  other arithmetic  1.21 us (2%)
  between operations  0.8 us (1%)
    ppermute x6, starting transfers between devices, swap(): return (lax.ppermute(a, axis, pairs(0)), lax.ppermute(b, axis, pairs(1)))  14.4 us
    all_to_all x1, starting transfers between devices, per_device(): lax.all_to_all(lines, 'gx', split_axis=0, concat_axis=0, tiled=True)  7.29 us
    pallas_call x1, Pallas kernels, per_device(): pl.pallas_call(second_half, out_shape=[plane, plane] + [window()] * 18, i...  7.09 us
    pallas_call x1, Pallas kernels, per_device(): pl.pallas_call(stack_fields, grid=(PACK_BLOCKS,), out_shape=[jax.ShapeDty...  6.23 us
    pallas_call x1, Pallas kernels, per_device(): pl.pallas_call(first_half, out_shape=[window()] * 4 + [power] + [window()...  5.62 us
    pallas_call x1, Pallas kernels, per_device(): pl.pallas_call(middle, out_shape=[window()] * 9 + [edge_kd] + [window()]...  5.53 us
    pallas_call x1, Pallas kernels, per_device(): pl.pallas_call(pack_lines, out_shape=jax.ShapeDtypeStruct((n_gx, checkpoi...  2.49 us
    pallas_call x1, Pallas kernels, per_device(): pl.pallas_call(pack_sides, grid=(1,), out_shape=[side, side], in_specs=sp...  2.19 us
  transfers between devices with their start and end apart: 7, of which 1 were waited for; matrix products, arithmetic and copies ran while one was open for 2% of the time, Pallas kernels for 36%

profile of v5, /device:TPU:104, one launch (start us, length us, event | category | flops | bytes accessed | tf_op | source)
XLA Modules:
  0.0 54.6 jit_solution(14109439602920221579)
XLA Ops:
  0.6 2.5 %pack_lines.1 = f32[16,4,4608]{2,1,0:T(4,128)} custom-call(f32[1,4,65536]{2,1,0:T(4,128)} %src.1), custom_call_target="tpu_custom_call" | custom-call | tf_op jit(solution)/shard_map/pack_lines/pallas_call | solution.py:589
  3.1 7.3 %all-to-all-start = ((f32[16,4,4608]{2,1,0:T(4,128)}), f32[16,4,4608]{2,1,0:T(4,128)}, u32[]{:S(2)}, u32[]{:S(2)}) async-start(f32[16,4,4608]{2,1,0:T(4,128)} %pack_lines.1), calls=%async_computation | async-start | bytes 2359296 | tf_op jit(solution)/shard_map/all_to_all | solution.py:602
  10.4 0.0 copy-start.4
  10.4 2.2 %pack_sides.1 = (f32[10,64,128]{2,1,0:T(8,128)}, f32[10,64,128]{2,1,0:T(8,128)}) custom-call(f32[64,4096]{1,0:T(8,128)} %kd_h.1, f32[64,4096]{1,0:T(8,128)} %kd_h.1, f32[3,64,4096]{2,1,0:T(8,128)} %v_h.1, f32[3,64,4096]{2,1,0:T(8,128)} %v_h.1, f32[64,4096]{1,0:T(8,128)} %sb.1, f32[64,4096]{1,0:T(8,128)} %sb.1, s32[64,4096]{1,0:T(8,128)} %cb.1, ...), custom_call_target="tpu_custom_call" | custom-call | tf_op jit(solution)/shard_map/pack_sides/pallas_call | solution.py:629
  12.6 4.3 %collective-permute-start.1 = (f32[10,64,128]{2,1,0:T(8,128)}, f32[10,64,128]{2,1,0:T(8,128)S(1)}, u32[]{:S(2)}, u32[]{:S(2)}) collective-permute-start(f32[10,64,128]{2,1,0:T(8,128)} %get-tuple-element.44), channel_id=1, source_target_pairs={{8,16},{16,8},{24,32},{32,24},{40,48},{48,40},{56,64},{64,56},{72,... | collective-permute-start | bytes 983048 | tf_op jit(solution)/shard_map/ppermute | solution.py:583
  16.9 0.1 collective-permute-start
  17.0 0.0 copy-done.4
  17.1 0.6 %fusion.7.code_rows = s32[8,128]{1,0:T(8,128)} fusion(s32[1024]{0:T(1024)S(1)} %copy-done.4, s32[]{:T(128)S(6)} %mul.7, s32[]{:T(128)S(6)} %mul.6), kind=kLoop, calls=%fused_computation.10 | loop fusion | flops 20480 | bytes 8200 | tf_op jit(solution)/shard_map/reshape | solution.py:610
  17.7 0.6 %add_select_fusion.codes = s32[1024]{0:T(1024)} fusion(s32[1024]{0:T(1024)S(1)} %copy-done.4, s32[]{:T(128)S(6)} %mul.7, s32[]{:T(128)S(6)} %mul.6), kind=kLoop, calls=%fused_computation | loop fusion | flops 20480 | bytes 8200 | tf_op jit(solution)/shard_map/jit(_where)/select_n | solution.py:609
  18.3 0.0 copy-start
  18.3 6.2 %stack_fields.1 = (f32[6,64,4096]{2,1,0:T(8,128)}, f32[7,2,4096]{2,1,0:T(2,128)}, f32[7,2,4096]{2,1,0:T(2,128)}, s32[1024]{0:T(1024)}, s32[1]{0:T(128)}) custom-call(f32[10,64,128]{2,1,0:T(8,128)} %get-tuple-element.41.side, s32[1024]{0:T(1024)} %add_select_fusion.codes, s32[8,128]{1,0:T(8,128)} %fusion.7.code_rows, f32[64,4096]{1,0:T(8,128)} %kd_h.1, ...), custom_call_target="tpu_custom_call" | custom-call | tf_op jit(solution)/shard_map/stack_fields/pallas_call | solution.py:638
  24.5 1.3 %collective-permute-start.4 = (f32[7,2,4096]{2,1,0:T(2,128)}, f32[7,2,4096]{2,1,0:T(2,128)}, u32[]{:S(2)}, u32[]{:S(2)}) collective-permute-start(f32[7,2,4096]{2,1,0:T(2,128)} %get-tuple-element.49), channel_id=1, source_target_pairs={{0,1},{1,0},{2,3},{3,2},{4,5},{5,4},{6,7},{7,6},{8,9},{9,8},{10,11... | collective-permute-start | bytes 688136 | tf_op jit(solution)/shard_map/ppermute | solution.py:583
  25.8 4.0 %collective-permute-start.5 = (f32[7,2,4096]{2,1,0:T(2,128)}, f32[7,2,4096]{2,1,0:T(2,128)}, u32[]{:S(2)}, u32[]{:S(2)}) collective-permute-start(f32[7,2,4096]{2,1,0:T(2,128)} %get-tuple-element.50), channel_id=1, source_target_pairs={{1,2},{2,1},{3,4},{4,3},{5,6},{6,5},{9,10},{10,9},{11,12},{12,11},... | collective-permute-start | bytes 688136 | tf_op jit(solution)/shard_map/ppermute | solution.py:583
  29.8 1.7 %collective-permute-done.1.x_b = f32[10,64,128]{2,1,0:T(8,128)S(1)} collective-permute-done((f32[10,64,128]{2,1,0:T(8,128)}, f32[10,64,128]{2,1,0:T(8,128)S(1)}, u32[]{:S(2)}, u32[]{:S(2)}) %collective-permute-start.1) | collective-permute-done | bytes 327712 | tf_op jit(solution)/shard_map/ppermute | solution.py:583
  31.4 0.0 collective-permute-done.x_a
  31.4 0.0 all-to-all-done.lines
  31.4 0.0 copy-done
  31.4 0.0 copy-start.2
  31.5 0.0 copy-start.3
  31.5 5.6 %first_half.1 = (f32[36,80,128]{2,1,0:T(8,128)S(1)}, f32[36,80,128]{2,1,0:T(8,128)S(1)}, f32[36,80,128]{2,1,0:T(8,128)S(1)}, f32[36,80,128]{2,1,0:T(8,128)S(1)},...) custom-call(f32[16,4,4608]{2,1,0:T(4,128)} %all-to-all-done.lines, ...), custom_call_target="tpu_custom_call" | custom-call | tf_op jit(solution)/shard_map/first_half/pallas_call | solution.py:659
  37.1 0.5 collective-permute-start.2
  37.6 4.3 %collective-permute-start.3 = (f32[4,5120]{1,0:T(4,128)S(1)}, f32[4,5120]{1,0:T(4,128)S(1)}, u32[]{:S(2)}, u32[]{:S(2)}) collective-permute-start(f32[4,5120]{1,0:T(4,128)S(1)} %get-tuple-element.47), channel_id=1, source_target_pairs={{1,2},{2,1},{3,4},{4,3},{5,6},{6,5},{9,10},{10,9},{11,12},{12,11},... | collective-permute-start | bytes 245768 | tf_op jit(solution)/shard_map/ppermute | solution.py:583
  41.9 0.0 collective-permute-done.4.y_a
  41.9 0.0 collective-permute-done.5.y_b
  41.9 0.0 copy-done.2
  41.9 0.0 copy-done.3
  41.9 0.0 copy-start.1
  41.9 5.5 %middle.1 = (f32[36,80,128]{2,1,0:T(8,128)S(1)}, f32[36,80,128]{2,1,0:T(8,128)S(1)}, f32[36,80,128]{2,1,0:T(8,128)S(1)}, f32[36,80,128]{2,1,0:T(8,128)S(1)}, f32...) custom-call(s32[1024]{0:T(1024)S(1)} %copy-done.3, ...), custom_call_target="tpu_custom_call", output_to_operand_aliasing={{0}: (9, {}), {1}: (10, {}), {2}: (11, {}), {3}: (12, {}), ... | custom-call | tf_op jit(solution)/shard_map/middle/pallas_call | solution.py:672
  47.5 0.0 collective-permute-done.2.msg_a
  47.5 0.0 collective-permute-done.3.msg_b
  47.5 0.0 copy-done.1
  47.5 7.1 %second_half.1 = (f32[64,4096]{1,0:T(8,128)}, f32[64,4096]{1,0:T(8,128)}, f32[36,80,128]{2,1,0:T(8,128)S(1)}, f32[36,80,128]{2,1,0:T(8,128)S(1)}, f32[36,80,128]...) custom-call(s32[1024]{0:T(1024)S(1)} %copy-done.3, ...), custom_call_target="tpu_custom_call", output_to_operand_aliasing={{2}: (7, {}), {3}: (8, {}), {4}: (9, {}), {5}: (10, {}), {6... | custom-call | tf_op jit(solution)/shard_map/second_half/pallas_call | solution.py:689
Async XLA Ops:
  3.1 28.3 %all-to-all-start = ((f32[16,4,4608]{2,1,0:T(4,128)}), f32[16,4,4608]{2,1,0:T(4,128)}, u32[]{:S(2)}, u32[]{:S(2)}) async-start(f32[16,4,4608]{2,1,0:T(4,128)} %pack_lines.1), calls=%async_computation | async-start | bytes 2359296 | tf_op jit(solution)/shard_map/all_to_all | solution.py:602
  10.4 6.6 %copy-start.4 = (s32[1024]{0:T(1024)S(1)}, s32[1024]{0:T(1024)}, u32[]{:S(2)}) copy-start(s32[1024]{0:T(1024)} %param.13) | copy-start | bytes 12292
  12.6 18.8 %collective-permute-start.1 = (f32[10,64,128]{2,1,0:T(8,128)}, f32[10,64,128]{2,1,0:T(8,128)S(1)}, u32[]{:S(2)}, u32[]{:S(2)}) collective-permute-start(f32[10,64,128]{2,1,0:T(8,128)} %get-tuple-element.44), channel_id=1, source_target_pairs={{8,16},{16,8},{24,32},{32,24},{40,48},{48,40},{56,64},{64,56},{72,... | collective-permute-start | bytes 983048 | tf_op jit(solution)/shard_map/ppermute | solution.py:583
  16.9 14.5 %collective-permute-start = (f32[10,64,128]{2,1,0:T(8,128)}, f32[10,64,128]{2,1,0:T(8,128)}, u32[]{:S(2)}, u32[]{:S(2)}) collective-permute-start(f32[10,64,128]{2,1,0:T(8,128)} %get-tuple-element.41.side), channel_id=1, source_target_pairs={{0,8},{8,0},{16,24},{24,16},{32,40},{40,32},{48,56},{56,48},{64,72... | collective-permute-start | bytes 983048 | tf_op jit(solution)/shard_map/ppermute | solution.py:583
  18.3 13.2 %copy-start = (f32[3,64,4096]{2,1,0:T(8,128)S(1)}, f32[3,64,4096]{2,1,0:T(8,128)}, u32[]{:S(2)}) copy-start(f32[3,64,4096]{2,1,0:T(8,128)} %v_h.1) | copy-start | bytes 9437188
  24.5 17.4 %collective-permute-start.4 = (f32[7,2,4096]{2,1,0:T(2,128)}, f32[7,2,4096]{2,1,0:T(2,128)}, u32[]{:S(2)}, u32[]{:S(2)}) collective-permute-start(f32[7,2,4096]{2,1,0:T(2,128)} %get-tuple-element.49), channel_id=1, source_target_pairs={{0,1},{1,0},{2,3},{3,2},{4,5},{5,4},{6,7},{7,6},{8,9},{9,8},{10,11... | collective-permute-start | bytes 688136 | tf_op jit(solution)/shard_map/ppermute | solution.py:583
  25.8 16.1 %collective-permute-start.5 = (f32[7,2,4096]{2,1,0:T(2,128)}, f32[7,2,4096]{2,1,0:T(2,128)}, u32[]{:S(2)}, u32[]{:S(2)}) collective-permute-start(f32[7,2,4096]{2,1,0:T(2,128)} %get-tuple-element.50), channel_id=1, source_target_pairs={{1,2},{2,1},{3,4},{4,3},{5,6},{6,5},{9,10},{10,9},{11,12},{12,11},... | collective-permute-start | bytes 688136 | tf_op jit(solution)/shard_map/ppermute | solution.py:583
  31.4 10.5 %copy-start.2 = (f32[64,4096]{1,0:T(8,128)S(1)}, f32[64,4096]{1,0:T(8,128)}, u32[]{:S(2)}) copy-start(f32[64,4096]{1,0:T(8,128)} %t_h.1) | copy-start | bytes 3145732
  31.5 10.5 %copy-start.3 = (s32[1024]{0:T(1024)S(1)}, s32[1024]{0:T(1024)}, u32[]{:S(2)}) copy-start(s32[1024]{0:T(1024)} %get-tuple-element.42.found) | copy-start | bytes 12292
  37.1 10.4 %collective-permute-start.2 = (f32[4,5120]{1,0:T(4,128)S(1)}, f32[4,5120]{1,0:T(4,128)S(1)}, u32[]{:S(2)}, u32[]{:S(2)}) collective-permute-start(f32[4,5120]{1,0:T(4,128)S(1)} %get-tuple-element.46), channel_id=1, source_target_pairs={{0,1},{1,0},{2,3},{3,2},{4,5},{5,4},{6,7},{7,6},{8,9},{9,8},{10,11... | collective-permute-start | bytes 245768 | tf_op jit(solution)/shard_map/ppermute | solution.py:583
  37.6 9.9 %collective-permute-start.3 = (f32[4,5120]{1,0:T(4,128)S(1)}, f32[4,5120]{1,0:T(4,128)S(1)}, u32[]{:S(2)}, u32[]{:S(2)}) collective-permute-start(f32[4,5120]{1,0:T(4,128)S(1)} %get-tuple-element.47), channel_id=1, source_target_pairs={{1,2},{2,1},{3,4},{4,3},{5,6},{6,5},{9,10},{10,9},{11,12},{12,11},... | collective-permute-start | bytes 245768 | tf_op jit(solution)/shard_map/ppermute | solution.py:583
  41.9 5.6 %copy-start.1 = (f32[64,4096]{1,0:T(8,128)S(1)}, f32[64,4096]{1,0:T(8,128)}, u32[]{:S(2)}) copy-start(f32[64,4096]{1,0:T(8,128)} %kd_h.1) | copy-start | bytes 3145732

commit v6 on v5

--- a/solution.py
+++ b/solution.py
@@ -532,12 +532,12 @@
         return tuple(easts)
 
     first_west = tuple(east_of(u0, 0, 0, a, 8) for a, _ in edge_spans)
-    lax.fori_loop(0, WT, edge_step, first_west, unroll=12)
+    lax.fori_loop(0, WT, edge_step, first_west, unroll=18)
 
     spans = range(BASE - 4, BASE + ROWS + 4, 8)
     outer = [a for a in spans if a not in INNER]
     step, start = second_step(fst, coef, src, rate, target, d2, mis, w, outer)
-    lax.fori_loop(1, WT - 1, step, start, unroll=9)
+    lax.fori_loop(1, WT - 1, step, start, unroll=17)
 
     weigh_outlets(found, count, mis, w, False)
     back = adjoint_step(coef, rate, mis, w, grad, w1, [a for a in spans if a not in BACK])

time: 55.3 us -> 54.6 us (0.987)
  waiting for transfers between devices: 1.69 us -> 0.89 us
  Pallas kernels: 29.1 us -> 28.5 us
    ppermute x6, waiting for transfers between devices: 1.69 us -> 0.89 us  [swap(): return (lax.ppermute(a, axis, pairs(0)), lax.ppermute(b, axis, pairs(1)))]
    pallas_call x1, Pallas kernels: 7.09 us -> 6.49 us  [per_device(): pl.pallas_call(second_half, out_shape=[plane, plane] + [window()] * 18, i...]
where the time goes in v6:
time: 54.6 us; the launch traced here: 53.6 us
  Pallas kernels  28.5 us (52%)
  starting transfers between devices  22.1 us (40%)
  other arithmetic  1.21 us (2%)
  waiting for transfers between devices  0.89 us (2%)
  between operations  0.8 us (1%)
    ppermute x6, starting transfers between devices, swap(): return (lax.ppermute(a, axis, pairs(0)), lax.ppermute(b, axis, pairs(1)))  14.8 us
    all_to_all x1, starting transfers between devices, per_device(): lax.all_to_all(lines, 'gx', split_axis=0, concat_axis=0, tiled=True)  7.29 us
    pallas_call x1, Pallas kernels, per_device(): pl.pallas_call(second_half, out_shape=[plane, plane] + [window()] * 18, i...  6.49 us
    pallas_call x1, Pallas kernels, per_device(): pl.pallas_call(stack_fields, grid=(PACK_BLOCKS,), out_shape=[jax.ShapeDty...  6.23 us
    pallas_call x1, Pallas kernels, per_device(): pl.pallas_call(first_half, out_shape=[window()] * 4 + [power] + [window()...  5.62 us
    pallas_call x1, Pallas kernels, per_device(): pl.pallas_call(middle, out_shape=[window()] * 9 + [edge_kd] + [window()]...  5.52 us
    pallas_call x1, Pallas kernels, per_device(): pl.pallas_call(pack_lines, out_shape=jax.ShapeDtypeStruct((n_gx, checkpoi...  2.49 us
    pallas_call x1, Pallas kernels, per_device(): pl.pallas_call(pack_sides, grid=(1,), out_shape=[side, side], in_specs=sp...  2.19 us
  transfers between devices with their start and end apart: 7, of which 1 were waited for; matrix products, arithmetic and copies ran while one was open for 2% of the time, Pallas kernels for 36%

profile of v6, /device:TPU:104, one launch (start us, length us, event | category | flops | bytes accessed | tf_op | source)
XLA Modules:
  0.0 53.6 jit_solution(6826302177074657618)
XLA Ops:
  0.6 2.5 %pack_lines.1 = f32[16,4,4608]{2,1,0:T(4,128)} custom-call(f32[1,4,65536]{2,1,0:T(4,128)} %src.1), custom_call_target="tpu_custom_call" | custom-call | tf_op jit(solution)/shard_map/pack_lines/pallas_call | solution.py:589
  3.1 7.3 %all-to-all-start = ((f32[16,4,4608]{2,1,0:T(4,128)}), f32[16,4,4608]{2,1,0:T(4,128)}, u32[]{:S(2)}, u32[]{:S(2)}) async-start(f32[16,4,4608]{2,1,0:T(4,128)} %pack_lines.1), calls=%async_computation | async-start | bytes 2359296 | tf_op jit(solution)/shard_map/all_to_all | solution.py:602
  10.4 0.0 copy-start.4
  10.4 2.2 %pack_sides.1 = (f32[10,64,128]{2,1,0:T(8,128)}, f32[10,64,128]{2,1,0:T(8,128)}) custom-call(f32[64,4096]{1,0:T(8,128)} %kd_h.1, f32[64,4096]{1,0:T(8,128)} %kd_h.1, f32[3,64,4096]{2,1,0:T(8,128)} %v_h.1, f32[3,64,4096]{2,1,0:T(8,128)} %v_h.1, f32[64,4096]{1,0:T(8,128)} %sb.1, f32[64,4096]{1,0:T(8,128)} %sb.1, s32[64,4096]{1,0:T(8,128)} %cb.1, ...), custom_call_target="tpu_custom_call" | custom-call | tf_op jit(solution)/shard_map/pack_sides/pallas_call | solution.py:629
  12.6 4.3 %collective-permute-start.1 = (f32[10,64,128]{2,1,0:T(8,128)}, f32[10,64,128]{2,1,0:T(8,128)S(1)}, u32[]{:S(2)}, u32[]{:S(2)}) collective-permute-start(f32[10,64,128]{2,1,0:T(8,128)} %get-tuple-element.44), channel_id=1, source_target_pairs={{8,16},{16,8},{24,32},{32,24},{40,48},{48,40},{56,64},{64,56},{72,... | collective-permute-start | bytes 983048 | tf_op jit(solution)/shard_map/ppermute | solution.py:583
  16.9 0.1 collective-permute-start
  17.0 0.0 copy-done.4
  17.1 0.6 %fusion.7.code_rows = s32[8,128]{1,0:T(8,128)} fusion(s32[1024]{0:T(1024)S(1)} %copy-done.4, s32[]{:T(128)S(6)} %mul.7, s32[]{:T(128)S(6)} %mul.6), kind=kLoop, calls=%fused_computation.10 | loop fusion | flops 20480 | bytes 8200 | tf_op jit(solution)/shard_map/reshape | solution.py:610
  17.7 0.6 %add_select_fusion.codes = s32[1024]{0:T(1024)} fusion(s32[1024]{0:T(1024)S(1)} %copy-done.4, s32[]{:T(128)S(6)} %mul.7, s32[]{:T(128)S(6)} %mul.6), kind=kLoop, calls=%fused_computation | loop fusion | flops 20480 | bytes 8200 | tf_op jit(solution)/shard_map/jit(_where)/select_n | solution.py:609
  18.3 0.0 copy-start
  18.3 6.2 %stack_fields.1 = (f32[6,64,4096]{2,1,0:T(8,128)}, f32[7,2,4096]{2,1,0:T(2,128)}, f32[7,2,4096]{2,1,0:T(2,128)}, s32[1024]{0:T(1024)}, s32[1]{0:T(128)}) custom-call(f32[10,64,128]{2,1,0:T(8,128)} %get-tuple-element.41.side, s32[1024]{0:T(1024)} %add_select_fusion.codes, s32[8,128]{1,0:T(8,128)} %fusion.7.code_rows, f32[64,4096]{1,0:T(8,128)} %kd_h.1, ...), custom_call_target="tpu_custom_call" | custom-call | tf_op jit(solution)/shard_map/stack_fields/pallas_call | solution.py:638
  24.5 0.5 collective-permute-start.4
  25.0 5.2 %collective-permute-start.5 = (f32[7,2,4096]{2,1,0:T(2,128)}, f32[7,2,4096]{2,1,0:T(2,128)}, u32[]{:S(2)}, u32[]{:S(2)}) collective-permute-start(f32[7,2,4096]{2,1,0:T(2,128)} %get-tuple-element.50), channel_id=1, source_target_pairs={{1,2},{2,1},{3,4},{4,3},{5,6},{6,5},{9,10},{10,9},{11,12},{12,11},... | collective-permute-start | bytes 688136 | tf_op jit(solution)/shard_map/ppermute | solution.py:583
  30.1 0.9 %collective-permute-done.1.x_b = f32[10,64,128]{2,1,0:T(8,128)S(1)} collective-permute-done((f32[10,64,128]{2,1,0:T(8,128)}, f32[10,64,128]{2,1,0:T(8,128)S(1)}, u32[]{:S(2)}, u32[]{:S(2)}) %collective-permute-start.1) | collective-permute-done | bytes 327712 | tf_op jit(solution)/shard_map/ppermute | solution.py:583
  31.0 0.0 collective-permute-done.x_a
  31.0 0.0 all-to-all-done.lines
  31.0 0.0 copy-done
  31.0 0.0 copy-start.2
  31.0 0.0 copy-start.3
  31.1 5.6 %first_half.1 = (f32[36,80,128]{2,1,0:T(8,128)S(1)}, f32[36,80,128]{2,1,0:T(8,128)S(1)}, f32[36,80,128]{2,1,0:T(8,128)S(1)}, f32[36,80,128]{2,1,0:T(8,128)S(1)},...) custom-call(f32[16,4,4608]{2,1,0:T(4,128)} %all-to-all-done.lines, ...), custom_call_target="tpu_custom_call" | custom-call | tf_op jit(solution)/shard_map/first_half/pallas_call | solution.py:659
  36.7 0.5 collective-permute-start.2
  37.2 4.3 %collective-permute-start.3 = (f32[4,5120]{1,0:T(4,128)S(1)}, f32[4,5120]{1,0:T(4,128)S(1)}, u32[]{:S(2)}, u32[]{:S(2)}) collective-permute-start(f32[4,5120]{1,0:T(4,128)S(1)} %get-tuple-element.47), channel_id=1, source_target_pairs={{1,2},{2,1},{3,4},{4,3},{5,6},{6,5},{9,10},{10,9},{11,12},{12,11},... | collective-permute-start | bytes 245768 | tf_op jit(solution)/shard_map/ppermute | solution.py:583
  41.5 0.0 collective-permute-done.4.y_a
  41.5 0.0 collective-permute-done.5.y_b
  41.5 0.0 copy-done.2
  41.5 0.0 copy-done.3
  41.5 0.0 copy-start.1
  41.5 5.5 %middle.1 = (f32[36,80,128]{2,1,0:T(8,128)S(1)}, f32[36,80,128]{2,1,0:T(8,128)S(1)}, f32[36,80,128]{2,1,0:T(8,128)S(1)}, f32[36,80,128]{2,1,0:T(8,128)S(1)}, f32...) custom-call(s32[1024]{0:T(1024)S(1)} %copy-done.3, ...), custom_call_target="tpu_custom_call", output_to_operand_aliasing={{0}: (9, {}), {1}: (10, {}), {2}: (11, {}), {3}: (12, {}), ... | custom-call | tf_op jit(solution)/shard_map/middle/pallas_call | solution.py:672
  47.0 0.0 collective-permute-done.2.msg_a
  47.1 0.0 collective-permute-done.3.msg_b
  47.1 0.0 copy-done.1
  47.1 6.5 %second_half.1 = (f32[64,4096]{1,0:T(8,128)}, f32[64,4096]{1,0:T(8,128)}, f32[36,80,128]{2,1,0:T(8,128)S(1)}, f32[36,80,128]{2,1,0:T(8,128)S(1)}, f32[36,80,128]...) custom-call(s32[1024]{0:T(1024)S(1)} %copy-done.3, ...), custom_call_target="tpu_custom_call", output_to_operand_aliasing={{2}: (7, {}), {3}: (8, {}), {4}: (9, {}), {5}: (10, {}), {6... | custom-call | tf_op jit(solution)/shard_map/second_half/pallas_call | solution.py:689
Async XLA Ops:
  3.1 27.9 %all-to-all-start = ((f32[16,4,4608]{2,1,0:T(4,128)}), f32[16,4,4608]{2,1,0:T(4,128)}, u32[]{:S(2)}, u32[]{:S(2)}) async-start(f32[16,4,4608]{2,1,0:T(4,128)} %pack_lines.1), calls=%async_computation | async-start | bytes 2359296 | tf_op jit(solution)/shard_map/all_to_all | solution.py:602
  10.4 6.6 %copy-start.4 = (s32[1024]{0:T(1024)S(1)}, s32[1024]{0:T(1024)}, u32[]{:S(2)}) copy-start(s32[1024]{0:T(1024)} %param.13) | copy-start | bytes 12292
  12.6 18.4 %collective-permute-start.1 = (f32[10,64,128]{2,1,0:T(8,128)}, f32[10,64,128]{2,1,0:T(8,128)S(1)}, u32[]{:S(2)}, u32[]{:S(2)}) collective-permute-start(f32[10,64,128]{2,1,0:T(8,128)} %get-tuple-element.44), channel_id=1, source_target_pairs={{8,16},{16,8},{24,32},{32,24},{40,48},{48,40},{56,64},{64,56},{72,... | collective-permute-start | bytes 983048 | tf_op jit(solution)/shard_map/ppermute | solution.py:583
  16.9 14.1 %collective-permute-start = (f32[10,64,128]{2,1,0:T(8,128)}, f32[10,64,128]{2,1,0:T(8,128)}, u32[]{:S(2)}, u32[]{:S(2)}) collective-permute-start(f32[10,64,128]{2,1,0:T(8,128)} %get-tuple-element.41.side), channel_id=1, source_target_pairs={{0,8},{8,0},{16,24},{24,16},{32,40},{40,32},{48,56},{56,48},{64,72... | collective-permute-start | bytes 983048 | tf_op jit(solution)/shard_map/ppermute | solution.py:583
  18.3 12.8 %copy-start = (f32[3,64,4096]{2,1,0:T(8,128)S(1)}, f32[3,64,4096]{2,1,0:T(8,128)}, u32[]{:S(2)}) copy-start(f32[3,64,4096]{2,1,0:T(8,128)} %v_h.1) | copy-start | bytes 9437188
  24.5 17.0 %collective-permute-start.4 = (f32[7,2,4096]{2,1,0:T(2,128)}, f32[7,2,4096]{2,1,0:T(2,128)}, u32[]{:S(2)}, u32[]{:S(2)}) collective-permute-start(f32[7,2,4096]{2,1,0:T(2,128)} %get-tuple-element.49), channel_id=1, source_target_pairs={{0,1},{1,0},{2,3},{3,2},{4,5},{5,4},{6,7},{7,6},{8,9},{9,8},{10,11... | collective-permute-start | bytes 688136 | tf_op jit(solution)/shard_map/ppermute | solution.py:583
  25.0 16.5 %collective-permute-start.5 = (f32[7,2,4096]{2,1,0:T(2,128)}, f32[7,2,4096]{2,1,0:T(2,128)}, u32[]{:S(2)}, u32[]{:S(2)}) collective-permute-start(f32[7,2,4096]{2,1,0:T(2,128)} %get-tuple-element.50), channel_id=1, source_target_pairs={{1,2},{2,1},{3,4},{4,3},{5,6},{6,5},{9,10},{10,9},{11,12},{12,11},... | collective-permute-start | bytes 688136 | tf_op jit(solution)/shard_map/ppermute | solution.py:583
  31.0 10.5 %copy-start.2 = (f32[64,4096]{1,0:T(8,128)S(1)}, f32[64,4096]{1,0:T(8,128)}, u32[]{:S(2)}) copy-start(f32[64,4096]{1,0:T(8,128)} %t_h.1) | copy-start | bytes 3145732
  31.0 10.5 %copy-start.3 = (s32[1024]{0:T(1024)S(1)}, s32[1024]{0:T(1024)}, u32[]{:S(2)}) copy-start(s32[1024]{0:T(1024)} %get-tuple-element.42.found) | copy-start | bytes 12292
  36.7 10.4 %collective-permute-start.2 = (f32[4,5120]{1,0:T(4,128)S(1)}, f32[4,5120]{1,0:T(4,128)S(1)}, u32[]{:S(2)}, u32[]{:S(2)}) collective-permute-start(f32[4,5120]{1,0:T(4,128)S(1)} %get-tuple-element.46), channel_id=1, source_target_pairs={{0,1},{1,0},{2,3},{3,2},{4,5},{5,4},{6,7},{7,6},{8,9},{9,8},{10,11... | collective-permute-start | bytes 245768 | tf_op jit(solution)/shard_map/ppermute | solution.py:583
  37.2 9.9 %collective-permute-start.3 = (f32[4,5120]{1,0:T(4,128)S(1)}, f32[4,5120]{1,0:T(4,128)S(1)}, u32[]{:S(2)}, u32[]{:S(2)}) collective-permute-start(f32[4,5120]{1,0:T(4,128)S(1)} %get-tuple-element.47), channel_id=1, source_target_pairs={{1,2},{2,1},{3,4},{4,3},{5,6},{6,5},{9,10},{10,9},{11,12},{12,11},... | collective-permute-start | bytes 245768 | tf_op jit(solution)/shard_map/ppermute | solution.py:583
  41.5 5.6 %copy-start.1 = (f32[64,4096]{1,0:T(8,128)S(1)}, f32[64,4096]{1,0:T(8,128)}, u32[]{:S(2)}) copy-start(f32[64,4096]{1,0:T(8,128)} %kd_h.1) | copy-start | bytes 3145732

commit v7 on v6

--- a/solution.py
+++ b/solution.py
@@ -160,11 +160,12 @@
 def coefficients(v0, v1, v2, drain):
     z = lax.broadcasted_iota(jnp.int32, v0.shape, v0.ndim - 1) & (NZ - 1)
     north = DISP - jnp.minimum(v0, 0.0)
-    south = DISP + jnp.maximum(v0, 0.0)
+    south = v0 + north
     east = DISP - jnp.minimum(v1, 0.0)
-    west = DISP + jnp.maximum(v1, 0.0)
-    up = jnp.where(z == NZ - 1, 0.0, DISP - jnp.minimum(v2, 0.0))
-    down = jnp.where(z == 0, 0.0, DISP + jnp.maximum(v2, 0.0))
+    west = v1 + east
+    rise = DISP - jnp.minimum(v2, 0.0)
+    up = jnp.where(z == NZ - 1, 0.0, rise)
+    down = jnp.where(z == 0, 0.0, v2 + rise)
     centre = ((north + south) + (east + west)) + ((up + down) + drain)
     return north, south, east, west, up, down, centre
 

time: 54.6 us -> 54.4 us (level)
  waiting for transfers between devices: 0.89 us -> 1.69 us
  starting transfers between devices: 22.1 us -> 21.4 us
    ppermute x6, waiting for transfers between devices: 0.89 us -> 1.69 us  [swap(): return (lax.ppermute(a, axis, pairs(0)), lax.ppermute(b, axis, pairs(1)))]
    ppermute x6, starting transfers between devices: 14.8 us -> 14.1 us  [swap(): return (lax.ppermute(a, axis, pairs(0)), lax.ppermute(b, axis, pairs(1)))]
  transfers between devices with their start and end apart: 7 -> 7, of which waited for: 1 -> 1; matrix products, arithmetic and copies ran while one was open for 2% -> 2% of each run, Pallas kernels for 36% -> 37%
where the time goes in v7:
time: 54.4 us; the launch traced here: 53.8 us
  Pallas kernels  28.7 us (53%)
  starting transfers between devices  21.4 us (39%)
  waiting for transfers between devices  1.69 us (3%)
  other arithmetic  1.21 us (2%)
  between operations  0.8 us (1%)
    ppermute x6, starting transfers between devices, swap(): return (lax.ppermute(a, axis, pairs(0)), lax.ppermute(b, axis, pairs(1)))  14.1 us
    all_to_all x1, starting transfers between devices, per_device(): lax.all_to_all(lines, 'gx', split_axis=0, concat_axis=0, tiled=True)  7.29 us
    pallas_call x1, Pallas kernels, per_device(): pl.pallas_call(stack_fields, grid=(PACK_BLOCKS,), out_shape=[jax.ShapeDty...  6.6 us
    pallas_call x1, Pallas kernels, per_device(): pl.pallas_call(second_half, out_shape=[plane, plane] + [window()] * 18, i...  6.5 us
    pallas_call x1, Pallas kernels, per_device(): pl.pallas_call(middle, out_shape=[window()] * 9 + [edge_kd] + [window()]...  5.5 us
    pallas_call x1, Pallas kernels, per_device(): pl.pallas_call(first_half, out_shape=[window()] * 4 + [power] + [window()...  5.46 us
    pallas_call x1, Pallas kernels, per_device(): pl.pallas_call(pack_lines, out_shape=jax.ShapeDtypeStruct((n_gx, checkpoi...  2.49 us
    pallas_call x1, Pallas kernels, per_device(): pl.pallas_call(pack_sides, grid=(1,), out_shape=[side, side], in_specs=sp...  2.19 us
  transfers between devices with their start and end apart: 7, of which 1 were waited for; matrix products, arithmetic and copies ran while one was open for 2% of the time, Pallas kernels for 37%

profile of v7, /device:TPU:104, one launch (start us, length us, event | category | flops | bytes accessed | tf_op | source)
XLA Modules:
  0.0 53.8 jit_solution(3118923058112507542)
XLA Ops:
  0.6 2.5 %pack_lines.1 = f32[16,4,4608]{2,1,0:T(4,128)} custom-call(f32[1,4,65536]{2,1,0:T(4,128)} %src.1), custom_call_target="tpu_custom_call" | custom-call | tf_op jit(solution)/shard_map/pack_lines/pallas_call | solution.py:590
  3.1 7.3 %all-to-all-start = ((f32[16,4,4608]{2,1,0:T(4,128)}), f32[16,4,4608]{2,1,0:T(4,128)}, u32[]{:S(2)}, u32[]{:S(2)}) async-start(f32[16,4,4608]{2,1,0:T(4,128)} %pack_lines.1), calls=%async_computation | async-start | bytes 2359296 | tf_op jit(solution)/shard_map/all_to_all | solution.py:603
  10.4 0.0 copy-start.4
  10.4 2.2 %pack_sides.1 = (f32[10,64,128]{2,1,0:T(8,128)}, f32[10,64,128]{2,1,0:T(8,128)}) custom-call(f32[64,4096]{1,0:T(8,128)} %kd_h.1, f32[64,4096]{1,0:T(8,128)} %kd_h.1, f32[3,64,4096]{2,1,0:T(8,128)} %v_h.1, f32[3,64,4096]{2,1,0:T(8,128)} %v_h.1, f32[64,4096]{1,0:T(8,128)} %sb.1, f32[64,4096]{1,0:T(8,128)} %sb.1, s32[64,4096]{1,0:T(8,128)} %cb.1, ...), custom_call_target="tpu_custom_call" | custom-call | tf_op jit(solution)/shard_map/pack_sides/pallas_call | solution.py:630
  12.6 4.3 %collective-permute-start.1 = (f32[10,64,128]{2,1,0:T(8,128)}, f32[10,64,128]{2,1,0:T(8,128)S(1)}, u32[]{:S(2)}, u32[]{:S(2)}) collective-permute-start(f32[10,64,128]{2,1,0:T(8,128)} %get-tuple-element.44), channel_id=1, source_target_pairs={{8,16},{16,8},{24,32},{32,24},{40,48},{48,40},{56,64},{64,56},{72,... | collective-permute-start | bytes 983048 | tf_op jit(solution)/shard_map/ppermute | solution.py:584
  16.9 0.1 collective-permute-start
  17.0 0.0 copy-done.4
  17.1 0.6 %fusion.7.code_rows = s32[8,128]{1,0:T(8,128)} fusion(s32[1024]{0:T(1024)S(1)} %copy-done.4, s32[]{:T(128)S(6)} %mul.7, s32[]{:T(128)S(6)} %mul.6), kind=kLoop, calls=%fused_computation.10 | loop fusion | flops 20480 | bytes 8200 | tf_op jit(solution)/shard_map/reshape | solution.py:611
  17.7 0.6 %add_select_fusion.codes = s32[1024]{0:T(1024)} fusion(s32[1024]{0:T(1024)S(1)} %copy-done.4, s32[]{:T(128)S(6)} %mul.7, s32[]{:T(128)S(6)} %mul.6), kind=kLoop, calls=%fused_computation | loop fusion | flops 20480 | bytes 8200 | tf_op jit(solution)/shard_map/jit(_where)/select_n | solution.py:610
  18.3 0.0 copy-start
  18.3 6.6 %stack_fields.1 = (f32[6,64,4096]{2,1,0:T(8,128)}, f32[7,2,4096]{2,1,0:T(2,128)}, f32[7,2,4096]{2,1,0:T(2,128)}, s32[1024]{0:T(1024)}, s32[1]{0:T(128)}) custom-call(f32[10,64,128]{2,1,0:T(8,128)} %get-tuple-element.41.side, s32[1024]{0:T(1024)} %add_select_fusion.codes, s32[8,128]{1,0:T(8,128)} %fusion.7.code_rows, f32[64,4096]{1,0:T(8,128)} %kd_h.1, ...), custom_call_target="tpu_custom_call" | custom-call | tf_op jit(solution)/shard_map/stack_fields/pallas_call | solution.py:639
  24.9 0.1 collective-permute-start.4
  25.0 4.8 %collective-permute-start.5 = (f32[7,2,4096]{2,1,0:T(2,128)}, f32[7,2,4096]{2,1,0:T(2,128)}, u32[]{:S(2)}, u32[]{:S(2)}) collective-permute-start(f32[7,2,4096]{2,1,0:T(2,128)} %get-tuple-element.50), channel_id=1, source_target_pairs={{1,2},{2,1},{3,4},{4,3},{5,6},{6,5},{9,10},{10,9},{11,12},{12,11},... | collective-permute-start | bytes 688136 | tf_op jit(solution)/shard_map/ppermute | solution.py:584
  29.8 1.7 %collective-permute-done.1.x_b = f32[10,64,128]{2,1,0:T(8,128)S(1)} collective-permute-done((f32[10,64,128]{2,1,0:T(8,128)}, f32[10,64,128]{2,1,0:T(8,128)S(1)}, u32[]{:S(2)}, u32[]{:S(2)}) %collective-permute-start.1) | collective-permute-done | bytes 327712 | tf_op jit(solution)/shard_map/ppermute | solution.py:584
  31.4 0.0 collective-permute-done.x_a
  31.4 0.0 all-to-all-done.lines
  31.4 0.0 copy-done
  31.4 0.0 copy-start.2
  31.5 0.0 copy-start.3
  31.5 5.5 %first_half.1 = (f32[36,80,128]{2,1,0:T(8,128)S(1)}, f32[36,80,128]{2,1,0:T(8,128)S(1)}, f32[36,80,128]{2,1,0:T(8,128)S(1)}, f32[36,80,128]{2,1,0:T(8,128)S(1)},...) custom-call(f32[16,4,4608]{2,1,0:T(4,128)} %all-to-all-done.lines, ...), custom_call_target="tpu_custom_call" | custom-call | tf_op jit(solution)/shard_map/first_half/pallas_call | solution.py:660
  36.9 0.5 collective-permute-start.2
  37.4 4.3 %collective-permute-start.3 = (f32[4,5120]{1,0:T(4,128)S(1)}, f32[4,5120]{1,0:T(4,128)S(1)}, u32[]{:S(2)}, u32[]{:S(2)}) collective-permute-start(f32[4,5120]{1,0:T(4,128)S(1)} %get-tuple-element.47), channel_id=1, source_target_pairs={{1,2},{2,1},{3,4},{4,3},{5,6},{6,5},{9,10},{10,9},{11,12},{12,11},... | collective-permute-start | bytes 245768 | tf_op jit(solution)/shard_map/ppermute | solution.py:584
  41.7 0.0 collective-permute-done.4.y_a
  41.7 0.0 collective-permute-done.5.y_b
  41.7 0.0 copy-done.2
  41.7 0.0 copy-done.3
  41.8 0.0 copy-start.1
  41.8 5.5 %middle.1 = (f32[36,80,128]{2,1,0:T(8,128)S(1)}, f32[36,80,128]{2,1,0:T(8,128)S(1)}, f32[36,80,128]{2,1,0:T(8,128)S(1)}, f32[36,80,128]{2,1,0:T(8,128)S(1)}, f32...) custom-call(s32[1024]{0:T(1024)S(1)} %copy-done.3, ...), custom_call_target="tpu_custom_call", output_to_operand_aliasing={{0}: (9, {}), {1}: (10, {}), {2}: (11, {}), {3}: (12, {}), ... | custom-call | tf_op jit(solution)/shard_map/middle/pallas_call | solution.py:673
  47.3 0.0 collective-permute-done.2.msg_a
  47.3 0.0 collective-permute-done.3.msg_b
  47.3 0.0 copy-done.1
  47.3 6.5 %second_half.1 = (f32[64,4096]{1,0:T(8,128)}, f32[64,4096]{1,0:T(8,128)}, f32[36,80,128]{2,1,0:T(8,128)S(1)}, f32[36,80,128]{2,1,0:T(8,128)S(1)}, f32[36,80,128]...) custom-call(s32[1024]{0:T(1024)S(1)} %copy-done.3, ...), custom_call_target="tpu_custom_call", output_to_operand_aliasing={{2}: (7, {}), {3}: (8, {}), {4}: (9, {}), {5}: (10, {}), {6... | custom-call | tf_op jit(solution)/shard_map/second_half/pallas_call | solution.py:690
Async XLA Ops:
  3.1 28.3 %all-to-all-start = ((f32[16,4,4608]{2,1,0:T(4,128)}), f32[16,4,4608]{2,1,0:T(4,128)}, u32[]{:S(2)}, u32[]{:S(2)}) async-start(f32[16,4,4608]{2,1,0:T(4,128)} %pack_lines.1), calls=%async_computation | async-start | bytes 2359296 | tf_op jit(solution)/shard_map/all_to_all | solution.py:603
  10.4 6.6 %copy-start.4 = (s32[1024]{0:T(1024)S(1)}, s32[1024]{0:T(1024)}, u32[]{:S(2)}) copy-start(s32[1024]{0:T(1024)} %param.13) | copy-start | bytes 12292
  12.6 18.8 %collective-permute-start.1 = (f32[10,64,128]{2,1,0:T(8,128)}, f32[10,64,128]{2,1,0:T(8,128)S(1)}, u32[]{:S(2)}, u32[]{:S(2)}) collective-permute-start(f32[10,64,128]{2,1,0:T(8,128)} %get-tuple-element.44), channel_id=1, source_target_pairs={{8,16},{16,8},{24,32},{32,24},{40,48},{48,40},{56,64},{64,56},{72,... | collective-permute-start | bytes 983048 | tf_op jit(solution)/shard_map/ppermute | solution.py:584
  16.9 14.5 %collective-permute-start = (f32[10,64,128]{2,1,0:T(8,128)}, f32[10,64,128]{2,1,0:T(8,128)}, u32[]{:S(2)}, u32[]{:S(2)}) collective-permute-start(f32[10,64,128]{2,1,0:T(8,128)} %get-tuple-element.41.side), channel_id=1, source_target_pairs={{0,8},{8,0},{16,24},{24,16},{32,40},{40,32},{48,56},{56,48},{64,72... | collective-permute-start | bytes 983048 | tf_op jit(solution)/shard_map/ppermute | solution.py:584
  18.3 13.2 %copy-start = (f32[3,64,4096]{2,1,0:T(8,128)S(1)}, f32[3,64,4096]{2,1,0:T(8,128)}, u32[]{:S(2)}) copy-start(f32[3,64,4096]{2,1,0:T(8,128)} %v_h.1) | copy-start | bytes 9437188
  24.9 16.8 %collective-permute-start.4 = (f32[7,2,4096]{2,1,0:T(2,128)}, f32[7,2,4096]{2,1,0:T(2,128)}, u32[]{:S(2)}, u32[]{:S(2)}) collective-permute-start(f32[7,2,4096]{2,1,0:T(2,128)} %get-tuple-element.49), channel_id=1, source_target_pairs={{0,1},{1,0},{2,3},{3,2},{4,5},{5,4},{6,7},{7,6},{8,9},{9,8},{10,11... | collective-permute-start | bytes 688136 | tf_op jit(solution)/shard_map/ppermute | solution.py:584
  25.0 16.8 %collective-permute-start.5 = (f32[7,2,4096]{2,1,0:T(2,128)}, f32[7,2,4096]{2,1,0:T(2,128)}, u32[]{:S(2)}, u32[]{:S(2)}) collective-permute-start(f32[7,2,4096]{2,1,0:T(2,128)} %get-tuple-element.50), channel_id=1, source_target_pairs={{1,2},{2,1},{3,4},{4,3},{5,6},{6,5},{9,10},{10,9},{11,12},{12,11},... | collective-permute-start | bytes 688136 | tf_op jit(solution)/shard_map/ppermute | solution.py:584
  31.4 10.3 %copy-start.2 = (f32[64,4096]{1,0:T(8,128)S(1)}, f32[64,4096]{1,0:T(8,128)}, u32[]{:S(2)}) copy-start(f32[64,4096]{1,0:T(8,128)} %t_h.1) | copy-start | bytes 3145732
  31.5 10.3 %copy-start.3 = (s32[1024]{0:T(1024)S(1)}, s32[1024]{0:T(1024)}, u32[]{:S(2)}) copy-start(s32[1024]{0:T(1024)} %get-tuple-element.42.found) | copy-start | bytes 12292
  36.9 10.4 %collective-permute-start.2 = (f32[4,5120]{1,0:T(4,128)S(1)}, f32[4,5120]{1,0:T(4,128)S(1)}, u32[]{:S(2)}, u32[]{:S(2)}) collective-permute-start(f32[4,5120]{1,0:T(4,128)S(1)} %get-tuple-element.46), channel_id=1, source_target_pairs={{0,1},{1,0},{2,3},{3,2},{4,5},{5,4},{6,7},{7,6},{8,9},{9,8},{10,11... | collective-permute-start | bytes 245768 | tf_op jit(solution)/shard_map/ppermute | solution.py:584
  37.4 9.9 %collective-permute-start.3 = (f32[4,5120]{1,0:T(4,128)S(1)}, f32[4,5120]{1,0:T(4,128)S(1)}, u32[]{:S(2)}, u32[]{:S(2)}) collective-permute-start(f32[4,5120]{1,0:T(4,128)S(1)} %get-tuple-element.47), channel_id=1, source_target_pairs={{1,2},{2,1},{3,4},{4,3},{5,6},{6,5},{9,10},{10,9},{11,12},{12,11},... | collective-permute-start | bytes 245768 | tf_op jit(solution)/shard_map/ppermute | solution.py:584
  41.8 5.5 %copy-start.1 = (f32[64,4096]{1,0:T(8,128)S(1)}, f32[64,4096]{1,0:T(8,128)}, u32[]{:S(2)}) copy-start(f32[64,4096]{1,0:T(8,128)} %kd_h.1) | copy-start | bytes 3145732
